TPU v7x, 32 devices: a whole 2x2x4 slice. The times are simulated.
32 devices in a mesh: fsdp: 8 (over y, x, core), tp: 4 (over z).
Axes of the slice: x: 2, y: 2, z: 4, core: 2. Of those that a mesh axis runs over, the one named last changes fastest.
Arguments:
- stream: bfloat16 [8, 1024, 2048], P('fsdp', 'tp'), may hold values from -6 to 6
- attn_gain: bfloat16 [2048], P('fsdp'), may hold values from 0.099609375 to 1.8984375
- w_query: bfloat16 [2048, 2048], P('fsdp', 'tp'), may hold values from -0.1875 to 0.1875
- w_key: bfloat16 [2048, 2048], P('fsdp', 'tp'), may hold values from -0.1875 to 0.1875
- w_value: bfloat16 [2048, 2048], P('fsdp', 'tp'), may hold values from -0.125 to 0.125
- w_out: bfloat16 [2048, 2048], P('fsdp', 'tp'), may hold values from -0.5 to 0.5
- mem_gate: float32 [16], P('tp'), may hold values from -3 to 3
- mlp_gain: bfloat16 [2048], P('fsdp'), may hold values from 0.099609375 to 1.8984375
- w_gate: bfloat16 [2048, 8192], P('fsdp', 'tp'), may hold values from -0.125 to 0.125
- w_up: bfloat16 [2048, 8192], P('fsdp', 'tp'), may hold values from -0.125 to 0.125
- w_down: bfloat16 [2048, 8192], P('fsdp', 'tp'), may hold values from -0.125 to 0.125
- memory: float32 [8, 16, 128, 128], P('fsdp', 'tp'), may hold values from -48 to 48
- normalizer: float32 [8, 16, 128], P('fsdp', 'tp'), may hold values from 0.5 to 4
- prefix: int32 [8], replicated, may hold values from 0 to 511
- valid: int32 [8], replicated, may hold values from 513 to 1024, as said below
- cotangent: bfloat16 [8, 1024, 2048], P('fsdp', 'tp'), may hold values from -6 to 6
Outputs:
- stream_out: bfloat16 [8, 1024, 2048], P('fsdp', 'tp')
- stream_grad: float32 [8, 1024, 2048], P('fsdp', 'tp')
- attn_gain_grad: float32 [2048], P('fsdp')
- w_query_grad: float32 [2048, 2048], P('fsdp', 'tp')
- w_key_grad: float32 [2048, 2048], P('fsdp', 'tp')
- w_value_grad: float32 [2048, 2048], P('fsdp', 'tp')
- w_out_grad: float32 [2048, 2048], P('fsdp', 'tp')
- mem_gate_grad: float32 [16], P('tp')
- mlp_gain_grad: float32 [2048], P('fsdp')
- w_gate_grad: float32 [2048, 8192], P('fsdp', 'tp')
- w_up_grad: float32 [2048, 8192], P('fsdp', 'tp')
- w_down_grad: float32 [2048, 8192], P('fsdp', 'tp')
- memory_next: float32 [8, 16, 128, 128], P('fsdp', 'tp')
- normalizer_next: float32 [8, 16, 128], P('fsdp', 'tp')
- memory_grad: float32 [8, 16, 128, 128], P('fsdp', 'tp')
- normalizer_grad: float32 [8, 16, 128], P('fsdp', 'tp')
- rms_stats: float32 [8, 3], P('fsdp')
Inputs may be any that keep to these rules, and one draw needn't show every extreme that they name: Every sequence has more valid tokens than half its length; in every draw some sequence has all 1024 tokens valid.
All inputs are finite; a program needn't handle non-finite values.
Results may differ from a plain program's by a relative error of at most 0.015.
Values may be sent and summed in bfloat16 or wider, within the bound.
A program may use at most 256 MiB of HBM per device.

v0:
```python
import jax
import jax.numpy as jnp
from jax import lax
from jax.sharding import PartitionSpec as P

norm_eps = 1e-06
rms_eps = 1e-06
neg_fill = -1e30


def normalize(rows_in):
    return rows_in * lax.rsqrt(jnp.mean(rows_in * rows_in, axis=-1, keepdims=True) + norm_eps)


def norm_gain(rows_in, gain_full):
    return normalize(rows_in) * gain_full


def glu_product(gate_pre, up_pre):
    return jax.nn.gelu(gate_pre) * up_pre


def memory_mix(query_f, local_f, memory_s, normalizer_s, gate_logit):
    mapped = jax.nn.elu(query_f) + 1.0
    numerator = jnp.einsum("lhd,hde->lhe", mapped, memory_s, precision=lax.Precision.HIGHEST)
    denominator = jnp.einsum("lhd,hd->lh", mapped, normalizer_s, precision=lax.Precision.HIGHEST)
    gate_open = jax.nn.sigmoid(gate_logit)[None, :, None]
    return gate_open * (numerator / denominator[:, :, None]) + (1.0 - gate_open) * local_f


def allowed_keys(row_first, row_count, key_count, prefix_len, valid_len):
    row_index = row_first + jnp.arange(row_count, dtype=jnp.int32)
    key_index = jnp.arange(key_count, dtype=jnp.int32)
    causal = key_index[None, :] <= row_index[:, None]
    return (key_index[None, :] < valid_len) & (causal | (key_index[None, :] < prefix_len))


def contract_rows(first_mat, second_mat):
    return lax.dot_general(
        first_mat, second_mat, (((0,), (0,)), ((), ())), preferred_element_type=jnp.float32
    )


def times_transpose(first_mat, second_mat):
    return lax.dot_general(
        first_mat, second_mat, (((1,), (1,)), ((), ())), preferred_element_type=jnp.float32
    )


def split_blocks(rows_in, block_rows):
    return rows_in.reshape((rows_in.shape[0] // block_rows, block_rows) + rows_in.shape[1:])


def attend_forward(query_rows, key_rows, value_rows, prefix_len, valid_len):
    query_count = query_rows.shape[0]
    key_count = key_rows.shape[0]
    block_rows = min(512, query_count)
    score_scale = query_rows.shape[-1] ** (-0.5)
    block_first = jnp.arange(query_count // block_rows, dtype=jnp.int32) * block_rows

    def one_block(block_pair):
        query_block, row_first = block_pair
        scores = (
            jnp.einsum("qhd,khd->hqk", query_block, key_rows, preferred_element_type=jnp.float32)
            * score_scale
        )
        masked = jnp.where(
            allowed_keys(row_first, block_rows, key_count, prefix_len, valid_len)[None],
            scores,
            neg_fill,
        )
        row_top = jnp.max(masked, axis=-1, keepdims=True)
        exp_scores = jnp.exp(masked - row_top)
        row_total = jnp.sum(exp_scores, axis=-1, keepdims=True)
        probs_low = (exp_scores / row_total).astype(jnp.bfloat16)
        mixed_rows = jnp.einsum(
            "hqk,khd->qhd", probs_low, value_rows, preferred_element_type=jnp.float32
        )
        return (mixed_rows, (row_top + jnp.log(row_total))[:, :, 0])

    mixed_rows, log_total = lax.map(one_block, (split_blocks(query_rows, block_rows), block_first))
    return (mixed_rows.reshape(query_rows.shape), log_total)


def attend_backward(query_rows, key_rows, value_rows, grad_local, log_total, prefix_len, valid_len):
    query_count = query_rows.shape[0]
    key_count = key_rows.shape[0]
    block_rows = min(512, query_count)
    score_scale = query_rows.shape[-1] ** (-0.5)
    block_first = jnp.arange(query_count // block_rows, dtype=jnp.int32) * block_rows

    def one_block(block_carry, inputs):
        grad_keys, grad_values = block_carry
        query_block, grad_block, block_total, row_first = inputs
        scores = (
            jnp.einsum("qhd,khd->hqk", query_block, key_rows, preferred_element_type=jnp.float32)
            * score_scale
        )
        masked = jnp.where(
            allowed_keys(row_first, block_rows, key_count, prefix_len, valid_len)[None],
            scores,
            neg_fill,
        )
        attn_probs = jnp.exp(masked - block_total[:, :, None])
        grad_probs = jnp.einsum(
            "qhd,khd->hqk", grad_block, value_rows, preferred_element_type=jnp.float32
        )
        row_delta = jnp.sum(attn_probs * grad_probs, axis=-1, keepdims=True)
        grad_scores = (attn_probs * (grad_probs - row_delta)).astype(jnp.bfloat16)
        grad_query = (
            jnp.einsum("hqk,khd->qhd", grad_scores, key_rows, preferred_element_type=jnp.float32)
            * score_scale
        )
        grad_keys = (
            grad_keys
            + jnp.einsum(
                "hqk,qhd->khd", grad_scores, query_block, preferred_element_type=jnp.float32
            )
            * score_scale
        )
        grad_values = grad_values + jnp.einsum(
            "hqk,qhd->khd",
            attn_probs.astype(jnp.bfloat16),
            grad_block,
            preferred_element_type=jnp.float32,
        )
        return ((grad_keys, grad_values), grad_query)

    zero_rows = jnp.zeros(key_rows.shape, jnp.float32)
    block_inputs = (
        split_blocks(query_rows, block_rows),
        split_blocks(grad_local, block_rows),
        log_total,
        block_first,
    )
    grad_pair, grad_query = lax.scan(one_block, (zero_rows, zero_rows), block_inputs)
    return (grad_query.reshape(query_rows.shape), grad_pair[0], grad_pair[1])


def fetch_attention(attn_gain, w_query, w_key, w_value, w_out):
    return (
        lax.all_gather(attn_gain, "fsdp", axis=0, tiled=True),
        lax.all_gather(w_query, "fsdp", axis=0, tiled=True),
        lax.all_gather(w_key, "fsdp", axis=0, tiled=True),
        lax.all_gather(w_value, "fsdp", axis=0, tiled=True),
        lax.all_gather(w_out, "fsdp", axis=0, tiled=True),
    )


def fetch_mlp(mlp_gain, w_gate, w_up, w_down):
    return (
        lax.all_gather(mlp_gain, "fsdp", axis=0, tiled=True),
        lax.all_gather(w_gate, "fsdp", axis=0, tiled=True),
        lax.all_gather(w_up, "fsdp", axis=0, tiled=True),
        lax.all_gather(w_down, "fsdp", axis=0, tiled=True),
    )


def on_device(
    stream,
    attn_gain,
    w_query,
    w_key,
    w_value,
    w_out,
    mem_gate,
    mlp_gain,
    w_gate,
    w_up,
    w_down,
    memory,
    normalizer,
    prefix,
    valid,
    cotangent,
):
    len_dev, width = (stream.shape[1], stream.shape[2])
    seq_len = len_dev * lax.axis_size("tp")
    heads_here = mem_gate.shape[0]
    head_dim = memory.shape[2]
    seq_here = lax.axis_index("fsdp")
    prefix_len = prefix[seq_here]
    valid_len = valid[seq_here]
    head_shape = (seq_len, heads_here, head_dim)
    full_shape = (1, seq_len, width)
    gain_one, query_full, key_full, value_full, out_full = fetch_attention(
        attn_gain, w_query, w_key, w_value, w_out
    )
    stream_f = stream.astype(jnp.float32)
    normed_local, norm_one_back = jax.vjp(norm_gain, stream_f, gain_one.astype(jnp.float32))
    normed_one = lax.all_gather(normed_local.astype(jnp.bfloat16), "tp", axis=1, tiled=True)
    flat_one = normed_one.reshape(seq_len, width)
    query_rows = (
        jnp.dot(flat_one, query_full, preferred_element_type=jnp.float32)
        .astype(jnp.bfloat16)
        .reshape(head_shape)
    )
    key_rows = (
        jnp.dot(flat_one, key_full, preferred_element_type=jnp.float32)
        .astype(jnp.bfloat16)
        .reshape(head_shape)
    )
    value_rows = (
        jnp.dot(flat_one, value_full, preferred_element_type=jnp.float32)
        .astype(jnp.bfloat16)
        .reshape(head_shape)
    )
    local_mix, log_total = attend_forward(query_rows, key_rows, value_rows, prefix_len, valid_len)
    combined_f, mix_pullback = jax.vjp(
        memory_mix, query_rows.astype(jnp.float32), local_mix, memory[0], normalizer[0], mem_gate
    )
    combined = combined_f.astype(jnp.bfloat16).reshape(seq_len, heads_here * head_dim)
    attn_branch = lax.psum_scatter(
        times_transpose(combined, out_full).reshape(full_shape),
        "tp",
        scatter_dimension=1,
        tiled=True,
    )
    middle = stream_f + attn_branch
    gain_two, gate_full, up_full, down_full = fetch_mlp(mlp_gain, w_gate, w_up, w_down)
    normed_mid, norm_two_back = jax.vjp(norm_gain, middle, gain_two.astype(jnp.float32))
    normed_two = lax.all_gather(normed_mid.astype(jnp.bfloat16), "tp", axis=1, tiled=True)
    flat_two = normed_two.reshape(seq_len, width)
    gate_pre = jnp.dot(flat_two, gate_full, preferred_element_type=jnp.float32)
    up_pre = jnp.dot(flat_two, up_full, preferred_element_type=jnp.float32)
    hidden_f, glu_back = jax.vjp(glu_product, gate_pre, up_pre)
    hidden = hidden_f.astype(jnp.bfloat16)
    mlp_branch = lax.psum_scatter(
        times_transpose(hidden, down_full).reshape(full_shape),
        "tp",
        scatter_dimension=1,
        tiled=True,
    )
    result = middle + mlp_branch
    stream_out = result.astype(jnp.bfloat16)
    row_live = (jnp.arange(seq_len, dtype=jnp.int32) < valid_len).astype(jnp.float32)
    keys_mapped = (jax.nn.elu(key_rows.astype(jnp.float32)) + 1.0) * row_live[:, None, None]
    memory_next = (
        memory
        + jnp.einsum(
            "lhd,lhe->hde",
            keys_mapped,
            value_rows.astype(jnp.float32),
            precision=lax.Precision.HIGHEST,
        )[None]
    )
    normalizer_next = normalizer + jnp.sum(keys_mapped, axis=0)[None]
    local_position = lax.axis_index("tp") * len_dev + jnp.arange(len_dev, dtype=jnp.int32)
    live_here = (local_position < valid_len).astype(jnp.float32)[None, :, None]

    def square_sum(values_in):
        return jnp.sum(values_in * values_in * live_here, axis=(1, 2))

    stat_terms = jnp.stack(
        [square_sum(result), square_sum(attn_branch), square_sum(mlp_branch)], axis=1
    )
    gain_two, gate_full, up_full, down_full = fetch_mlp(mlp_gain, w_gate, w_up, w_down)
    cot_all = lax.all_gather(cotangent, "tp", axis=1, tiled=True).reshape(seq_len, width)
    grad_hidden = jnp.dot(cot_all, down_full, preferred_element_type=jnp.float32)
    grad_down = contract_rows(cot_all, hidden)
    grad_gate_pre, grad_up_pre = glu_back(grad_hidden)
    gate_low = grad_gate_pre.astype(jnp.bfloat16)
    up_low = grad_up_pre.astype(jnp.bfloat16)
    two_terms = times_transpose(gate_low, gate_full) + times_transpose(up_low, up_full)
    grad_normed_two = lax.psum_scatter(
        two_terms.reshape(full_shape), "tp", scatter_dimension=1, tiled=True
    )
    grad_gate = contract_rows(flat_two, gate_low)
    grad_up = contract_rows(flat_two, up_low)
    grad_middle_in, grad_gain_two = norm_two_back(grad_normed_two)
    grad_middle = cotangent.astype(jnp.float32) + grad_middle_in
    gain_one, query_full, key_full, value_full, out_full = fetch_attention(
        attn_gain, w_query, w_key, w_value, w_out
    )
    branch_low = lax.all_gather(grad_middle.astype(jnp.bfloat16), "tp", axis=1, tiled=True).reshape(
        seq_len, width
    )
    grad_out = contract_rows(branch_low, combined)
    grad_combined = jnp.dot(branch_low, out_full, preferred_element_type=jnp.float32).reshape(
        head_shape
    )
    grad_query_mem, grad_local, grad_memory, grad_normalizer, grad_gate_logit = mix_pullback(
        grad_combined
    )
    grad_local_low = grad_local.astype(jnp.bfloat16)
    grad_query_att, grad_keys, grad_values = attend_backward(
        query_rows, key_rows, value_rows, grad_local_low, log_total, prefix_len, valid_len
    )
    query_low = (
        (grad_query_att + grad_query_mem)
        .astype(jnp.bfloat16)
        .reshape(seq_len, heads_here * head_dim)
    )
    key_low = grad_keys.astype(jnp.bfloat16).reshape(seq_len, heads_here * head_dim)
    value_low = grad_values.astype(jnp.bfloat16).reshape(seq_len, heads_here * head_dim)
    memory_grad = grad_memory[None]
    normalizer_grad = grad_normalizer[None]
    one_terms = (
        times_transpose(query_low, query_full)
        + times_transpose(key_low, key_full)
        + times_transpose(value_low, value_full)
    )
    grad_normed_one = lax.psum_scatter(
        one_terms.reshape(full_shape), "tp", scatter_dimension=1, tiled=True
    )
    grad_query = contract_rows(flat_one, query_low)
    grad_key = contract_rows(flat_one, key_low)
    grad_value = contract_rows(flat_one, value_low)
    grad_stream_in, grad_gain_one = norm_one_back(grad_normed_one)
    stream_grad = grad_middle + grad_stream_in
    gate_tiled = jnp.tile(grad_gate_logit, lax.axis_size("fsdp"))
    joined = (
        lax.psum_scatter(grad_gain_one, "fsdp", scatter_dimension=0, tiled=True),
        lax.psum_scatter(grad_query, "fsdp", scatter_dimension=0, tiled=True),
        lax.psum_scatter(grad_key, "fsdp", scatter_dimension=0, tiled=True),
        lax.psum_scatter(grad_value, "fsdp", scatter_dimension=0, tiled=True),
        lax.psum_scatter(grad_out, "fsdp", scatter_dimension=0, tiled=True),
        lax.psum_scatter(gate_tiled, "fsdp", scatter_dimension=0, tiled=True),
        lax.psum_scatter(grad_gain_two, "fsdp", scatter_dimension=0, tiled=True),
        lax.psum_scatter(grad_gate, "fsdp", scatter_dimension=0, tiled=True),
        lax.psum_scatter(grad_up, "fsdp", scatter_dimension=0, tiled=True),
        lax.psum_scatter(grad_down, "fsdp", scatter_dimension=0, tiled=True),
    )
    stat_sums, gain_one_grad, gain_two_grad = lax.psum((stat_terms, joined[0], joined[6]), "tp")
    token_count = valid_len.astype(jnp.float32) * width
    rms_stats = jnp.sqrt(stat_sums / token_count + rms_eps)
    return (
        stream_out,
        stream_grad,
        gain_one_grad,
        joined[1],
        joined[2],
        joined[3],
        joined[4],
        joined[5],
        gain_two_grad,
        joined[7],
        joined[8],
        joined[9],
        memory_next,
        normalizer_next,
        memory_grad,
        normalizer_grad,
        rms_stats,
    )


def solution(mesh):
    placed = (
        P("fsdp", "tp", None),
        P("fsdp"),
        P("fsdp", "tp"),
        P("fsdp", "tp"),
        P("fsdp", "tp"),
        P("fsdp", "tp"),
        P("tp"),
        P("fsdp"),
        P("fsdp", "tp"),
        P("fsdp", "tp"),
        P("fsdp", "tp"),
        P("fsdp", "tp", None, None),
        P("fsdp", "tp", None),
        P(),
        P(),
        P("fsdp", "tp", None),
    )
    return jax.shard_map(
        on_device,
        mesh=mesh,
        in_specs=placed,
        out_specs=(
            P("fsdp", "tp", None),
            P("fsdp", "tp", None),
            P("fsdp"),
            P("fsdp", "tp"),
            P("fsdp", "tp"),
            P("fsdp", "tp"),
            P("fsdp", "tp"),
            P("tp"),
            P("fsdp"),
            P("fsdp", "tp"),
            P("fsdp", "tp"),
            P("fsdp", "tp"),
            P("fsdp", "tp", None, None),
            P("fsdp", "tp", None),
            P("fsdp", "tp", None, None),
            P("fsdp", "tp", None),
            P("fsdp", None),
        ),
        check_vma=False,
    )
```

profile of v0, /device:TPU:0, one launch (start us, length us, event | category | flops | bytes accessed | tf_op | source)
XLA Modules:
  0.0 1943.7 jit_solution(17430341816614370978)
XLA Ops:
  40.5 82.9 %all-gather.14.cloned.1.call-done = bf16[1,1024,2048]{2,1,0:T(8,128)(2,1)} async-done(((bf16[1,256,2048]{2,1,0:T(8,128)(2,1)}), bf16[1,1024,2048]{2,1,0:T(8,128)(2,1)}) %all-gather.14.cloned.1.call-update) | async-done | bytes 4194320 | tf_op jit(solution)/shard_map/all_gather | solution.py:191
  130.9 20.9 %all-gather.16.cloned.1.call-done = bf16[2048,512]{1,0:T(8,128)(2,1)} async-done(((bf16[256,512]{1,0:T(8,128)(2,1)}), bf16[2048,512]{1,0:T(8,128)(2,1)}) %all-gather.16.cloned.1.call-update) | async-done | bytes 2097168 | tf_op jit(solution)/shard_map/all_gather | solution.py:143
  159.8 21.7 %all-gather.20.cloned.1.call-done = bf16[2048,512]{1,0:T(8,128)(2,1)} async-done(((bf16[256,512]{1,0:T(8,128)(2,1)}), bf16[2048,512]{1,0:T(8,128)(2,1)}) %all-gather.20.cloned.1.call-update) | async-done | bytes 2097168 | tf_op jit(solution)/shard_map/all_gather | solution.py:145
  190.0 68.2 %while.27 = (s32[]{:T(128)}, f32[2,512,4,128]{1,0,3,2:T(2,128)}, f32[2,4,512]{2,1,0:T(4,128)S(1)}, s32[]{:T(128)}, s32[2]{0:T(128)S(1)}, /*index=5*/s32[]{:T(128...) while((s32[]{:T(128)}, f32[2,512,4,128]{1,0,3,2:T(2,128)}, ...), condition=%wide.region_4.5_spmd, body=%wide.region_1.4_spmd.sunk | while | flops 1100481024 | bytes 35201168 | solution.py:81
  288.5 134.9 %reduce-scatter.12.cloned.1.call-done = f32[1,256,2048]{2,1,0:T(8,128)} async-done(((f32[1,1024,2048]{2,1,0:T(8,128)}), f32[1,256,2048]{2,1,0:T(8,128)}) %reduce-scatter.12.cloned.1.call-update) | async-done | bytes 2097168 | tf_op jit(solution)/shard_map/reduce_scatter | solution.py:213
  429.0 51.5 %all-gather.28.cloned.1.call-done = bf16[2048,2048]{1,0:T(8,128)(2,1)} async-done(((bf16[256,2048]{1,0:T(8,128)(2,1)}), bf16[2048,2048]{1,0:T(8,128)(2,1)}) %all-gather.28.cloned.1.call-update) | async-done | bytes 8388624 | tf_op jit(solution)/shard_map/all_gather | solution.py:154
  480.5 82.9 %all-gather.24.cloned.1.call-done = bf16[1,1024,2048]{2,1,0:T(8,128)(2,1)} async-done(((bf16[1,256,2048]{2,1,0:T(8,128)(2,1)}), bf16[1,1024,2048]{2,1,0:T(8,128)(2,1)}) %all-gather.24.cloned.1.call-update) | async-done | bytes 4194320 | tf_op jit(solution)/shard_map/all_gather | solution.py:222
  578.0 40.3 %all-gather.26.cloned.1.call-done = bf16[2048,2048]{1,0:T(8,128)(2,1)} async-done(((bf16[256,2048]{1,0:T(8,128)(2,1)}), bf16[2048,2048]{1,0:T(8,128)(2,1)}) %all-gather.26.cloned.1.call-update) | async-done | bytes 8388624 | tf_op jit(solution)/shard_map/all_gather | solution.py:153
  632.8 67.7 %all-gather.32.cloned.1.call-done = bf16[1,1024,2048]{2,1,0:T(8,128)(2,1)} async-done(((bf16[1,256,2048]{2,1,0:T(8,128)(2,1)}), bf16[1,1024,2048]{2,1,0:T(8,128)(2,1)}) %all-gather.32.cloned.1.call-update) | async-done | bytes 4194320 | tf_op jit(solution)/shard_map/all_gather | solution.py:258
  700.5 54.8 %all-gather.30.cloned.1.call-done = bf16[2048,2048]{1,0:T(8,128)(2,1)} async-done(((bf16[256,2048]{1,0:T(8,128)(2,1)}), bf16[2048,2048]{1,0:T(8,128)(2,1)}) %all-gather.30.cloned.1.call-update) | async-done | bytes 8388624 | tf_op jit(solution)/shard_map/all_gather | solution.py:155
  755.3 23.9 %multiply_convert_fusion.1 = (bf16[1024,2048]{1,0:T(8,128)(2,1)S(1)}, bf16[1024,2048]{1,0:T(8,128)(2,1)}, bf16[1024,2048]{1,0:T(8,128)(2,1)}) fusion(f32[1024,2048]{1,0:T(8,128)} %fusion.60, f32[1024,2048]{1,0:T(8,128)} %fusion.58, bf16[2048,2048]{1,0:T(8,128)(2,1)} %all-gather.30.cloned.1.call-done, bf16[1,1024,2048]{2,1,0:T(8,128)(2,1)} %all-gather.32.cloned.1.call-done), kind=kOutput, calls=%fused_computation.68 | convolution fusion | flops 8644460544 | bytes 41943040 | tf_op jit(solution)/shard_map/dot_general | solution.py:259
  822.4 129.2 %reduce-scatter.16.cloned.1.call-done = f32[1,256,2048]{2,1,0:T(8,128)} async-done(((f32[1,1024,2048]{2,1,0:T(8,128)}), f32[1,256,2048]{2,1,0:T(8,128)}) %reduce-scatter.16.cloned.1.call-update) | async-done | bytes 2097168 | tf_op jit(solution)/shard_map/reduce_scatter | solution.py:265
  951.6 147.6 %reduce-scatter.14.cloned.1.call-done = f32[1,256,2048]{2,1,0:T(8,128)} async-done(((f32[1,1024,2048]{2,1,0:T(8,128)}), f32[1,256,2048]{2,1,0:T(8,128)}) %reduce-scatter.14.cloned.1.call-update) | async-done | bytes 2097168 | tf_op jit(solution)/shard_map/reduce_scatter | solution.py:228
  1127.4 61.8 %all-gather.34.cloned.1.call-done = bf16[1,1024,2048]{2,1,0:T(8,128)(2,1)} async-done(((bf16[1,256,2048]{2,1,0:T(8,128)(2,1)}), bf16[1,1024,2048]{2,1,0:T(8,128)(2,1)}) %all-gather.34.cloned.1.call-update) | async-done | bytes 4194320 | tf_op jit(solution)/shard_map/all_gather | solution.py:275
  1205.1 104.8 %while.28 = (s32[]{:T(128)}, f32[1024,4,128]{0,2,1:T(8,128)S(1)}, f32[1024,4,128]{0,2,1:T(8,128)}, f32[2,512,4,128]{1,0,3,2:T(2,128)}, bf16[2,512,4,128]{3,1,2,0...) while((s32[]{:T(128)}, f32[1024,4,128]{0,2,1:T(8,128)S(1)}, ...), condition=%wide.region_12.13_spmd.clone, body=%wide.region_10.12_spmd.clone.sunk | while | flops 2720268800 | bytes 146867568 | solution.py:136
  1226.4 19.8 %dynamic_update_slice.18 = f32[2,512,4,128]{1,0,3,2:T(2,128)} dynamic-update-slice(f32[2,512,4,128]{1,0,3,2:T(2,128)} %get-tuple-element.567, f32[1,512,4,128]{1,0,3,2:T(1,128)} %copy.130, s32[]{:T(128)} %get-tuple-element.564, s32[]{:T(128)} %constant.55.clone.1..sunk.1, s32[]{:T(128)} %constant.55.clone.1..sunk.1, s32[]{:T(128)} %constant.55.clone.1..sunk.1) | dynamic-update-slice | bytes 2097156 | tf_op jit(solution)/shard_map/while/body/jit(dynamic_update_index_in_dim)/dynamic_update_slice | solution.py:81
  1409.6 64.6 %reduce-scatter.18.cloned.1.call-done = f32[1,256,2048]{2,1,0:T(8,128)} async-done(((f32[1,1024,2048]{2,1,0:T(8,128)}), f32[1,256,2048]{2,1,0:T(8,128)}) %reduce-scatter.18.cloned.1.call-update) | async-done | bytes 2097168 | tf_op jit(solution)/shard_map/reduce_scatter | solution.py:303
  1476.5 23.8 %all-reduce.3 = (f32[2048]{0:T(1024)S(1)}, f32[32]{0:T(128)S(1)}, f32[2048]{0:T(1024)S(1)}) all-reduce(f32[2048]{0:T(1024)S(1)} %get-tuple-element.291, f32[32]{0:T(128)S(1)} %tile.10, f32[2048]{0:T(1024)S(1)} %copy-done.33), channel_id=6, replica_groups=mesh['fsdp'=8,'tp'=4] {'fsdp'}, use_global_device_ids=true, to_apply=%region_17.18.clone | all-reduce | flops 4128 | bytes 33024
  1519.4 75.5 %reduce-scatter.28.cloned.1.call-done = f32[256,2048]{1,0:T(8,128)} async-done(((f32[2048,2048]{1,0:T(8,128)}), f32[256,2048]{1,0:T(8,128)}) %reduce-scatter.28.cloned.1.call-update) | async-done | bytes 2097168 | tf_op jit(solution)/shard_map/reduce_scatter | solution.py:320
  1594.9 120.0 %reduce-scatter.30.cloned.1.call-done = f32[256,2048]{1,0:T(8,128)} async-done(((f32[2048,2048]{1,0:T(8,128)}), f32[256,2048]{1,0:T(8,128)}) %reduce-scatter.30.cloned.1.call-update) | async-done | bytes 2097168 | tf_op jit(solution)/shard_map/reduce_scatter | solution.py:321
  1714.9 55.3 %reduce-scatter.26.cloned.1.call-done = f32[256,512]{1,0:T(8,128)} async-done(((f32[2048,512]{1,0:T(8,128)}), f32[256,512]{1,0:T(8,128)}) %reduce-scatter.26.cloned.1.call-update) | async-done | bytes 524304 | tf_op jit(solution)/shard_map/reduce_scatter | solution.py:317
  1770.2 55.5 %reduce-scatter.20.cloned.1.call-done = f32[256,512]{1,0:T(8,128)} async-done(((f32[2048,512]{1,0:T(8,128)}), f32[256,512]{1,0:T(8,128)}) %reduce-scatter.20.cloned.1.call-update) | async-done | bytes 524304 | tf_op jit(solution)/shard_map/reduce_scatter | solution.py:314
  1825.7 55.3 %reduce-scatter.22.cloned.1.call-done = f32[256,512]{1,0:T(8,128)} async-done(((f32[2048,512]{1,0:T(8,128)}), f32[256,512]{1,0:T(8,128)}) %reduce-scatter.22.cloned.1.call-update) | async-done | bytes 524304 | tf_op jit(solution)/shard_map/reduce_scatter | solution.py:315
  1881.0 55.7 %reduce-scatter.24.cloned.1.call-done = f32[256,512]{1,0:T(8,128)} async-done(((f32[2048,512]{1,0:T(8,128)}), f32[256,512]{1,0:T(8,128)}) %reduce-scatter.24.cloned.1.call-update) | async-done | bytes 524304 | tf_op jit(solution)/shard_map/reduce_scatter | solution.py:316
  (325 shorter events, 480.2 us)
Async XLA Ops:
  7.2 33.4 %all-gather.18.cloned.1.call-start = ((), (), s32[]{:S(2)}) async-start(), calls=%async_computation.13 | async-start | bytes 2359296 | tf_op jit(solution)/shard_map/all_gather | solution.py:144
  7.9 115.6 %all-gather.14.cloned.1.call-start = ((), (), s32[]{:S(2)}) async-start(), calls=%async_computation.11 | async-start | bytes 5242880 | tf_op jit(solution)/shard_map/all_gather | solution.py:191
  24.2 127.7 %all-gather.16.cloned.1.call-start = ((), (), s32[]{:S(2)}) async-start(), calls=%async_computation.12 | async-start | bytes 2359296 | tf_op jit(solution)/shard_map/all_gather | solution.py:143
  24.9 156.6 %all-gather.20.cloned.1.call-start = ((), (), s32[]{:S(2)}) async-start(), calls=%async_computation.14 | async-start | bytes 2359296 | tf_op jit(solution)/shard_map/all_gather | solution.py:145
  25.5 245.6 %all-gather.22.cloned.1.call-start = ((), (), s32[]{:S(2)}) async-start(), calls=%async_computation.15 | async-start | bytes 2359296 | tf_op jit(solution)/shard_map/all_gather | solution.py:146
  26.1 397.4 %reduce-scatter.12.cloned.1.call-start = ((), (), s32[]{:S(2)}) async-start(), calls=%async_computation.16 | async-start | bytes 10485760 | tf_op jit(solution)/shard_map/reduce_scatter | solution.py:213
  278.8 201.7 %all-gather.28.cloned.1.call-start = ((), (), s32[]{:S(2)}) async-start(), calls=%async_computation.19 | async-start | bytes 9437184 | tf_op jit(solution)/shard_map/all_gather | solution.py:154
  279.6 283.8 %all-gather.24.cloned.1.call-start = ((), (), s32[]{:S(2)}) async-start(), calls=%async_computation.17 | async-start | bytes 5242880 | tf_op jit(solution)/shard_map/all_gather | solution.py:222
  288.5 816.7 %copy-start.25 = (f32[8,1,256]{2,1,0:T(1,128)}, f32[8,1,256]{2,1,0:T(1,128)S(1)}, u32[]{:S(2)}) copy-start(f32[8,1,256]{2,1,0:T(1,128)S(1)} %convert_element_type.124) | copy-start | bytes 24580
  425.4 679.8 %copy-start.7 = (f32[1,256,2048]{2,1,0:T(8,128)}, f32[1,256,2048]{2,1,0:T(8,128)S(1)}, u32[]{:S(2)}) copy-start(f32[1,256,2048]{2,1,0:T(8,128)S(1)} %get-tuple-element.348) | copy-start | bytes 6291460
  426.8 191.4 %all-gather.26.cloned.1.call-start = ((), (), s32[]{:S(2)}) async-start(), calls=%async_computation.18 | async-start | bytes 9437184 | tf_op jit(solution)/shard_map/all_gather | solution.py:153
  427.6 272.9 %all-gather.32.cloned.1.call-start = ((), (), s32[]{:S(2)}) async-start(), calls=%async_computation.22 | async-start | bytes 5242880 | tf_op jit(solution)/shard_map/all_gather | solution.py:258
  428.2 327.1 %all-gather.30.cloned.1.call-start = ((), (), s32[]{:S(2)}) async-start(), calls=%async_computation.20 | async-start | bytes 9437184 | tf_op jit(solution)/shard_map/all_gather | solution.py:155
  428.9 522.7 %reduce-scatter.16.cloned.1.call-start = ((), (), s32[]{:S(2)}) async-start(), calls=%async_computation.23 | async-start | bytes 10485760 | tf_op jit(solution)/shard_map/reduce_scatter | solution.py:265
  807.0 292.2 %reduce-scatter.14.cloned.1.call-start = ((), (), s32[]{:S(2)}) async-start(), calls=%async_computation.21 | async-start | bytes 10485760 | tf_op jit(solution)/shard_map/reduce_scatter | solution.py:228
  821.7 367.4 %all-gather.34.cloned.1.call-start = ((), (), s32[]{:S(2)}) async-start(), calls=%async_computation.24 | async-start | bytes 5242880 | tf_op jit(solution)/shard_map/all_gather | solution.py:275
  1107.5 299.1 %reduce-scatter.32.cloned.1.call-start = ((), (), s32[]{:S(2)}) async-start(), calls=%async_computation.32 | async-start | bytes 18874368 | tf_op jit(solution)/shard_map/reduce_scatter | solution.py:322
  1123.3 350.9 %reduce-scatter.18.cloned.1.call-start = ((), (), s32[]{:S(2)}) async-start(), calls=%async_computation.25 | async-start | bytes 10485760 | tf_op jit(solution)/shard_map/reduce_scatter | solution.py:303
  1331.2 263.7 %reduce-scatter.28.cloned.1.call-start = ((), (), s32[]{:S(2)}) async-start(), calls=%async_computation.30 | async-start | bytes 18874368 | tf_op jit(solution)/shard_map/reduce_scatter | solution.py:320
  1346.8 368.1 %reduce-scatter.30.cloned.1.call-start = ((), (), s32[]{:S(2)}) async-start(), calls=%async_computation.31 | async-start | bytes 18874368 | tf_op jit(solution)/shard_map/reduce_scatter | solution.py:321
  1362.2 407.9 %reduce-scatter.26.cloned.1.call-start = ((), (), s32[]{:S(2)}) async-start(), calls=%async_computation.29 | async-start | bytes 4718592 | tf_op jit(solution)/shard_map/reduce_scatter | solution.py:317
  1369.2 456.6 %reduce-scatter.20.cloned.1.call-start = ((), (), s32[]{:S(2)}) async-start(), calls=%async_computation.26 | async-start | bytes 4718592 | tf_op jit(solution)/shard_map/reduce_scatter | solution.py:314
  1376.2 504.8 %reduce-scatter.22.cloned.1.call-start = ((), (), s32[]{:S(2)}) async-start(), calls=%async_computation.27 | async-start | bytes 4718592 | tf_op jit(solution)/shard_map/reduce_scatter | solution.py:315
  1382.9 553.8 %reduce-scatter.24.cloned.1.call-start = ((), (), s32[]{:S(2)}) async-start(), calls=%async_computation.28 | async-start | bytes 4718592 | tf_op jit(solution)/shard_map/reduce_scatter | solution.py:316
  (74 other events, 2908.5 us)
Sparse Core Ops, SparseCore 0:
  9.9 30.5 all-gather.17
  42.7 80.7 all-gather.13
  125.4 26.4 all-gather.15
  153.6 27.8 all-gather.19
  183.2 27.9 all-gather.21
  278.9 144.4 reduce-scatter.11
  425.3 55.0 all-gather.27
  482.6 80.7 all-gather.23
  565.3 52.9 all-gather.25
  619.7 80.7 all-gather.31
  702.4 52.9 all-gather.29
  807.1 144.4 reduce-scatter.15
  954.0 145.1 reduce-scatter.13
  1107.6 81.4 all-gather.33
  1192.5 114.4 reduce-scatter.31
  1331.4 142.8 reduce-scatter.17
  1478.2 116.6 reduce-scatter.27
  1598.9 115.9 reduce-scatter.29
  1718.8 51.3 reduce-scatter.25
  1774.3 51.3 reduce-scatter.19
  1829.7 51.2 reduce-scatter.21
  1885.3 51.3 reduce-scatter.23
where the time goes:
time: 1950 us; the launch traced here: 1940 us
  waiting for transfers between devices  1400 us (72%)
  matrix products  290 us (15%)
  local copies, waits for them, and re-layouts  135 us (7%)
  blocking collectives  55.1 us (3%)
  other arithmetic  48.7 us (2%)
    reduce_scatter x1, waiting for transfers between devices, on_device(): lax.psum_scatter(times_transpose(hidden, down_full).reshape(full_shape),...  148 us
    reduce_scatter x1, waiting for transfers between devices, on_device(): lax.psum_scatter(times_transpose(combined, out_full).reshape(full_shape),...  135 us
    reduce_scatter x1, waiting for transfers between devices, on_device(): lax.psum_scatter(two_terms.reshape(full_shape), 'tp', scatter_dimension=1...  129 us
    reduce_scatter x1, waiting for transfers between devices, on_device(): lax.psum_scatter(grad_up, 'fsdp', scatter_dimension=0, tiled=True)  120 us
    dynamic_update_slice x8, local copies, waits for them, and re-layouts, attend_forward(): lax.map(one_block, (split_blocks(query_rows, block_rows), block_first))  90.7 us
    all_gather x1, waiting for transfers between devices, on_device(): lax.all_gather(normed_local.astype(jnp.bfloat16), 'tp', axis=1, tiled=True)  82.9 us
    all_gather x1, waiting for transfers between devices, on_device(): lax.all_gather(normed_mid.astype(jnp.bfloat16), 'tp', axis=1, tiled=True)  82.9 us
    reduce_scatter x1, waiting for transfers between devices, on_device(): lax.psum_scatter(grad_gate, 'fsdp', scatter_dimension=0, tiled=True)  75.5 us
  transfers between devices with their start and end apart: 22, of which 20 were waited for; matrix products, arithmetic and copies ran while one was open for 20% of the time, Pallas kernels for 0%

commit v1 on v0

v1 whole, which is shorter than its diff:
```python
import functools

import jax
import jax.numpy as jnp
from jax import lax
from jax.experimental import pallas as pl
from jax.experimental.pallas import tpu as pltpu
from jax.sharding import PartitionSpec as P

NEG = -1e30
LOG2E = 1.4426950408889634


def split_two(x):
    high = x.astype(jnp.bfloat16)
    return high, (x - high.astype(jnp.float32)).astype(jnp.bfloat16)


def dot32(a, b, dims):
    return lax.dot_general(a, b, (dims, ((), ())), preferred_element_type=jnp.float32)


def dot_three(a, b, dims):
    ah, al = split_two(a)
    bh, bl = split_two(b)
    return dot32(ah, bh, dims) + dot32(ah, bl, dims) + dot32(al, bh, dims)


NN, NT, TN = ((1,), (0,)), ((1,), (1,)), ((0,), (0,))


def mapped(v):
    return jnp.where(v > 0, v + 1.0, jnp.exp(jnp.minimum(v, 0.0)))


def key_reach(first, rows, keys):
    return min(keys, max(keys // 2, first + rows))


def key_limit(first, rows, prefix, valid):
    row = first + lax.broadcasted_iota(jnp.int32, (1, rows), 1)
    return jnp.minimum(valid - 1, jnp.maximum(row, prefix - 1))


def forward_kernel(bounds, q_ref, k_ref, v_ref, mem_ref, norm_ref, gate_ref, comb_ref, mix_ref, lse_ref, memo_ref, normo_ref, *, block):
    keys, hd = k_ref.shape
    prefix, valid = bounds[0], bounds[1]
    scale = hd ** -0.5 * LOG2E
    gate = jax.nn.sigmoid(gate_ref[0])
    memory = mem_ref[0]
    norm = norm_ref[0]
    for first in range(0, keys, block):
        reach = key_reach(first, block, keys)
        q = q_ref[first : first + block, :]
        s = dot32(k_ref[:reach, :], q, NT) * scale
        limit = key_limit(first, block, prefix, valid)
        s = jnp.where(lax.broadcasted_iota(jnp.int32, s.shape, 0) <= limit, s, NEG)
        top = jnp.max(s, axis=0, keepdims=True)
        p = jnp.exp2(s - top)
        total = jnp.sum(p, axis=0, keepdims=True)
        mixed = dot32(v_ref[:reach, :], p.astype(jnp.bfloat16), TN) / total
        mixed = mixed.T
        lse_ref[0, :, first : first + block] = top + jnp.log2(total)
        qm = mapped(q.astype(jnp.float32))
        denominator = jnp.sum(qm * norm, axis=-1, keepdims=True)
        retrieved = dot_three(qm, memory, NN) / denominator
        mix_ref[first : first + block, :] = mixed
        comb_ref[first : first + block, :] = (gate * retrieved + (1.0 - gate) * mixed).astype(jnp.bfloat16)
    km = mapped(k_ref[...].astype(jnp.float32))
    km = jnp.where(lax.broadcasted_iota(jnp.int32, km.shape, 0) < valid, km, 0.0)
    kh, kl = split_two(km)
    memo_ref[0] = memory + dot32(kh, v_ref[...], TN) + dot32(kl, v_ref[...], TN)
    normo_ref[0] = norm + jnp.sum(km, axis=0, keepdims=True)


def backward_kernel(bounds, q_ref, k_ref, v_ref, gc_ref, mix_ref, lse_ref, mem_ref, norm_ref, gate_ref, dq_ref, dk_ref, dv_ref, dmem_ref, dnorm_ref, dgate_ref, dk_acc, dv_acc, *, block):
    keys, hd = k_ref.shape
    prefix, valid = bounds[0], bounds[1]
    scale = hd ** -0.5
    gate = jax.nn.sigmoid(gate_ref[0])
    memory = mem_ref[0]
    norm = norm_ref[0]
    dmem = jnp.zeros((hd, hd), jnp.float32)
    dnorm = jnp.zeros((1, hd), jnp.float32)
    dgate = jnp.zeros((1, hd), jnp.float32)
    for first in range(keys - block, -1, -block):
        reach = key_reach(first, block, keys)
        rows = slice(first, first + block)
        q = q_ref[rows, :]
        gc = gc_ref[rows, :].astype(jnp.float32)
        mixed = mix_ref[rows, :]
        qm = mapped(q.astype(jnp.float32))
        inverse = 1.0 / jnp.sum(qm * norm, axis=-1, keepdims=True)
        retrieved = dot_three(qm, memory, NN) * inverse
        dgate = dgate + jnp.sum(gc * (retrieved - mixed), axis=0, keepdims=True)
        gnum = gate * gc * inverse
        gden = -jnp.sum(gnum * retrieved, axis=-1, keepdims=True)
        dmem = dmem + dot_three(qm, gnum, TN)
        dnorm = dnorm + jnp.sum(gden * qm, axis=0, keepdims=True)
        dq_mem = (dot_three(gnum, memory, NT) + gden * norm) * jnp.minimum(qm, 1.0)
        low = ((1.0 - gate) * gc).astype(jnp.bfloat16)
        delta = jnp.sum((low.astype(jnp.float32) * mixed).T, axis=0, keepdims=True)
        s = dot32(k_ref[:reach, :], q, NT) * (scale * LOG2E)
        limit = key_limit(first, block, prefix, valid)
        s = jnp.where(lax.broadcasted_iota(jnp.int32, s.shape, 0) <= limit, s - lse_ref[0, :, rows], NEG)
        p = jnp.exp2(s)
        gp = dot32(v_ref[:reach, :], low, NT)
        gs = (p * (gp - delta)).astype(jnp.bfloat16)
        dv = dot32(p.astype(jnp.bfloat16), low, NN)
        dk = dot32(gs, q, NN)
        if first == keys - block:
            dv_acc[...] = dv
            dk_acc[...] = dk
        else:
            dv_acc[:reach, :] += dv
            dk_acc[:reach, :] += dk
        dq = dot32(k_ref[:reach, :], gs, TN).T * scale
        dq_ref[rows, :] = (dq + dq_mem).astype(jnp.bfloat16)
    dk_ref[...] = (dk_acc[...] * scale).astype(jnp.bfloat16)
    dv_ref[...] = dv_acc[...].astype(jnp.bfloat16)
    dmem_ref[0] = dmem
    dnorm_ref[0] = dnorm
    dgate_ref[0] = dgate * (gate * (1.0 - gate))


def head_specs(keys, hd):
    rows = pl.BlockSpec((keys, hd), lambda h: (0, h))
    square = pl.BlockSpec((1, hd, hd), lambda h: (h, 0, 0))
    line = pl.BlockSpec((1, 1, hd), lambda h: (h, 0, 0))
    long = pl.BlockSpec((1, 1, keys), lambda h: (h, 0, 0))
    return rows, square, line, long


def attend(bounds, q, k, v, memory, norm, gate, block=256):
    keys = q.shape[0]
    heads, hd = memory.shape[:2]
    rows, square, line, long = head_specs(keys, hd)
    f32 = jnp.float32
    S = jax.ShapeDtypeStruct
    return pl.pallas_call(
        functools.partial(forward_kernel, block=block),
        grid=(heads,),
        in_specs=[pl.BlockSpec(memory_space=pltpu.SMEM), rows, rows, rows, square, line, line],
        out_specs=[rows, rows, long, square, line],
        out_shape=[S(q.shape, jnp.bfloat16), S(q.shape, f32), S((heads, 1, keys), f32), S((heads, hd, hd), f32), S((heads, 1, hd), f32)],
        compiler_params=pltpu.CompilerParams(vmem_limit_bytes=48 * 2**20),
        name="attend_forward",
    )(bounds, q, k, v, memory, norm.reshape(heads, 1, hd), jnp.broadcast_to(gate[:, None, None], (heads, 1, hd)))


def attend_back(bounds, q, k, v, gc, mix, lse, memory, norm, gate, block=256):
    keys = q.shape[0]
    heads, hd = memory.shape[:2]
    rows, square, line, long = head_specs(keys, hd)
    f32 = jnp.float32
    S = jax.ShapeDtypeStruct
    low = S(q.shape, jnp.bfloat16)
    return pl.pallas_call(
        functools.partial(backward_kernel, block=block),
        grid=(heads,),
        in_specs=[pl.BlockSpec(memory_space=pltpu.SMEM), rows, rows, rows, rows, rows, long, square, line, line],
        out_specs=[rows, rows, rows, square, line, line],
        out_shape=[low, low, low, S((heads, hd, hd), f32), S((heads, 1, hd), f32), S((heads, 1, hd), f32)],
        scratch_shapes=[pltpu.VMEM((keys, hd), f32), pltpu.VMEM((keys, hd), f32)],
        compiler_params=pltpu.CompilerParams(vmem_limit_bytes=48 * 2**20),
        name="attend_backward",
    )(bounds, q, k, v, gc, mix, lse, memory, norm.reshape(heads, 1, hd), jnp.broadcast_to(gate[:, None, None], (heads, 1, hd)))

norm_eps = 1e-06
rms_eps = 1e-06


def normalize(rows_in):
    return rows_in * lax.rsqrt(jnp.mean(rows_in * rows_in, axis=-1, keepdims=True) + norm_eps)


def norm_gain(rows_in, gain_full):
    return normalize(rows_in) * gain_full


def glu_product(gate_pre, up_pre):
    return jax.nn.gelu(gate_pre) * up_pre


def contract_rows(first_mat, second_mat):
    return lax.dot_general(
        first_mat, second_mat, (((0,), (0,)), ((), ())), preferred_element_type=jnp.float32
    )


def times_transpose(first_mat, second_mat):
    return lax.dot_general(
        first_mat, second_mat, (((1,), (1,)), ((), ())), preferred_element_type=jnp.float32
    )


def scatter_low(terms, axis, dim):
    return lax.psum_scatter(
        terms.astype(jnp.bfloat16), axis, scatter_dimension=dim, tiled=True
    ).astype(jnp.float32)


def fetch_attention(attn_gain, w_query, w_key, w_value, w_out):
    return (
        lax.all_gather(attn_gain, "fsdp", axis=0, tiled=True),
        lax.all_gather(w_query, "fsdp", axis=0, tiled=True),
        lax.all_gather(w_key, "fsdp", axis=0, tiled=True),
        lax.all_gather(w_value, "fsdp", axis=0, tiled=True),
        lax.all_gather(w_out, "fsdp", axis=0, tiled=True),
    )


def fetch_mlp(mlp_gain, w_gate, w_up, w_down):
    return (
        lax.all_gather(mlp_gain, "fsdp", axis=0, tiled=True),
        lax.all_gather(w_gate, "fsdp", axis=0, tiled=True),
        lax.all_gather(w_up, "fsdp", axis=0, tiled=True),
        lax.all_gather(w_down, "fsdp", axis=0, tiled=True),
    )


def on_device(
    stream,
    attn_gain,
    w_query,
    w_key,
    w_value,
    w_out,
    mem_gate,
    mlp_gain,
    w_gate,
    w_up,
    w_down,
    memory,
    normalizer,
    prefix,
    valid,
    cotangent,
):
    len_dev, width = (stream.shape[1], stream.shape[2])
    seq_len = len_dev * lax.axis_size("tp")
    seq_here = lax.axis_index("fsdp")
    prefix_len = prefix[seq_here]
    valid_len = valid[seq_here]
    full_shape = (1, seq_len, width)
    gain_one, query_full, key_full, value_full, out_full = fetch_attention(
        attn_gain, w_query, w_key, w_value, w_out
    )
    stream_f = stream.astype(jnp.float32)
    normed_local, norm_one_back = jax.vjp(norm_gain, stream_f, gain_one.astype(jnp.float32))
    normed_one = lax.all_gather(normed_local.astype(jnp.bfloat16), "tp", axis=1, tiled=True)
    flat_one = normed_one.reshape(seq_len, width)
    def project(weight):
        return jnp.dot(flat_one, weight, preferred_element_type=jnp.float32).astype(jnp.bfloat16)

    query_rows, key_rows, value_rows = project(query_full), project(key_full), project(value_full)
    bounds = jnp.stack([prefix_len, valid_len])
    combined, local_mix, log_total, memory_next, normalizer_next = attend(
        bounds, query_rows, key_rows, value_rows, memory[0], normalizer[0], mem_gate
    )
    attn_branch = scatter_low(times_transpose(combined, out_full).reshape(full_shape), "tp", 1)
    middle = stream_f + attn_branch
    gain_two, gate_full, up_full, down_full = fetch_mlp(mlp_gain, w_gate, w_up, w_down)
    normed_mid, norm_two_back = jax.vjp(norm_gain, middle, gain_two.astype(jnp.float32))
    normed_two = lax.all_gather(normed_mid.astype(jnp.bfloat16), "tp", axis=1, tiled=True)
    flat_two = normed_two.reshape(seq_len, width)
    gate_pre = jnp.dot(flat_two, gate_full, preferred_element_type=jnp.float32)
    up_pre = jnp.dot(flat_two, up_full, preferred_element_type=jnp.float32)
    hidden_f, glu_back = jax.vjp(glu_product, gate_pre, up_pre)
    hidden = hidden_f.astype(jnp.bfloat16)
    mlp_branch = scatter_low(times_transpose(hidden, down_full).reshape(full_shape), "tp", 1)
    result = middle + mlp_branch
    stream_out = result.astype(jnp.bfloat16)
    local_position = lax.axis_index("tp") * len_dev + jnp.arange(len_dev, dtype=jnp.int32)
    live_here = (local_position < valid_len).astype(jnp.float32)[None, :, None]

    def square_sum(values_in):
        return jnp.sum(values_in * values_in * live_here, axis=(1, 2))

    stat_terms = jnp.stack(
        [square_sum(result), square_sum(attn_branch), square_sum(mlp_branch)], axis=1
    )
    gain_two, gate_full, up_full, down_full = fetch_mlp(mlp_gain, w_gate, w_up, w_down)
    cot_all = lax.all_gather(cotangent, "tp", axis=1, tiled=True).reshape(seq_len, width)
    grad_hidden = jnp.dot(cot_all, down_full, preferred_element_type=jnp.float32)
    grad_down = contract_rows(cot_all, hidden)
    grad_gate_pre, grad_up_pre = glu_back(grad_hidden)
    gate_low = grad_gate_pre.astype(jnp.bfloat16)
    up_low = grad_up_pre.astype(jnp.bfloat16)
    two_terms = times_transpose(gate_low, gate_full) + times_transpose(up_low, up_full)
    grad_normed_two = scatter_low(two_terms.reshape(full_shape), "tp", 1)
    grad_gate = contract_rows(flat_two, gate_low)
    grad_up = contract_rows(flat_two, up_low)
    grad_middle_in, grad_gain_two = norm_two_back(grad_normed_two)
    grad_middle = cotangent.astype(jnp.float32) + grad_middle_in
    gain_one, query_full, key_full, value_full, out_full = fetch_attention(
        attn_gain, w_query, w_key, w_value, w_out
    )
    branch_low = lax.all_gather(grad_middle.astype(jnp.bfloat16), "tp", axis=1, tiled=True).reshape(
        seq_len, width
    )
    grad_out = contract_rows(branch_low, combined)
    grad_combined = jnp.dot(branch_low, out_full, preferred_element_type=jnp.float32)
    query_low, key_low, value_low, grad_memory, grad_normalizer, gate_parts = attend_back(
        bounds, query_rows, key_rows, value_rows, grad_combined, local_mix, log_total,
        memory[0], normalizer[0], mem_gate,
    )
    grad_gate_logit = jnp.sum(gate_parts, axis=(1, 2))
    one_terms = (
        times_transpose(query_low, query_full)
        + times_transpose(key_low, key_full)
        + times_transpose(value_low, value_full)
    )
    grad_normed_one = scatter_low(one_terms.reshape(full_shape), "tp", 1)
    grad_query = contract_rows(flat_one, query_low)
    grad_key = contract_rows(flat_one, key_low)
    grad_value = contract_rows(flat_one, value_low)
    grad_stream_in, grad_gain_one = norm_one_back(grad_normed_one)
    stream_grad = grad_middle + grad_stream_in
    gate_tiled = jnp.tile(grad_gate_logit, lax.axis_size("fsdp"))
    joined = (
        lax.psum_scatter(grad_gain_one, "fsdp", scatter_dimension=0, tiled=True),
        scatter_low(grad_query, "fsdp", 0),
        scatter_low(grad_key, "fsdp", 0),
        scatter_low(grad_value, "fsdp", 0),
        scatter_low(grad_out, "fsdp", 0),
        lax.psum_scatter(gate_tiled, "fsdp", scatter_dimension=0, tiled=True),
        lax.psum_scatter(grad_gain_two, "fsdp", scatter_dimension=0, tiled=True),
        scatter_low(grad_gate, "fsdp", 0),
        scatter_low(grad_up, "fsdp", 0),
        scatter_low(grad_down, "fsdp", 0),
    )
    stat_sums, gain_one_grad, gain_two_grad = lax.psum((stat_terms, joined[0], joined[6]), "tp")
    token_count = valid_len.astype(jnp.float32) * width
    rms_stats = jnp.sqrt(stat_sums / token_count + rms_eps)
    return (
        stream_out,
        stream_grad,
        gain_one_grad,
        joined[1],
        joined[2],
        joined[3],
        joined[4],
        joined[5],
        gain_two_grad,
        joined[7],
        joined[8],
        joined[9],
        memory_next[None],
        normalizer_next[:, 0][None],
        grad_memory[None],
        grad_normalizer[:, 0][None],
        rms_stats,
    )


def solution(mesh):
    placed = (
        P("fsdp", "tp", None),
        P("fsdp"),
        P("fsdp", "tp"),
        P("fsdp", "tp"),
        P("fsdp", "tp"),
        P("fsdp", "tp"),
        P("tp"),
        P("fsdp"),
        P("fsdp", "tp"),
        P("fsdp", "tp"),
        P("fsdp", "tp"),
        P("fsdp", "tp", None, None),
        P("fsdp", "tp", None),
        P(),
        P(),
        P("fsdp", "tp", None),
    )
    return jax.shard_map(
        on_device,
        mesh=mesh,
        in_specs=placed,
        out_specs=(
            P("fsdp", "tp", None),
            P("fsdp", "tp", None),
            P("fsdp"),
            P("fsdp", "tp"),
            P("fsdp", "tp"),
            P("fsdp", "tp"),
            P("fsdp", "tp"),
            P("tp"),
            P("fsdp"),
            P("fsdp", "tp"),
            P("fsdp", "tp"),
            P("fsdp", "tp"),
            P("fsdp", "tp", None, None),
            P("fsdp", "tp", None),
            P("fsdp", "tp", None, None),
            P("fsdp", "tp", None),
            P("fsdp", None),
        ),
        check_vma=False,
    )
```

time: 1950 us -> 1460 us (0.75)
  waiting for transfers between devices: 1400 us -> 1100 us
  local copies, waits for them, and re-layouts: 135 us -> 11.6 us
  matrix products: 290 us -> 200 us
  Pallas kernels: 0 us -> 25.7 us
    reduce_scatter x11, waiting for transfers between devices: 894 us -> 611 us  [scatter_low(): lax.psum_scatter(terms.astype(jnp.bfloat16), axis, scatter_dimension=dim,...]
    dynamic_update_slice x8 -> x0, local copies, waits for them, and re-layouts: 90.7 us -> none  [attend_forward(): lax.map(one_block, (split_blocks(query_rows, block_rows), block_first))]
    dot_general x23 -> x3, matrix products: 94.2 us -> 15.6 us  [project(): jnp.dot(flat_one, weight, preferred_element_type=jnp.float32)]
    pallas_call x0 -> x2, Pallas kernels: none -> 25.7 us  [the longest x1 15.4 us: attend_back(): pl.pallas_call(functools.partial(backward_kernel, block=block), grid=(hea...]
    all_gather x1, waiting for transfers between devices: 61.8 us -> 38.3 us  [on_device(): lax.all_gather(grad_middle.astype(jnp.bfloat16), 'tp', axis=1, tiled=True)]
  transfers between devices with their start and end apart: 22 -> 22, of which waited for: 20 -> 22; matrix products, arithmetic and copies ran while one was open for 20% -> 12% of each run, Pallas kernels for 0% -> 2%
where the time goes in v1:
time: 1460 us
  waiting for transfers between devices  1100 us (75%)
  matrix products  200 us (14%)
  blocking collectives  55 us (4%)
  other arithmetic  40 us (3%)
  Pallas kernels  25.7 us (2%)
  between operations  16.9 us (1%)
    reduce_scatter x11, waiting for transfers between devices, scatter_low(): lax.psum_scatter(terms.astype(jnp.bfloat16), axis, scatter_dimension=dim,...  611 us
    all_gather x1, waiting for transfers between devices, on_device(): lax.all_gather(normed_mid.astype(jnp.bfloat16), 'tp', axis=1, tiled=True)  83 us
    all_gather x1, waiting for transfers between devices, on_device(): lax.all_gather(normed_local.astype(jnp.bfloat16), 'tp', axis=1, tiled=True)  82.9 us
    all_gather x1, waiting for transfers between devices, on_device(): lax.all_gather(cotangent, 'tp', axis=1, tiled=True).reshape(seq_len, width)  67.7 us
    dot_general x7, matrix products, contract_rows(): lax.dot_general(first_mat, second_mat, (((0,), (0,)), ((), ())), preferre...  64.3 us
    dot_general x7, matrix products, times_transpose(): lax.dot_general(first_mat, second_mat, (((1,), (1,)), ((), ())), preferre...  60.1 us
    all_gather x1, waiting for transfers between devices, fetch_mlp(): lax.all_gather(w_down, 'fsdp', axis=0, tiled=True)  55 us
    all_gather x1, waiting for transfers between devices, fetch_mlp(): lax.all_gather(w_up, 'fsdp', axis=0, tiled=True)  50.3 us
  transfers between devices with their start and end apart: 22, of which 22 were waited for; matrix products, arithmetic and copies ran while one was open for 12% of the time, Pallas kernels for 2%

profile of v1, /device:TPU:0, one launch (start us, length us, event | category | flops | bytes accessed | tf_op | source)
XLA Modules:
  0.0 1455.2 jit_solution(17119976796035559696)
XLA Ops:
  40.6 82.9 %all-gather.14.cloned.1.call-done = bf16[1,1024,2048]{2,1,0:T(8,128)(2,1)} async-done(((bf16[1,256,2048]{2,1,0:T(8,128)(2,1)}), bf16[1,1024,2048]{2,1,0:T(8,128)(2,1)}) %all-gather.14.cloned.1.call-update) | async-done | bytes 4194320 | tf_op jit(solution)/shard_map/all_gather | solution.py:251
  128.7 23.2 %all-gather.18.cloned.1.call-done = bf16[2048,512]{1,0:T(8,128)(2,1)} async-done(((bf16[256,512]{1,0:T(8,128)(2,1)}), bf16[2048,512]{1,0:T(8,128)(2,1)}) %all-gather.18.cloned.1.call-update) | async-done | bytes 2097168 | tf_op jit(solution)/shard_map/all_gather | solution.py:207
  157.1 24.4 %all-gather.20.cloned.1.call-done = bf16[2048,512]{1,0:T(8,128)(2,1)} async-done(((bf16[256,512]{1,0:T(8,128)(2,1)}), bf16[2048,512]{1,0:T(8,128)(2,1)}) %all-gather.20.cloned.1.call-update) | async-done | bytes 2097168 | tf_op jit(solution)/shard_map/all_gather | solution.py:208
  227.2 67.2 %reduce-scatter.12.cloned.1.call-done = bf16[1,256,2048]{2,1,0:T(8,128)(2,1)} async-done(((bf16[1,1024,2048]{2,1,0:T(8,128)(2,1)}), bf16[1,256,2048]{2,1,0:T(8,128)(2,1)}) %reduce-scatter.12.cloned.1.call-update) | async-done | bytes 1048592 | tf_op jit(solution)/shard_map/reduce_scatter | solution.py:198
  301.2 50.3 %all-gather.28.cloned.1.call-done = bf16[2048,2048]{1,0:T(8,128)(2,1)} async-done(((bf16[256,2048]{1,0:T(8,128)(2,1)}), bf16[2048,2048]{1,0:T(8,128)(2,1)}) %all-gather.28.cloned.1.call-update) | async-done | bytes 8388624 | tf_op jit(solution)/shard_map/all_gather | solution.py:217
  351.4 83.0 %all-gather.24.cloned.1.call-done = bf16[1,1024,2048]{2,1,0:T(8,128)(2,1)} async-done(((bf16[1,256,2048]{2,1,0:T(8,128)(2,1)}), bf16[1,1024,2048]{2,1,0:T(8,128)(2,1)}) %all-gather.24.cloned.1.call-update) | async-done | bytes 4194320 | tf_op jit(solution)/shard_map/all_gather | solution.py:265
  434.5 14.6 %fusion.18 = f32[1024,2048]{1,0:T(8,128)} fusion(bf16[2048,2048]{1,0:T(8,128)(2,1)} %all-gather.28.cloned.1.call-done, bf16[1,1024,2048]{2,1,0:T(8,128)(2,1)} %all-gather.24.cloned.1.call-done), kind=kOutput, calls=%fused_computation.28 | convolution fusion | flops 8589934592 | bytes 20971520 | tf_op jit(solution)/shard_map/dot_general | solution.py:268
  449.0 40.4 %all-gather.26.cloned.1.call-done = bf16[2048,2048]{1,0:T(8,128)(2,1)} async-done(((bf16[256,2048]{1,0:T(8,128)(2,1)}), bf16[2048,2048]{1,0:T(8,128)(2,1)}) %all-gather.26.cloned.1.call-update) | async-done | bytes 8388624 | tf_op jit(solution)/shard_map/all_gather | solution.py:216
  489.5 14.5 fusion.20
  504.0 67.7 %all-gather.32.cloned.1.call-done = bf16[1,1024,2048]{2,1,0:T(8,128)(2,1)} async-done(((bf16[1,256,2048]{2,1,0:T(8,128)(2,1)}), bf16[1,1024,2048]{2,1,0:T(8,128)(2,1)}) %all-gather.32.cloned.1.call-update) | async-done | bytes 4194320 | tf_op jit(solution)/shard_map/all_gather | solution.py:284
  571.8 55.0 %all-gather.30.cloned.1.call-done = bf16[2048,2048]{1,0:T(8,128)(2,1)} async-done(((bf16[256,2048]{1,0:T(8,128)(2,1)}), bf16[2048,2048]{1,0:T(8,128)(2,1)}) %all-gather.30.cloned.1.call-update) | async-done | bytes 8388624 | tf_op jit(solution)/shard_map/all_gather | solution.py:218
  626.8 23.7 %multiply_convert_fusion = (bf16[1024,2048]{1,0:T(8,128)(2,1)S(1)}, bf16[1024,2048]{1,0:T(8,128)(2,1)}, bf16[1024,2048]{1,0:T(8,128)(2,1)}) fusion(f32[1024,2048]{1,0:T(8,128)} %fusion.20, f32[1024,2048]{1,0:T(8,128)} %fusion.18, bf16[2048,2048]{1,0:T(8,128)(2,1)} %all-gather.30.cloned.1.call-done, bf16[1,1024,2048]{2,1,0:T(8,128)(2,1)} %all-gather.32.cloned.1.call-done), kind=kOutput, calls=%fused_computation.12 | convolution fusion | flops 8644460544 | bytes 41943040 | tf_op jit(solution)/shard_map/dot_general | solution.py:285
  692.3 62.1 %reduce-scatter.16.cloned.1.call-done = bf16[1,256,2048]{2,1,0:T(8,128)(2,1)} async-done(((bf16[1,1024,2048]{2,1,0:T(8,128)(2,1)}), bf16[1,256,2048]{2,1,0:T(8,128)(2,1)}) %reduce-scatter.16.cloned.1.call-update) | async-done | bytes 1048592 | tf_op jit(solution)/shard_map/reduce_scatter | solution.py:198
  754.4 79.6 %reduce-scatter.14.cloned.1.call-done = bf16[1,256,2048]{2,1,0:T(8,128)(2,1)} async-done(((bf16[1,1024,2048]{2,1,0:T(8,128)(2,1)}), bf16[1,256,2048]{2,1,0:T(8,128)(2,1)}) %reduce-scatter.14.cloned.1.call-update) | async-done | bytes 1048592 | tf_op jit(solution)/shard_map/reduce_scatter | solution.py:198
  884.8 38.3 %all-gather.34.cloned.1.call-done = bf16[1,1024,2048]{2,1,0:T(8,128)(2,1)} async-done(((bf16[1,256,2048]{2,1,0:T(8,128)(2,1)}), bf16[1,1024,2048]{2,1,0:T(8,128)(2,1)}) %all-gather.34.cloned.1.call-update) | async-done | bytes 4194320 | tf_op jit(solution)/shard_map/all_gather | solution.py:299
  936.4 15.4 %attend_backward.1 = (bf16[1024,512]{1,0:T(8,128)(2,1)S(1)}, bf16[1024,512]{1,0:T(8,128)(2,1)S(1)}, bf16[1024,512]{1,0:T(8,128)(2,1)S(1)}, f32[4,128,128]{2,1,0:...) custom-call(s32[2]{0:T(128)S(1)} %copy-done.8, bf16[1024,512]{1,0:T(8,128)(2,1)S(1)} %fusion.62.q_ref, ...), custom_call_target="tpu_custom_call" | custom-call | tf_op jit(solution)/shard_map/attend_backward/pallas_call | solution.py:158
  999.5 71.8 %reduce-scatter.30.cloned.1.call-done = bf16[256,2048]{1,0:T(8,128)(2,1)} async-done(((bf16[2048,2048]{1,0:T(8,128)(2,1)}), bf16[256,2048]{1,0:T(8,128)(2,1)}) %reduce-scatter.30.cloned.1.call-update) | async-done | bytes 1048592 | tf_op jit(solution)/shard_map/reduce_scatter | solution.py:198
  1074.1 72.2 %reduce-scatter.32.cloned.1.call-done = bf16[256,2048]{0,1:T(8,128)(2,1)} async-done(((bf16[2048,2048]{0,1:T(8,128)(2,1)}), bf16[256,2048]{0,1:T(8,128)(2,1)}) %reduce-scatter.32.cloned.1.call-update) | async-done | bytes 1048592 | tf_op jit(solution)/shard_map/reduce_scatter | solution.py:198
  1149.1 41.6 %reduce-scatter.26.cloned.1.call-done = bf16[256,512]{1,0:T(8,128)(2,1)} async-done(((bf16[2048,512]{1,0:T(8,128)(2,1)}), bf16[256,512]{1,0:T(8,128)(2,1)}) %reduce-scatter.26.cloned.1.call-update) | async-done | bytes 262160 | tf_op jit(solution)/shard_map/reduce_scatter | solution.py:198
  1192.5 43.7 %reduce-scatter.20.cloned.1.call-done = bf16[256,512]{1,0:T(8,128)(2,1)} async-done(((bf16[2048,512]{1,0:T(8,128)(2,1)}), bf16[256,512]{1,0:T(8,128)(2,1)}) %reduce-scatter.20.cloned.1.call-update) | async-done | bytes 262160 | tf_op jit(solution)/shard_map/reduce_scatter | solution.py:198
  1237.9 42.6 %reduce-scatter.22.cloned.1.call-done = bf16[256,512]{1,0:T(8,128)(2,1)} async-done(((bf16[2048,512]{1,0:T(8,128)(2,1)}), bf16[256,512]{1,0:T(8,128)(2,1)}) %reduce-scatter.22.cloned.1.call-update) | async-done | bytes 262160 | tf_op jit(solution)/shard_map/reduce_scatter | solution.py:198
  1282.3 43.1 %reduce-scatter.24.cloned.1.call-done = bf16[256,512]{1,0:T(8,128)(2,1)} async-done(((bf16[2048,512]{1,0:T(8,128)(2,1)}), bf16[256,512]{1,0:T(8,128)(2,1)}) %reduce-scatter.24.cloned.1.call-update) | async-done | bytes 262160 | tf_op jit(solution)/shard_map/reduce_scatter | solution.py:198
  1327.2 77.3 %reduce-scatter.18.cloned.1.call-done = bf16[1,256,2048]{2,1,0:T(8,128)(2,1)} async-done(((bf16[1,1024,2048]{2,1,0:T(8,128)(2,1)}), bf16[1,256,2048]{2,1,0:T(8,128)(2,1)}) %reduce-scatter.18.cloned.1.call-update) | async-done | bytes 1048592 | tf_op jit(solution)/shard_map/reduce_scatter | solution.py:198
  1406.8 24.0 %all-reduce.3 = (f32[2048]{0:T(1024)S(1)}, f32[32]{0:T(128)S(1)}, f32[2048]{0:T(1024)S(1)}) all-reduce(f32[2048]{0:T(1024)S(1)} %get-tuple-element.93, f32[32]{0:T(128)S(1)} %tile.10, f32[2048]{0:T(1024)S(1)} %get-tuple-element.90), channel_id=6, replica_groups=mesh['fsdp'=8,'tp'=4] {'fsdp'}, use_global_device_ids=true, to_apply=%region_9.0.clone | all-reduce | flops 4128 | bytes 33024
  (178 shorter events, 279.5 us)
Async XLA Ops:
  7.2 33.4 %all-gather.16.cloned.1.call-start = ((), (), s32[]{:S(2)}) async-start(), calls=%async_computation.12 | async-start | bytes 2359296 | tf_op jit(solution)/shard_map/all_gather | solution.py:206
  7.9 115.6 %all-gather.14.cloned.1.call-start = ((), (), s32[]{:S(2)}) async-start(), calls=%async_computation.11 | async-start | bytes 5242880 | tf_op jit(solution)/shard_map/all_gather | solution.py:251
  24.2 127.6 %all-gather.18.cloned.1.call-start = ((), (), s32[]{:S(2)}) async-start(), calls=%async_computation.13 | async-start | bytes 2359296 | tf_op jit(solution)/shard_map/all_gather | solution.py:207
  25.0 156.6 %all-gather.20.cloned.1.call-start = ((), (), s32[]{:S(2)}) async-start(), calls=%async_computation.14 | async-start | bytes 2359296 | tf_op jit(solution)/shard_map/all_gather | solution.py:208
  25.5 185.6 %all-gather.22.cloned.1.call-start = ((), (), s32[]{:S(2)}) async-start(), calls=%async_computation.15 | async-start | bytes 2359296 | tf_op jit(solution)/shard_map/all_gather | solution.py:209
  26.1 268.3 %reduce-scatter.12.cloned.1.call-start = ((), (), s32[]{:S(2)}) async-start(), calls=%async_computation.16 | async-start | bytes 5242880 | tf_op jit(solution)/shard_map/reduce_scatter | solution.py:198
  217.5 133.9 %all-gather.28.cloned.1.call-start = ((), (), s32[]{:S(2)}) async-start(), calls=%async_computation.19 | async-start | bytes 9437184 | tf_op jit(solution)/shard_map/all_gather | solution.py:217
  218.3 216.2 %all-gather.24.cloned.1.call-start = ((), (), s32[]{:S(2)}) async-start(), calls=%async_computation.17 | async-start | bytes 5242880 | tf_op jit(solution)/shard_map/all_gather | solution.py:265
  298.7 190.7 %all-gather.26.cloned.1.call-start = ((), (), s32[]{:S(2)}) async-start(), calls=%async_computation.18 | async-start | bytes 9437184 | tf_op jit(solution)/shard_map/all_gather | solution.py:216
  299.5 272.3 %all-gather.32.cloned.1.call-start = ((), (), s32[]{:S(2)}) async-start(), calls=%async_computation.22 | async-start | bytes 5242880 | tf_op jit(solution)/shard_map/all_gather | solution.py:284
  300.0 326.7 %all-gather.30.cloned.1.call-start = ((), (), s32[]{:S(2)}) async-start(), calls=%async_computation.20 | async-start | bytes 9437184 | tf_op jit(solution)/shard_map/all_gather | solution.py:218
  300.8 453.7 %reduce-scatter.16.cloned.1.call-start = ((), (), s32[]{:S(2)}) async-start(), calls=%async_computation.23 | async-start | bytes 5242880 | tf_op jit(solution)/shard_map/reduce_scatter | solution.py:198
  677.5 156.5 %reduce-scatter.14.cloned.1.call-start = ((), (), s32[]{:S(2)}) async-start(), calls=%async_computation.21 | async-start | bytes 5242880 | tf_op jit(solution)/shard_map/reduce_scatter | solution.py:198
  691.6 231.6 %all-gather.34.cloned.1.call-start = ((), (), s32[]{:S(2)}) async-start(), calls=%async_computation.24 | async-start | bytes 5242880 | tf_op jit(solution)/shard_map/all_gather | solution.py:299
  841.7 155.0 %reduce-scatter.28.cloned.1.call-start = ((), (), s32[]{:S(2)}) async-start(), calls=%async_computation.30 | async-start | bytes 9437184 | tf_op jit(solution)/shard_map/reduce_scatter | solution.py:198
  856.1 215.2 %reduce-scatter.30.cloned.1.call-start = ((), (), s32[]{:S(2)}) async-start(), calls=%async_computation.31 | async-start | bytes 9437184 | tf_op jit(solution)/shard_map/reduce_scatter | solution.py:198
  870.2 276.1 %reduce-scatter.32.cloned.1.call-start = ((), (), s32[]{:S(2)}) async-start(), calls=%async_computation.32 | async-start | bytes 9437184 | tf_op jit(solution)/shard_map/reduce_scatter | solution.py:198
  884.8 305.9 %reduce-scatter.26.cloned.1.call-start = ((), (), s32[]{:S(2)}) async-start(), calls=%async_computation.29 | async-start | bytes 2359296 | tf_op jit(solution)/shard_map/reduce_scatter | solution.py:198
  929.1 307.1 %reduce-scatter.20.cloned.1.call-start = ((), (), s32[]{:S(2)}) async-start(), calls=%async_computation.26 | async-start | bytes 2359296 | tf_op jit(solution)/shard_map/reduce_scatter | solution.py:198
  957.5 323.0 %reduce-scatter.22.cloned.1.call-start = ((), (), s32[]{:S(2)}) async-start(), calls=%async_computation.27 | async-start | bytes 2359296 | tf_op jit(solution)/shard_map/reduce_scatter | solution.py:198
  963.5 361.9 %reduce-scatter.24.cloned.1.call-start = ((), (), s32[]{:S(2)}) async-start(), calls=%async_computation.28 | async-start | bytes 2359296 | tf_op jit(solution)/shard_map/reduce_scatter | solution.py:198
  969.5 435.0 %reduce-scatter.18.cloned.1.call-start = ((), (), s32[]{:S(2)}) async-start(), calls=%async_computation.25 | async-start | bytes 5242880 | tf_op jit(solution)/shard_map/reduce_scatter | solution.py:198
  999.5 405.0 %copy-start.23 = (f32[8,1,256]{2,1,0:T(1,128)S(1)}, f32[8,1,256]{2,1,0:T(1,128)}, u32[]{:S(2)}) copy-start(f32[8,1,256]{2,1,0:T(1,128)} %copy-done.22) | copy-start | bytes 24580
  999.5 405.0 %copy-start.25 = (f32[256]{0:T(256)S(1)}, f32[256]{0:T(256)}, u32[]{:S(2)}) copy-start(f32[256]{0:T(256)} %copy-done.24) | copy-start | bytes 3076
  (34 other events, 2002.9 us)
Sparse Core Ops, SparseCore 0:
  9.9 30.5 all-gather.15
  42.7 80.7 all-gather.13
  125.4 26.4 all-gather.17
  153.6 27.8 all-gather.19
  183.3 27.8 all-gather.21
  217.6 76.7 reduce-scatter.11
  296.5 54.9 all-gather.27
  353.7 80.7 all-gather.23
  436.5 52.9 all-gather.25
  491.0 80.7 all-gather.31
  573.8 52.9 all-gather.29
  677.6 76.7 reduce-scatter.15
  756.7 77.2 reduce-scatter.13
  841.8 81.2 all-gather.33
  926.8 69.8 reduce-scatter.27
  1000.0 71.2 reduce-scatter.29
  1075.0 71.2 reduce-scatter.31
  1149.5 41.1 reduce-scatter.25
  1194.9 41.2 reduce-scatter.19
  1239.3 41.1 reduce-scatter.21
  1284.1 41.2 reduce-scatter.23
  1327.7 76.7 reduce-scatter.17

commit v2 on v1

--- a/solution.py
+++ b/solution.py
@@ -7,6 +7,7 @@
 from jax.experimental.pallas import tpu as pltpu
 from jax.sharding import PartitionSpec as P
 
+rms_eps = 1e-06
 NEG = -1e30
 LOG2E = 1.4426950408889634
 
@@ -166,20 +167,444 @@
         name="attend_backward",
     )(bounds, q, k, v, gc, mix, lse, memory, norm.reshape(heads, 1, hd), jnp.broadcast_to(gate[:, None, None], (heads, 1, hd)))
 
+
 norm_eps = 1e-06
-rms_eps = 1e-06
-
-
-def normalize(rows_in):
-    return rows_in * lax.rsqrt(jnp.mean(rows_in * rows_in, axis=-1, keepdims=True) + norm_eps)
-
-
-def norm_gain(rows_in, gain_full):
-    return normalize(rows_in) * gain_full
-
-
-def glu_product(gate_pre, up_pre):
-    return jax.nn.gelu(gate_pre) * up_pre
+MESH = pl.DeviceIdType.MESH
+RIGHT, LEFT = 0, 1
+
+
+class Line:
+    def __init__(self, size, send_sem, recv_sem):
+        self.size, self.send_sem, self.recv_sem = size, send_sem, recv_sem
+        self.here = lax.axis_index("tp")
+
+    def meet(self):
+        barrier = pltpu.get_barrier_semaphore()
+        last = self.size - 1
+
+        @pl.when(self.here > 0)
+        def _():
+            pl.semaphore_signal(barrier, inc=1, device_id={"tp": self.here - 1}, device_id_type=MESH)
+
+        @pl.when(self.here < last)
+        def _():
+            pl.semaphore_signal(barrier, inc=1, device_id={"tp": self.here + 1}, device_id_type=MESH)
+
+        peers = (self.here > 0).astype(jnp.int32) + (self.here < last).astype(jnp.int32)
+        pl.semaphore_wait(barrier, peers)
+
+    def copy(self, phase, way, slot, src, dst):
+        to = self.here + 1 if way == RIGHT else self.here - 1
+        return pltpu.make_async_remote_copy(
+            src_ref=src,
+            dst_ref=dst,
+            send_sem=self.send_sem.at[phase, way, slot],
+            recv_sem=self.recv_sem.at[phase, way, slot],
+            device_id={"tp": to},
+            device_id_type=MESH,
+        )
+
+    def arrived(self, phase, way, slot, dst):
+        self.copy(phase, way, slot, dst, dst).wait_recv()
+
+    def scatter_step(self, phase, k, part, land_right, land_left):
+        n, t = self.size, self.here
+        far, near = n - 1 - k, k
+
+        def pass_on(way, shard, land, first):
+            @pl.when(jnp.logical_not(first))
+            def _():
+                self.arrived(phase, way, k, land)
+                part[shard] = (part[shard].astype(jnp.float32) + land[...].astype(jnp.float32)).astype(part.dtype)
+
+            self.copy(phase, way, k, part.at[shard], land).start()
+
+        @pl.when(t < far)
+        def _():
+            pass_on(RIGHT, far, land_right.at[far - 1], t == 0)
+
+        @pl.when(t > near)
+        def _():
+            pass_on(LEFT, near, land_left.at[near], t == n - 1)
+
+    def scatter_end(self, phase, part, land_right, land_left, total):
+        n, t = self.size, self.here
+        total[...] = part[t].astype(jnp.float32)
+
+        @pl.when(t > 0)
+        def _():
+            self.arrived(phase, RIGHT, n - 1 - t, land_right.at[t - 1])
+            total[...] += land_right[t - 1].astype(jnp.float32)
+
+        @pl.when(t < n - 1)
+        def _():
+            self.arrived(phase, LEFT, t, land_left.at[t])
+            total[...] += land_left[t].astype(jnp.float32)
+
+    def scatter_sent(self, phase, part, land_right, land_left):
+        n, t = self.size, self.here
+        for k in range(n - 1):
+            far, near = n - 1 - k, k
+
+            @pl.when(t < far)
+            def _():
+                self.copy(phase, RIGHT, k, part.at[far], land_right.at[far - 1]).wait_send()
+
+            @pl.when(t > near)
+            def _():
+                self.copy(phase, LEFT, k, part.at[near], land_left.at[near]).wait_send()
+
+    def gather_step(self, phase, k, rows):
+        n, t = self.size, self.here
+
+        @pl.when(t >= k)
+        def _():
+            shard = rows.at[t - k]
+            if k > 0:
+                self.arrived(phase, RIGHT, k - 1, shard)
+            if k < n - 1:
+                @pl.when(t < n - 1)
+                def _():
+                    self.copy(phase, RIGHT, k, shard, shard).start()
+
+        @pl.when(t + k <= n - 1)
+        def _():
+            shard = rows.at[t + k]
+            if k > 0:
+                self.arrived(phase, LEFT, k - 1, shard)
+            if k < n - 1:
+                @pl.when(t > 0)
+                def _():
+                    self.copy(phase, LEFT, k, shard, shard).start()
+
+    def gather_sent(self, phase, rows):
+        n, t = self.size, self.here
+        for k in range(n - 1):
+            @pl.when((t >= k) & (t < n - 1))
+            def _():
+                self.copy(phase, RIGHT, k, rows.at[t - k], rows.at[t - k]).wait_send()
+
+            @pl.when((t + k <= n - 1) & (t > 0))
+            def _():
+                self.copy(phase, LEFT, k, rows.at[t + k], rows.at[t + k]).wait_send()
+
+
+GELU_A, GELU_B = 0.7978845608028654, 0.044715
+
+
+def gelu_pair(v):
+    square = v * v
+    curve = jnp.tanh(v * (GELU_A + GELU_A * GELU_B * square))
+    half = 0.5 + 0.5 * curve
+    slope = half + (0.5 * v) * (1.0 - curve * curve) * (GELU_A + 3.0 * GELU_A * GELU_B * square)
+    return v * half, slope
+
+
+def middle_kernel(
+    blocks, comb_hbm, wout_hbm, stream_hbm, cot_hbm, cot_all_hbm, gain_ref, *rest,
+    chunks, size, masks, halves, tile,
+):
+    weights_in = rest[:blocks]
+    (x_out, hid_out, gl_out, ul_out, mlp_out, mid_out, gmid_out, ggain_ref, stat_ref,
+     w_three, x, cot, hid, gl, ul, part, land_r, land_l, stream, mid, total,
+     load_sem, weight_sem, comb_sem, wout_sem, out_sem, send_sem, recv_sem, live_ref) = rest[blocks:]
+    n, c_rows = size, x.shape[2]
+    t, f = lax.axis_index("tp"), lax.axis_index("fsdp")
+    width = x.shape[3]
+    units = hid.shape[1]
+    line = Line(n, send_sem, recv_sem)
+
+    inner = comb_hbm.shape[-1]
+    loads = [pltpu.make_async_copy(stream_hbm, stream, load_sem.at[2])]
+    for c in range(chunks):
+        for s in range(n):
+            loads.append(
+                pltpu.make_async_copy(
+                    comb_hbm.at[s * chunks + c],
+                    hid.at[s * c_rows : (s + 1) * c_rows, c * inner : (c + 1) * inner],
+                    comb_sem.at[c * n + s],
+                )
+            )
+    for j in range(width // tile):
+        loads.append(
+            pltpu.make_async_copy(
+                wout_hbm.at[j * tile : (j + 1) * tile, :], gl.at[:, j * inner : (j + 1) * inner], wout_sem.at[j]
+            )
+        )
+    for item in loads:
+        item.start()
+    cot_own = stream
+    cot_load = pltpu.make_async_copy(cot_hbm, cot_own, load_sem.at[3])
+    cot_loads = [pltpu.make_async_copy(cot_all_hbm.at[c], cot, load_sem.at[4 + c]) for c in range(chunks)]
+    cot_loads[0].start()
+    weight_loads = []
+    half_rows = width // (len(masks) * halves)
+    for b, block in enumerate(weights_in):
+        mask, half = masks[b // halves], b % halves
+        owner = lax.bitwise_xor(f, mask) if mask else f
+        rows = pl.ds(pl.multiple_of(owner * (half_rows * halves) + half * half_rows, half_rows), half_rows)
+        weight_loads.append(pltpu.make_async_copy(block, w_three.at[:, rows, :], weight_sem.at[b]))
+    for item in weight_loads:
+        item.start()
+    line.meet()
+    for item in loads[1:]:
+        item.wait()
+
+    def project(c):
+        flat = part.at[c].reshape(n * c_rows, width)
+
+        @pl.loop(0, width // tile)
+        def _(j):
+            cols = pl.ds(pl.multiple_of(j * tile, tile), tile)
+            weight = gl[:, pl.ds(pl.multiple_of(j * inner, inner), inner)]
+            flat[:, cols] = dot32(hid[:, c * inner : (c + 1) * inner], weight, NT).astype(jnp.bfloat16)
+
+    def inverse_rms(v):
+        return lax.rsqrt(jnp.mean(v * v, axis=-1, keepdims=True) + norm_eps)
+
+    def norm_two(c):
+        rows = slice(c * c_rows, (c + 1) * c_rows)
+        branch = total[...]
+        live = live_ref[rows, :]
+        stat_ref[...] += jnp.sum(jnp.sum(branch * branch, axis=-1, keepdims=True) * live, axis=0, keepdims=True)
+        m = stream[rows, :].astype(jnp.float32) + branch
+        mid[rows, :] = m
+        x[c, t] = (m * inverse_rms(m) * gain_ref[...]).astype(jnp.bfloat16)
+
+    def first_half(c, service):
+        flat = x.at[c].reshape(n * c_rows, width)
+        @pl.loop(0, units // tile)
+        def _(j):
+            cols = pl.ds(pl.multiple_of(j * tile, tile), tile)
+            gate_pre = dot32(flat[...], w_three[0, :, cols], NN)
+            up_pre = dot32(flat[...], w_three[1, :, cols], NN)
+            grad_hidden = dot32(cot[...], w_three[2, :, cols], NN)
+            value, slope = gelu_pair(gate_pre)
+            hid[:, cols] = (value * up_pre).astype(jnp.bfloat16)
+            ul[:, cols] = (grad_hidden * value).astype(jnp.bfloat16)
+            gl[:, cols] = (grad_hidden * up_pre * slope).astype(jnp.bfloat16)
+            service(j)
+
+    def second_half(c, service):
+        flat = part.at[c].reshape(n * c_rows, width)
+
+        @pl.loop(0, width // tile)
+        def _(j):
+            cols = pl.ds(pl.multiple_of(j * tile, tile), tile)
+            terms = dot32(gl[...], w_three[0, cols, :], NT) + dot32(ul[...], w_three[1, cols, :], NT)
+            flat[:, cols] = terms.astype(jnp.bfloat16)
+            service(j)
+
+    def branch_terms(c):
+        @pl.loop(0, width // tile)
+        def _(j):
+            cols = pl.ds(pl.multiple_of(j * tile, tile), tile)
+            terms = dot32(hid[...], w_three[2, cols, :], NT).astype(jnp.bfloat16)
+            ul[:, cols] = terms
+
+    def norm_back(c):
+        rows = slice(c * c_rows, (c + 1) * c_rows)
+        m = mid[rows, :]
+        inv = inverse_rms(m)
+        u = m * inv
+        gn = total[...]
+        e = gn * gain_ref[...]
+        ggain_ref[...] += jnp.sum(gn * u, axis=0, keepdims=True)
+        total[...] = cot_own[rows, :].astype(jnp.float32) + inv * (e - u * jnp.mean(e * u, axis=-1, keepdims=True))
+
+    RS1, AG2, RS3 = 0, 1, 2
+
+    def ph(kind, c):
+        return kind * chunks + c
+
+    def lands(c):
+        return part.at[c], land_r.at[c], land_l.at[c]
+
+    ggain_ref[...] = jnp.zeros_like(ggain_ref)
+    stat_ref[...] = jnp.zeros_like(stat_ref)
+    for c in range(chunks):
+        project(c)
+        line.scatter_step(ph(RS1, c), 0, *lands(c))
+    loads[0].wait()
+    for k in range(1, n - 1):
+        line.scatter_step(ph(RS1, 0), k, *lands(0))
+    for c in range(chunks):
+        line.scatter_end(ph(RS1, c), *lands(c), total)
+        norm_two(c)
+        line.gather_step(ph(AG2, c), 0, x.at[c])
+        if c + 1 < chunks:
+            for k in range(1, n):
+                if k < n - 1:
+                    line.scatter_step(ph(RS1, c + 1), k, *lands(c + 1))
+                line.gather_step(ph(AG2, c), k, x.at[c])
+    cot_load.start()
+    for item in weight_loads:
+        item.wait()
+    cot_load.wait()
+    outs = {}
+
+    def send_out(name, c, src, dst, sem):
+        outs[name, c] = pltpu.make_async_copy(src, dst.at[c], out_sem.at[sem])
+        outs[name, c].start()
+
+    last = chunks - 1
+    for c in range(chunks):
+        cot_loads[c].wait()
+
+        def during_first(j, c=c):
+            for k in range(1, n):
+                @pl.when(j == k - 1)
+                def _():
+                    if c == last - 1:
+                        line.gather_step(ph(AG2, last), k, x.at[last])
+                    if c > 0 and k < n - 1:
+                        line.scatter_step(ph(RS3, c - 1), k, *lands(c - 1))
+
+        if chunks == 1:
+            for k in range(1, n):
+                line.gather_step(ph(AG2, 0), k, x.at[0])
+        if c > 0:
+            for name in ("hid", "gl", "ul"):
+                outs[name, c - 1].wait()
+        first_half(c, during_first)
+        if c + 1 < chunks:
+            cot_loads[c + 1].start()
+        send_out("x", c, x.at[c], x_out, 0)
+        send_out("hid", c, hid, hid_out, 1)
+        send_out("gl", c, gl, gl_out, 2)
+        send_out("ulk", c, ul, ul_out, 3)
+        line.scatter_sent(ph(RS1, c), *lands(c))
+
+        def finish(c):
+            rows = pl.ds(c * c_rows, c_rows)
+            line.scatter_end(ph(RS3, c), *lands(c), total)
+            norm_back(c)
+            out = pltpu.make_async_copy(total, gmid_out.at[rows, :], out_sem.at[5])
+            out.start()
+            out.wait()
+
+        second_half(c, lambda j: None)
+        line.scatter_step(ph(RS3, c), 0, *lands(c))
+        outs["ulk", c].wait()
+        if c > 0:
+            finish(c - 1)
+        branch_terms(c)
+        send_out("ul", c, ul, mlp_out, 4)
+        outs["x", c].wait()
+    for k in range(1, n - 1):
+        line.scatter_step(ph(RS3, last), k, *lands(last))
+    out = pltpu.make_async_copy(mid, mid_out, out_sem.at[6])
+    out.start()
+    finish(last)
+    out.wait()
+    for name in ("hid", "gl", "ul"):
+        outs[name, last].wait()
+    for c in range(chunks):
+        line.scatter_sent(ph(RS3, c), *lands(c))
+        line.gather_sent(ph(AG2, c), x.at[c])
+
+
+def middle(combined, w_out, stream, cot, cot_all, gain, live, blocks, masks, halves, size, collective_id, chunks=2, tile=512):
+    rows, width = stream.shape
+    units = blocks[0].shape[-1]
+    inner = combined.shape[1]
+    c_rows = rows // chunks
+    bf, f32 = jnp.bfloat16, jnp.float32
+    S = jax.ShapeDtypeStruct
+    any_space = pl.BlockSpec(memory_space=pl.ANY)
+    vmem = pl.BlockSpec(memory_space=pltpu.VMEM)
+    all_rows = (chunks, size * c_rows)
+    phases = 3 * chunks
+    V = pltpu.VMEM
+
+    def body(comb, wout, st, ct, ct_all, gain_ref, live_ref, *rest):
+        middle_kernel(
+            len(blocks), comb, wout, st, ct, ct_all, gain_ref, *rest, live_ref,
+            chunks=chunks, size=size, masks=masks, halves=halves, tile=tile,
+        )
+
+    return pl.pallas_call(
+        body,
+        in_specs=[any_space] * 5 + [vmem, vmem] + [any_space] * len(blocks),
+        out_specs=[any_space] * 7 + [vmem, vmem],
+        out_shape=[
+            S((chunks, size, c_rows, width), bf),
+            S(all_rows + (units,), bf), S(all_rows + (units,), bf), S(all_rows + (units,), bf),
+            S(all_rows + (width,), bf),
+            S((rows, width), f32), S((rows, width), f32),
+            S((1, width), f32), S((1, 1), f32),
+        ],
+        scratch_shapes=[
+            V((3, width, units), bf),
+            V((chunks, size, c_rows, width), bf),
+            V((size * c_rows, width), bf),
+            V((size * c_rows, units), bf), V((size * c_rows, units), bf), V((size * c_rows, units), bf),
+            V((chunks, size, c_rows, width), bf),
+            V((chunks, size - 1, c_rows, width), bf), V((chunks, size - 1, c_rows, width), bf),
+            V((rows, width), bf),
+            V((rows, width), f32), V((c_rows, width), f32),
+            pltpu.SemaphoreType.DMA((4 + chunks,)),
+            pltpu.SemaphoreType.DMA((len(blocks),)),
+            pltpu.SemaphoreType.DMA((chunks * size,)),
+            pltpu.SemaphoreType.DMA((width // tile,)),
+            pltpu.SemaphoreType.DMA((7,)),
+            pltpu.SemaphoreType.DMA((phases, 2, size - 1)),
+            pltpu.SemaphoreType.DMA((phases, 2, size - 1)),
+        ],
+        compiler_params=pltpu.CompilerParams(
+            collective_id=collective_id, has_side_effects=True, vmem_limit_bytes=60 * 2**20
+        ),
+        name="middle_layer",
+    )(combined.reshape(size * chunks, c_rows, inner), w_out, stream, cot, cot_all, gain, live, *blocks)
+
+
+def project_kernel(stream_ref, gain_ref, *rest, masks, halves, parts, tile):
+    blocks = rest[: len(masks) * halves]
+    weights_out, x_ref, *outs, weights, weight_sem, out_sem = rest[len(masks) * halves :]
+    f = lax.axis_index("fsdp")
+    width = stream_ref.shape[1]
+    half_rows = width // (len(masks) * halves)
+    loads = []
+    for b, block in enumerate(blocks):
+        mask, half = masks[b // halves], b % halves
+        owner = lax.bitwise_xor(f, mask) if mask else f
+        rows = pl.ds(pl.multiple_of(owner * (half_rows * halves) + half * half_rows, half_rows), half_rows)
+        loads.append(pltpu.make_async_copy(block, weights.at[:, rows, :], weight_sem.at[b]))
+    for item in loads:
+        item.start()
+    for first in range(0, stream_ref.shape[0], tile):
+        v = stream_ref[first : first + tile, :].astype(jnp.float32)
+        inv = lax.rsqrt(jnp.mean(v * v, axis=-1, keepdims=True) + norm_eps)
+        x_ref[first : first + tile, :] = (v * inv * gain_ref[...]).astype(jnp.bfloat16)
+    for item in loads:
+        item.wait()
+    out = pltpu.make_async_copy(weights, weights_out, out_sem)
+    out.start()
+    for p in range(parts):
+        outs[p][...] = dot32(x_ref[...], weights[p], NN).astype(jnp.bfloat16)
+    out.wait()
+
+
+def project_rows(stream_all, gain, blocks, masks, halves, parts=3, tile=256):
+    length, width = stream_all.shape
+    inner = blocks[0].shape[-1]
+    kinds = blocks[0].shape[0]
+    S = jax.ShapeDtypeStruct
+    bf = jnp.bfloat16
+    any_space, vmem = pl.BlockSpec(memory_space=pl.ANY), pl.BlockSpec(memory_space=pltpu.VMEM)
+    return pl.pallas_call(
+        functools.partial(project_kernel, masks=masks, halves=halves, parts=parts, tile=tile),
+        in_specs=[vmem, vmem] + [any_space] * len(blocks),
+        out_specs=[any_space] + [vmem] * (1 + parts),
+        out_shape=[S((kinds, width, inner), bf), S((length, width), bf)] + [S((length, inner), bf)] * parts,
+        scratch_shapes=[
+            pltpu.VMEM((kinds, width, inner), bf),
+            pltpu.SemaphoreType.DMA((len(blocks),)),
+            pltpu.SemaphoreType.DMA,
+        ],
+        compiler_params=pltpu.CompilerParams(vmem_limit_bytes=48 * 2**20),
+        name="project_rows",
+    )(stream_all, gain, *blocks)
 
 
 def contract_rows(first_mat, second_mat):
@@ -194,29 +619,62 @@
     )
 
 
-def scatter_low(terms, axis, dim):
-    return lax.psum_scatter(
-        terms.astype(jnp.bfloat16), axis, scatter_dimension=dim, tiled=True
-    ).astype(jnp.float32)
-
-
-def fetch_attention(attn_gain, w_query, w_key, w_value, w_out):
-    return (
-        lax.all_gather(attn_gain, "fsdp", axis=0, tiled=True),
-        lax.all_gather(w_query, "fsdp", axis=0, tiled=True),
-        lax.all_gather(w_key, "fsdp", axis=0, tiled=True),
-        lax.all_gather(w_value, "fsdp", axis=0, tiled=True),
-        lax.all_gather(w_out, "fsdp", axis=0, tiled=True),
-    )
-
-
-def fetch_mlp(mlp_gain, w_gate, w_up, w_down):
-    return (
-        lax.all_gather(mlp_gain, "fsdp", axis=0, tiled=True),
-        lax.all_gather(w_gate, "fsdp", axis=0, tiled=True),
-        lax.all_gather(w_up, "fsdp", axis=0, tiled=True),
-        lax.all_gather(w_down, "fsdp", axis=0, tiled=True),
-    )
+def exchange(own, axis, bits):
+    size = lax.axis_size(axis)
+    got = {0: own}
+    for bit in bits:
+        for mask in list(got):
+            got[mask ^ bit] = lax.ppermute(got[mask], axis, [(i, i ^ bit) for i in range(size)])
+    return got
+
+
+def gather_blocks(stacked, axis):
+    size = lax.axis_size(axis)
+    ups = [1 << b for b in range(1, size.bit_length() - 1)]
+    rows = stacked.shape[1] // 2
+    first = exchange(stacked[:, :rows], axis, ups[::-1] + [1])
+    second = exchange(stacked[:, rows:], axis, ups + [1])
+    masks = sorted(first)
+    return masks, [half[mask] for mask in masks for half in (first, second)]
+
+
+def ring_gather(own, axis):
+    size = lax.axis_size(axis)
+    here = lax.axis_index(axis)
+    whole = jnp.zeros((size,) + own.shape, own.dtype)
+    moving = own
+    for k in range(size):
+        if k:
+            moving = lax.ppermute(moving, axis, [(i, (i + 1) % size) for i in range(size)])
+        whole = lax.dynamic_update_index_in_dim(whole, moving, lax.rem(here - k + size, size), 0)
+    return whole
+
+
+def halve(terms, axis, bits):
+    size = lax.axis_size(axis)
+    here = lax.axis_index(axis)
+    left = [1 << b for b in range(size.bit_length() - 2, -1, -1)]
+    for bit in bits:
+        at = left.index(bit)
+        mine = lax.rem(here // bit, 2)
+        kept = lax.dynamic_index_in_dim(terms, mine, at, keepdims=False)
+        sent = lax.dynamic_index_in_dim(terms, 1 - mine, at, keepdims=False)
+        came = lax.ppermute(sent, axis, [(i, i ^ bit) for i in range(size)])
+        total = kept.astype(jnp.float32) + came.astype(jnp.float32)
+        left.pop(at)
+        terms = total if not left else total.astype(jnp.bfloat16)
+    return terms
+
+
+def scatter_blocks(grad, axis):
+    size = lax.axis_size(axis)
+    levels = size.bit_length() - 1
+    ups = [1 << b for b in range(1, levels)]
+    rows = grad.shape[0] // size
+    split = grad.reshape((2,) * levels + (2, rows // 2, grad.shape[1]))
+    first = halve(lax.index_in_dim(split, 0, levels, keepdims=False), axis, [1] + ups)
+    second = halve(lax.index_in_dim(split, 1, levels, keepdims=False), axis, [1] + ups[::-1])
+    return jnp.concatenate([first, second], axis=0)
 
 
 def on_device(
@@ -237,115 +695,106 @@
     valid,
     cotangent,
 ):
+    f32, bf16 = jnp.float32, jnp.bfloat16
     len_dev, width = (stream.shape[1], stream.shape[2])
-    seq_len = len_dev * lax.axis_size("tp")
-    seq_here = lax.axis_index("fsdp")
+    tp_size, fsdp_size = lax.axis_size("tp"), lax.axis_size("fsdp")
+    tp_here, seq_here = lax.axis_index("tp"), lax.axis_index("fsdp")
+    seq_len = len_dev * tp_size
+    heads_here = mem_gate.shape[0]
     prefix_len = prefix[seq_here]
     valid_len = valid[seq_here]
-    full_shape = (1, seq_len, width)
-    gain_one, query_full, key_full, value_full, out_full = fetch_attention(
-        attn_gain, w_query, w_key, w_value, w_out
-    )
-    stream_f = stream.astype(jnp.float32)
-    normed_local, norm_one_back = jax.vjp(norm_gain, stream_f, gain_one.astype(jnp.float32))
-    normed_one = lax.all_gather(normed_local.astype(jnp.bfloat16), "tp", axis=1, tiled=True)
-    flat_one = normed_one.reshape(seq_len, width)
-    def project(weight):
-        return jnp.dot(flat_one, weight, preferred_element_type=jnp.float32).astype(jnp.bfloat16)
-
-    query_rows, key_rows, value_rows = project(query_full), project(key_full), project(value_full)
+    chunks = 2
+    stream, cotangent = stream[0], cotangent[0]
+
+    gains = lax.all_gather(jnp.stack([attn_gain, mlp_gain]), "fsdp", axis=1, tiled=True).astype(f32)
+    masks, attn_blocks = gather_blocks(jnp.stack([w_query, w_key, w_value, w_out]), "fsdp")
+    stream_all = ring_gather(stream, "tp").reshape(seq_len, width)
+    masks, mlp_blocks = gather_blocks(jnp.stack([w_gate, w_up, w_down]), "fsdp")
+    cot_all = ring_gather(cotangent, "tp")
+    cot_all = (
+        cot_all.reshape(tp_size, chunks, len_dev // chunks, width).swapaxes(0, 1).reshape(chunks, seq_len // chunks, width)
+    )
+    weights, flat_one, query_rows, key_rows, value_rows = project_rows(
+        stream_all, gains[:1], attn_blocks, masks, 2
+    )
+    query_full, key_full, value_full, out_full = weights[0], weights[1], weights[2], weights[3]
     bounds = jnp.stack([prefix_len, valid_len])
     combined, local_mix, log_total, memory_next, normalizer_next = attend(
         bounds, query_rows, key_rows, value_rows, memory[0], normalizer[0], mem_gate
     )
-    attn_branch = scatter_low(times_transpose(combined, out_full).reshape(full_shape), "tp", 1)
-    middle = stream_f + attn_branch
-    gain_two, gate_full, up_full, down_full = fetch_mlp(mlp_gain, w_gate, w_up, w_down)
-    normed_mid, norm_two_back = jax.vjp(norm_gain, middle, gain_two.astype(jnp.float32))
-    normed_two = lax.all_gather(normed_mid.astype(jnp.bfloat16), "tp", axis=1, tiled=True)
-    flat_two = normed_two.reshape(seq_len, width)
-    gate_pre = jnp.dot(flat_two, gate_full, preferred_element_type=jnp.float32)
-    up_pre = jnp.dot(flat_two, up_full, preferred_element_type=jnp.float32)
-    hidden_f, glu_back = jax.vjp(glu_product, gate_pre, up_pre)
-    hidden = hidden_f.astype(jnp.bfloat16)
-    mlp_branch = scatter_low(times_transpose(hidden, down_full).reshape(full_shape), "tp", 1)
-    result = middle + mlp_branch
-    stream_out = result.astype(jnp.bfloat16)
-    local_position = lax.axis_index("tp") * len_dev + jnp.arange(len_dev, dtype=jnp.int32)
-    live_here = (local_position < valid_len).astype(jnp.float32)[None, :, None]
-
-    def square_sum(values_in):
-        return jnp.sum(values_in * values_in * live_here, axis=(1, 2))
-
-    stat_terms = jnp.stack(
-        [square_sum(result), square_sum(attn_branch), square_sum(mlp_branch)], axis=1
-    )
-    gain_two, gate_full, up_full, down_full = fetch_mlp(mlp_gain, w_gate, w_up, w_down)
-    cot_all = lax.all_gather(cotangent, "tp", axis=1, tiled=True).reshape(seq_len, width)
-    grad_hidden = jnp.dot(cot_all, down_full, preferred_element_type=jnp.float32)
-    grad_down = contract_rows(cot_all, hidden)
-    grad_gate_pre, grad_up_pre = glu_back(grad_hidden)
-    gate_low = grad_gate_pre.astype(jnp.bfloat16)
-    up_low = grad_up_pre.astype(jnp.bfloat16)
-    two_terms = times_transpose(gate_low, gate_full) + times_transpose(up_low, up_full)
-    grad_normed_two = scatter_low(two_terms.reshape(full_shape), "tp", 1)
-    grad_gate = contract_rows(flat_two, gate_low)
-    grad_up = contract_rows(flat_two, up_low)
-    grad_middle_in, grad_gain_two = norm_two_back(grad_normed_two)
-    grad_middle = cotangent.astype(jnp.float32) + grad_middle_in
-    gain_one, query_full, key_full, value_full, out_full = fetch_attention(
-        attn_gain, w_query, w_key, w_value, w_out
-    )
-    branch_low = lax.all_gather(grad_middle.astype(jnp.bfloat16), "tp", axis=1, tiled=True).reshape(
-        seq_len, width
-    )
-    grad_out = contract_rows(branch_low, combined)
-    grad_combined = jnp.dot(branch_low, out_full, preferred_element_type=jnp.float32)
+    local_position = tp_here * len_dev + jnp.arange(len_dev, dtype=jnp.int32)
+    live_here = (local_position < valid_len).astype(f32)[:, None]
+    flat_two, hidden, gate_low, up_low, mlp_terms, middle_rows, grad_middle, gain_two_terms, branch_squares = middle(
+        combined, out_full, stream, cotangent, cot_all, gains[1:], live_here, mlp_blocks, masks, 2, tp_size, 1
+    )
+    branch_low = ring_gather(grad_middle.astype(bf16), "tp").reshape(seq_len, width)
+    mlp_branch = lax.psum_scatter(
+        mlp_terms.reshape(chunks, tp_size, len_dev // chunks, width), "tp", scatter_dimension=1, tiled=True
+    ).reshape(len_dev, width).astype(f32)
+    result = middle_rows + mlp_branch
+    stream_out = result.astype(bf16)
+
+    def rows_of(chunked):
+        return chunked.reshape(seq_len, chunked.shape[-1])
+
+    down_grad = scatter_blocks(contract_rows(rows_of(cot_all), rows_of(hidden)).astype(bf16), "fsdp")
+    gate_grad = scatter_blocks(contract_rows(rows_of(flat_two), rows_of(gate_low)).astype(bf16), "fsdp")
+    up_grad = scatter_blocks(contract_rows(rows_of(flat_two), rows_of(up_low)).astype(bf16), "fsdp")
+
+    out_grad = scatter_blocks(contract_rows(branch_low, combined).astype(bf16), "fsdp")
+    grad_combined = jnp.dot(branch_low, out_full, preferred_element_type=f32)
     query_low, key_low, value_low, grad_memory, grad_normalizer, gate_parts = attend_back(
         bounds, query_rows, key_rows, value_rows, grad_combined, local_mix, log_total,
         memory[0], normalizer[0], mem_gate,
     )
-    grad_gate_logit = jnp.sum(gate_parts, axis=(1, 2))
     one_terms = (
         times_transpose(query_low, query_full)
         + times_transpose(key_low, key_full)
         + times_transpose(value_low, value_full)
     )
-    grad_normed_one = scatter_low(one_terms.reshape(full_shape), "tp", 1)
-    grad_query = contract_rows(flat_one, query_low)
-    grad_key = contract_rows(flat_one, key_low)
-    grad_value = contract_rows(flat_one, value_low)
-    grad_stream_in, grad_gain_one = norm_one_back(grad_normed_one)
-    stream_grad = grad_middle + grad_stream_in
-    gate_tiled = jnp.tile(grad_gate_logit, lax.axis_size("fsdp"))
-    joined = (
-        lax.psum_scatter(grad_gain_one, "fsdp", scatter_dimension=0, tiled=True),
-        scatter_low(grad_query, "fsdp", 0),
-        scatter_low(grad_key, "fsdp", 0),
-        scatter_low(grad_value, "fsdp", 0),
-        scatter_low(grad_out, "fsdp", 0),
-        lax.psum_scatter(gate_tiled, "fsdp", scatter_dimension=0, tiled=True),
-        lax.psum_scatter(grad_gain_two, "fsdp", scatter_dimension=0, tiled=True),
-        scatter_low(grad_gate, "fsdp", 0),
-        scatter_low(grad_up, "fsdp", 0),
-        scatter_low(grad_down, "fsdp", 0),
-    )
-    stat_sums, gain_one_grad, gain_two_grad = lax.psum((stat_terms, joined[0], joined[6]), "tp")
-    token_count = valid_len.astype(jnp.float32) * width
+    grad_normed_one = lax.psum_scatter(one_terms.astype(bf16), "tp", scatter_dimension=0, tiled=True).astype(f32)
+    query_grad = scatter_blocks(contract_rows(flat_one, query_low).astype(bf16), "fsdp")
+    key_grad = scatter_blocks(contract_rows(flat_one, key_low).astype(bf16), "fsdp")
+    value_grad = scatter_blocks(contract_rows(flat_one, value_low).astype(bf16), "fsdp")
+
+    stream_f = stream.astype(f32)
+    inverse = lax.rsqrt(jnp.mean(stream_f * stream_f, axis=-1, keepdims=True) + norm_eps)
+    unit = stream_f * inverse
+    gain_one_terms = jnp.sum(grad_normed_one * unit, axis=0)
+    scaled = grad_normed_one * gains[0]
+    stream_grad = grad_middle + inverse * (scaled - unit * jnp.mean(scaled * unit, axis=-1, keepdims=True))
+
+    stats = jnp.stack(
+        [jnp.sum(result * result * live_here), branch_squares[0, 0], jnp.sum(mlp_branch * mlp_branch * live_here)]
+    )
+    gate_terms = jnp.zeros((tp_size, heads_here), f32).at[tp_here].set(jnp.sum(gate_parts, axis=(1, 2)))
+    stat_terms = jnp.zeros((fsdp_size, 3), f32).at[seq_here].set(stats)
+    joined = lax.psum(
+        jnp.concatenate([gain_one_terms, gain_two_terms[0], gate_terms.reshape(-1), stat_terms.reshape(-1)]),
+        ("fsdp", "tp"),
+    )
+    shard = width // fsdp_size
+    gain_one_grad = lax.dynamic_slice_in_dim(joined[:width], seq_here * shard, shard)
+    gain_two_grad = lax.dynamic_slice_in_dim(joined[width : 2 * width], seq_here * shard, shard)
+    gates = joined[2 * width : 2 * width + tp_size * heads_here].reshape(tp_size, heads_here)
+    sums = joined[2 * width + tp_size * heads_here :].reshape(fsdp_size, 3)
+    gate_grad_logit = lax.dynamic_index_in_dim(gates, tp_here, 0, keepdims=False)
+    stat_sums = lax.dynamic_index_in_dim(sums, seq_here, 0)
+    token_count = valid_len.astype(f32) * width
     rms_stats = jnp.sqrt(stat_sums / token_count + rms_eps)
     return (
-        stream_out,
-        stream_grad,
+        stream_out[None],
+        stream_grad[None],
         gain_one_grad,
-        joined[1],
-        joined[2],
-        joined[3],
-        joined[4],
-        joined[5],
+        query_grad,
+        key_grad,
+        value_grad,
+        out_grad,
+        gate_grad_logit,
         gain_two_grad,
-        joined[7],
-        joined[8],
-        joined[9],
+        gate_grad,
+        up_grad,
+        down_grad,
         memory_next[None],
         normalizer_next[:, 0][None],
         grad_memory[None],

time: 1460 us -> 932 us (0.64)
  waiting for transfers between devices: 1100 us -> 220 us
  Pallas kernels: 25.7 us -> 303 us
  matrix products: 200 us -> 65.5 us
  starting transfers between devices: 1.44 us -> 102 us
  local copies, waits for them, and re-layouts: 11.6 us -> 105 us
  other arithmetic: 40 us -> 64 us
    reduce_scatter x11 -> x2, waiting for transfers between devices: 611 us -> 14.1 us  [the longest x1 14.1 us: on_device(): lax.psum_scatter(one_terms.astype(bf16), 'tp', scatter_dimension=0, tiled...]
    all_gather x11 -> x0, waiting for transfers between devices: 489 us -> none  [the longest x1 83 us: on_device(): lax.all_gather(normed_mid.astype(jnp.bfloat16), 'tp', axis=1, tiled=True)]
    pallas_call x0 -> x2, Pallas kernels: none -> 278 us  [the longest x1 264 us: middle(): pl.pallas_call(body, in_specs=[any_space] * 5 + [vmem, vmem] + [any_space...]
    ppermute x0 -> x79, waiting for transfers between devices: none -> 206 us  [the longest x9 125 us: ring_gather(): lax.ppermute(moving, axis, [(i, (i + 1) % size) for i in range(size)])]
    ppermute x0 -> x79, starting transfers between devices: none -> 102 us  [the longest x9 52 us: ring_gather(): lax.ppermute(moving, axis, [(i, (i + 1) % size) for i in range(size)])]
    dot_general x7 -> x1, matrix products: 75.6 us -> 5.24 us  [on_device(): grad_combined = jnp.dot(branch_low, out_full, preferred_element_type=f32)]
    dot_general x7 -> x3, matrix products: 60.1 us -> 17.5 us  [times_transpose(): lax.dot_general(first_mat, second_mat, (((1,), (1,)), ((), ())), preferre...]
    psum x1, blocking collectives: 11.8 us -> 40.9 us  [on_device(): lax.psum(jnp.concatenate([gain_one_terms, gain_two_terms[0], gate_terms.r...]
  transfers between devices with their start and end apart: 22 -> 81, of which waited for: 22 -> 23; matrix products, arithmetic and copies ran while one was open for 12% -> 18% of each run, Pallas kernels for 2% -> 4%
where the time goes in v2:
time: 932 us; the launch traced here: 926 us
  Pallas kernels  303 us (33%)
  waiting for transfers between devices  220 us (24%)
  local copies, waits for them, and re-layouts  105 us (11%)
  starting transfers between devices  102 us (11%)
  matrix products  65.5 us (7%)
  other arithmetic  64 us (7%)
  blocking collectives  49.8 us (5%)
  between operations  16.7 us (2%)
    pallas_call x1, Pallas kernels, middle(): pl.pallas_call(body, in_specs=[any_space] * 5 + [vmem, vmem] + [any_space...  264 us
    ppermute x9, waiting for transfers between devices, ring_gather(): lax.ppermute(moving, axis, [(i, (i + 1) % size) for i in range(size)])  125 us
    ppermute x28, waiting for transfers between devices, exchange(): lax.ppermute(got[mask], axis, [(i, i ^ bit) for i in range(size)])  67.9 us
    ppermute x9, starting transfers between devices, ring_gather(): lax.ppermute(moving, axis, [(i, (i + 1) % size) for i in range(size)])  52 us
    dot_general x7, matrix products, contract_rows(): lax.dot_general(first_mat, second_mat, (((0,), (0,)), ((), ())), preferre...  42.8 us
    psum x1, blocking collectives, on_device(): lax.psum(jnp.concatenate([gain_one_terms, gain_two_terms[0], gate_terms.r...  40.9 us
    ppermute x42, starting transfers between devices, halve(): came = lax.ppermute(sent, axis, [(i, i ^ bit) for i in range(size)])  34.9 us
    unnamed x231, local copies, waits for them, and re-layouts  32.5 us
  transfers between devices with their start and end apart: 81, of which 23 were waited for; matrix products, arithmetic and copies ran while one was open for 18% of the time, Pallas kernels for 4%

profile of v2, /device:TPU:0, one launch (start us, length us, event | category | flops | bytes accessed | tf_op | source)
XLA Modules:
  0.0 925.9 jit_solution(6102261544447739686)
XLA Ops:
  16.4 8.2 collective-permute-done.9.rest_8_
  26.7 8.3 collective-permute-done.10.rest_9_
  56.6 12.8 %collective-permute-done.17 = bf16[256,2048]{1,0:T(8,128)(2,1)} collective-permute-done((bf16[256,2048]{1,0:T(8,128)(2,1)S(1)}, bf16[256,2048]{1,0:T(8,128)(2,1)}, u32[]{:S(2)}, u32[]{:S(2)}) %collective-permute-start.17) | collective-permute-done | bytes 1048608 | tf_op jit(solution)/shard_map/ppermute | solution.py:648
  74.9 10.5 %collective-permute-done.26.rest_8_ = bf16[3,128,2048]{2,1,0:T(8,128)(2,1)} collective-permute-done((bf16[3,128,2048]{2,1,0:T(8,128)(2,1)}, bf16[3,128,2048]{2,1,0:T(8,128)(2,1)}, u32[]{:S(2)}, u32[]{:S(2)}) %collective-permute-start.26) | collective-permute-done | bytes 1572896 | tf_op jit(solution)/shard_map/ppermute | solution.py:627
  93.2 31.0 %collective-permute-done.22.rest_4_ = bf16[3,128,2048]{2,1,0:T(8,128)(2,1)} collective-permute-done((bf16[3,128,2048]{2,1,0:T(8,128)(2,1)}, bf16[3,128,2048]{2,1,0:T(8,128)(2,1)}, u32[]{:S(2)}, u32[]{:S(2)}) %collective-permute-start.22) | collective-permute-done | bytes 1572896 | tf_op jit(solution)/shard_map/ppermute | solution.py:627
  127.0 8.9 all_gather.3
  144.2 8.2 collective-permute-done.18
  156.6 18.2 %collective-permute-done.2 = bf16[256,2048]{1,0:T(8,128)(2,1)S(1)} collective-permute-done((bf16[256,2048]{1,0:T(8,128)(2,1)}, bf16[256,2048]{1,0:T(8,128)(2,1)S(1)}, u32[]{:S(2)}, u32[]{:S(2)}) %collective-permute-start.2) | collective-permute-done | bytes 1048608 | tf_op jit(solution)/shard_map/ppermute | solution.py:648
  174.7 20.6 %collective-permute-done.19 = bf16[256,2048]{1,0:T(8,128)(2,1)S(1)} collective-permute-done((bf16[256,2048]{1,0:T(8,128)(2,1)}, bf16[256,2048]{1,0:T(8,128)(2,1)S(1)}, u32[]{:S(2)}, u32[]{:S(2)}) %collective-permute-start.19) | collective-permute-done | bytes 1048608 | tf_op jit(solution)/shard_map/ppermute | solution.py:648
  203.6 14.2 %project_rows.1 = (bf16[4,2048,512]{2,1,0:T(8,128)(2,1)}, bf16[1024,2048]{1,0:T(8,128)(2,1)}, bf16[1024,512]{1,0:T(8,128)(2,1)}, bf16[1024,512]{1,0:T(8,128)(2,1)}, bf16[1024,512]{1,0:T(8,128)(2,1)}) custom-call(bf16[1024,2048]{1,0:T(8,128)(2,1)} %bitcast.381, f32[1,2048]{1,0:T(1,128)S(1)} %get-tuple-element.132.gain_ref, ...), custom_call_target="tpu_custom_call" | custom-call | tf_op jit(solution)/shard_map/project_rows/pallas_call | solution.py:595
  221.5 10.2 %attend_forward.1 = (bf16[1024,512]{1,0:T(8,128)(2,1)S(1)}, f32[1024,512]{1,0:T(8,128)}, f32[4,1,1024]{2,1,0:T(1,128)S(1)}, f32[4,128,128]{2,1,0:T(8,128)}, f32[4,1,128]{2,1,0:T(1,128)}) custom-call(s32[2]{0:T(128)S(1)} %pad_add_fusion.2.bounds, bf16[1024,512]{1,0:T(8,128)(2,1)S(1)} %copy-done, bf16[1024,512]{1,0:T(8,128)(2,1)S(1)} %copy-done.2, ...), custom_call_target="tpu_custom_call" | custom-call | tf_op jit(solution)/shard_map/attend_forward/pallas_call | solution.py:141
  235.2 263.8 %middle_layer.1 = (bf16[2,4,128,2048]{3,2,1,0:T(8,128)(2,1)}, bf16[2,512,2048]{2,1,0:T(8,128)(2,1)}, bf16[2,512,2048]{2,1,0:T(8,128)(2,1)}, bf16[2,512,2048]{2,1...) custom-call(bf16[8,128,512]{2,1,0:T(8,128)(2,1)} %bitcast.369, ...), custom_call_target="tpu_custom_call" | custom-call | tf_op jit(solution)/shard_map/middle_layer/pallas_call | solution.py:526
  499.1 12.0 %convolution_convert_fusion.1 = bf16[2048,2048]{1,0:T(8,128)(2,1)S(1)} fusion(bf16[1024,2048]{1,0:T(8,128)(2,1)} %bitcast.409, bf16[1024,2048]{1,0:T(8,128)(2,1)} %bitcast.413), kind=kOutput, calls=%fused_computation.2 | convolution fusion | flops 8594128896 | bytes 16777216 | tf_op jit(solution)/shard_map/dot_general | solution.py:611
  513.6 11.1 %convolution_convert_fusion = bf16[2048,2048]{1,0:T(8,128)(2,1)S(1)} fusion(bf16[1024,2048]{1,0:T(8,128)(2,1)S(1)} %bitcast.379, bf16[1024,2048]{1,0:T(8,128)(2,1)} %bitcast.412), kind=kOutput, calls=%fused_computation.1 | convolution fusion | flops 8594128896 | bytes 16777216 | tf_op jit(solution)/shard_map/dot_general | solution.py:611
  544.2 10.0 %convolution_convert_fusion.2 = bf16[2048,2048]{1,0:T(8,128)(2,1)S(1)} fusion(bf16[1024,2048]{1,0:T(8,128)(2,1)S(1)} %bitcast.410, bf16[1024,2048]{1,0:T(8,128)(2,1)S(1)} %bitcast.411), kind=kOutput, calls=%fused_computation.3 | convolution fusion | flops 8594128896 | bytes 16777216 | tf_op jit(solution)/shard_map/dot_general | solution.py:611
  574.0 16.0 %collective-permute-done.34 = bf16[256,2048]{1,0:T(8,128)(2,1)} collective-permute-done((bf16[256,2048]{1,0:T(8,128)(2,1)}, bf16[256,2048]{1,0:T(8,128)(2,1)}, u32[]{:S(2)}, u32[]{:S(2)}) %collective-permute-start.34) | collective-permute-done | bytes 1048608 | tf_op jit(solution)/shard_map/ppermute | solution.py:648
  595.3 15.6 %collective-permute-start.35 = (bf16[256,2048]{1,0:T(8,128)(2,1)}, bf16[256,2048]{1,0:T(8,128)(2,1)S(1)}, u32[]{:S(2)}, u32[]{:S(2)}) collective-permute-start(bf16[256,2048]{1,0:T(8,128)(2,1)} %collective-permute-done.34), channel_id=1, source_target_pairs={{0,1},{1,2},{2,3},{3,0},{4,5},{5,6},{6,7},{7,4},{8,9},{9,10},{10,1... | collective-permute-start | bytes 3145736 | tf_op jit(solution)/shard_map/ppermute | solution.py:648
  627.8 29.2 %collective-permute-done.35 = bf16[256,2048]{1,0:T(8,128)(2,1)S(1)} collective-permute-done((bf16[256,2048]{1,0:T(8,128)(2,1)}, bf16[256,2048]{1,0:T(8,128)(2,1)S(1)}, u32[]{:S(2)}, u32[]{:S(2)}) %collective-permute-start.35) | collective-permute-done | bytes 1048608 | tf_op jit(solution)/shard_map/ppermute | solution.py:648
  657.0 22.8 %collective-permute-start.36 = (bf16[256,2048]{1,0:T(8,128)(2,1)S(1)}, bf16[256,2048]{1,0:T(8,128)(2,1)S(1)}, u32[]{:S(2)}, u32[]{:S(2)}) collective-permute-start(bf16[256,2048]{1,0:T(8,128)(2,1)S(1)} %collective-permute-done.35), channel_id=1, source_target_pairs={{0,1},{1,2},{2,3},{3,0},{4,5},{5,6},{6,7},{7,4},{8,9},{9,10},{10,1... | collective-permute-start | bytes 3145736 | tf_op jit(solution)/shard_map/ppermute | solution.py:648
  684.5 20.3 %collective-permute-done.36 = bf16[256,2048]{1,0:T(8,128)(2,1)S(1)} collective-permute-done((bf16[256,2048]{1,0:T(8,128)(2,1)S(1)}, bf16[256,2048]{1,0:T(8,128)(2,1)S(1)}, u32[]{:S(2)}, u32[]{:S(2)}) %collective-permute-start.36) | collective-permute-done | bytes 1048608 | tf_op jit(solution)/shard_map/ppermute | solution.py:648
  715.8 14.8 %attend_backward.1 = (bf16[1024,512]{1,0:T(8,128)(2,1)S(1)}, bf16[1024,512]{1,0:T(8,128)(2,1)S(1)}, bf16[1024,512]{1,0:T(8,128)(2,1)S(1)}, f32[4,128,128]{2,1,0:...) custom-call(s32[2]{0:T(128)S(1)} %pad_add_fusion.2.bounds, bf16[1024,512]{1,0:T(8,128)(2,1)S(1)} %copy-done.1, ...), custom_call_target="tpu_custom_call" | custom-call | tf_op jit(solution)/shard_map/attend_backward/pallas_call | solution.py:159
  777.3 9.2 add_convert_fusion
  855.9 14.1 %reduce-scatter.5.cloned.1.call-done = bf16[256,2048]{1,0:T(8,128)(2,1)} async-done(((bf16[1024,2048]{1,0:T(8,128)(2,1)}), bf16[256,2048]{1,0:T(8,128)(2,1)}) %reduce-scatter.5.cloned.1.call-update) | async-done | bytes 1048592 | tf_op jit(solution)/shard_map/reduce_scatter | solution.py:755
  872.2 40.9 %psum.7 = f32[4136]{0:T(1024)S(1)} all-reduce(f32[4136]{0:T(1024)S(1)} %concatenate.39), channel_id=1, replica_groups=mesh['fsdp'=8,'tp'=4] {'fsdp','tp'}, use_global_device_ids=true, to_apply=%region_10.11 | all-reduce | flops 4136 | bytes 33088 | tf_op jit(solution)/shard_map/psum | solution.py:772
  (545 shorter events, 278.2 us)
Async XLA Ops:
  7.2 839.8 %reduce-scatter.3.cloned.1.call-start = ((), (), s32[]{:S(2)}) async-start(), calls=%async_computation.2 | async-start | bytes 5242880 | tf_op jit(solution)/shard_map/reduce_scatter | solution.py:731
  55.1 69.1 %collective-permute-start.22 = (bf16[3,128,2048]{2,1,0:T(8,128)(2,1)}, bf16[3,128,2048]{2,1,0:T(8,128)(2,1)}, u32[]{:S(2)}, u32[]{:S(2)}) collective-permute-start(bf16[3,128,2048]{2,1,0:T(8,128)(2,1)} %get-tuple-element.110.rest_0_), channel_id=1, source_target_pairs={{0,8},{4,12},{8,0},{12,4},{16,24},{20,28},{24,16},{28,20},{1,9},{5... | collective-permute-start | bytes 4718600 | tf_op jit(solution)/shard_map/ppermute | solution.py:627
  74.2 65.0 %collective-permute-start.27 = (bf16[3,128,2048]{2,1,0:T(8,128)(2,1)}, bf16[3,128,2048]{2,1,0:T(8,128)(2,1)}, u32[]{:S(2)}, u32[]{:S(2)}) collective-permute-start(bf16[3,128,2048]{2,1,0:T(8,128)(2,1)} %get-tuple-element.109.rest_1_), channel_id=1, source_target_pairs={{0,16},{4,20},{8,24},{12,28},{16,0},{20,4},{24,8},{28,12},{1,17},{... | collective-permute-start | bytes 4718600 | tf_op jit(solution)/shard_map/ppermute | solution.py:627
  74.7 65.0 %collective-permute-start.20 = (bf16[3,128,2048]{2,1,0:T(8,128)(2,1)}, bf16[3,128,2048]{2,1,0:T(8,128)(2,1)}, u32[]{:S(2)}, u32[]{:S(2)}) collective-permute-start(bf16[3,128,2048]{2,1,0:T(8,128)(2,1)} %get-tuple-element.110.rest_0_), channel_id=1, source_target_pairs={{0,4},{4,0},{8,12},{12,8},{16,20},{20,16},{24,28},{28,24},{1,5},{5... | collective-permute-start | bytes 4718600 | tf_op jit(solution)/shard_map/ppermute | solution.py:627
  85.4 54.3 %collective-permute-start.21 = (bf16[3,128,2048]{2,1,0:T(8,128)(2,1)}, bf16[3,128,2048]{2,1,0:T(8,128)(2,1)}, u32[]{:S(2)}, u32[]{:S(2)}) collective-permute-start(bf16[3,128,2048]{2,1,0:T(8,128)(2,1)} %get-tuple-element.109.rest_1_), channel_id=1, source_target_pairs={{0,4},{4,0},{8,12},{12,8},{16,20},{20,16},{24,28},{28,24},{1,5},{5... | collective-permute-start | bytes 4718600 | tf_op jit(solution)/shard_map/ppermute | solution.py:627
  91.6 51.0 %collective-permute-start.1 = (bf16[256,2048]{1,0:T(8,128)(2,1)}, bf16[256,2048]{1,0:T(8,128)(2,1)}, u32[]{:S(2)}, u32[]{:S(2)}) collective-permute-start(bf16[256,2048]{1,0:T(8,128)(2,1)} %collective-permute-done), channel_id=1, source_target_pairs={{0,1},{1,2},{2,3},{3,0},{4,5},{5,6},{6,7},{7,4},{8,9},{9,10},{10,1... | collective-permute-start | bytes 3145736 | tf_op jit(solution)/shard_map/ppermute | solution.py:648
  139.1 56.7 %collective-permute-start.31 = (bf16[3,128,2048]{2,1,0:T(8,128)(2,1)}, bf16[3,128,2048]{2,1,0:T(8,128)(2,1)S(1)}, u32[]{:S(2)}, u32[]{:S(2)}) collective-permute-start(bf16[3,128,2048]{2,1,0:T(8,128)(2,1)} %collective-permute-done.23.rest_5_), channel_id=1, source_target_pairs={{0,16},{4,20},{8,24},{12,28},{16,0},{20,4},{24,8},{28,12},{1,17},{... | collective-permute-start | bytes 4718600 | tf_op jit(solution)/shard_map/ppermute | solution.py:627
  139.7 56.3 %collective-permute-start.25 = (bf16[3,128,2048]{2,1,0:T(8,128)(2,1)}, bf16[3,128,2048]{2,1,0:T(8,128)(2,1)S(1)}, u32[]{:S(2)}, u32[]{:S(2)}) collective-permute-start(bf16[3,128,2048]{2,1,0:T(8,128)(2,1)} %collective-permute-done.23.rest_5_), channel_id=1, source_target_pairs={{0,4},{4,0},{8,12},{12,8},{16,20},{20,16},{24,28},{28,24},{1,5},{5... | collective-permute-start | bytes 4718600 | tf_op jit(solution)/shard_map/ppermute | solution.py:627
  139.7 55.6 %collective-permute-start.30 = (bf16[3,128,2048]{2,1,0:T(8,128)(2,1)}, bf16[3,128,2048]{2,1,0:T(8,128)(2,1)}, u32[]{:S(2)}, u32[]{:S(2)}) collective-permute-start(bf16[3,128,2048]{2,1,0:T(8,128)(2,1)} %collective-permute-done.26.rest_8_), channel_id=1, source_target_pairs={{0,8},{4,12},{8,0},{12,4},{16,24},{20,28},{24,16},{28,20},{1,9},{5... | collective-permute-start | bytes 4718600 | tf_op jit(solution)/shard_map/ppermute | solution.py:627
  174.7 60.5 %collective-permute-start.28 = (bf16[3,128,2048]{2,1,0:T(8,128)(2,1)}, bf16[3,128,2048]{2,1,0:T(8,128)(2,1)}, u32[]{:S(2)}, u32[]{:S(2)}) collective-permute-start(bf16[3,128,2048]{2,1,0:T(8,128)(2,1)} %collective-permute-done.26.rest_8_), channel_id=1, source_target_pairs={{0,4},{4,0},{8,12},{12,8},{16,20},{20,16},{24,28},{28,24},{1,5},{5... | collective-permute-start | bytes 4718600 | tf_op jit(solution)/shard_map/ppermute | solution.py:627
  537.1 58.3 %collective-permute-start.73 = (bf16[2,2,128,2048]{3,2,0,1:T(8,128)(2,1)}, bf16[2,2,128,2048]{3,2,0,1:T(8,128)(2,1)}, u32[]{:S(2)}, u32[]{:S(2)}) collective-permute-start(bf16[2,2,128,2048]{3,2,0,1:T(8,128)(2,1)} %bitcast.362), channel_id=1, source_target_pairs={{0,4},{4,0},{8,12},{12,8},{16,20},{20,16},{24,28},{28,24},{1,5},{5... | collective-permute-start | bytes 6291464 | tf_op jit(solution)/shard_map/ppermute | solution.py:662
  538.5 53.8 %collective-permute-start.76 = (bf16[2,2,128,2048]{3,2,1,0:T(8,128)(2,1)}, bf16[2,2,128,2048]{3,2,1,0:T(8,128)(2,1)}, u32[]{:S(2)}, u32[]{:S(2)}) collective-permute-start(bf16[2,2,128,2048]{3,2,1,0:T(8,128)(2,1)} %dynamic-slice_bitcast_fusion), channel_id=1, source_target_pairs={{0,4},{4,0},{8,12},{12,8},{16,20},{20,16},{24,28},{28,24},{1,5},{5... | collective-permute-start | bytes 6291464 | tf_op jit(solution)/shard_map/ppermute | solution.py:662
  540.5 78.1 %collective-permute-start.67 = (bf16[2,2,128,2048]{3,2,0,1:T(8,128)(2,1)}, bf16[2,2,128,2048]{3,2,0,1:T(8,128)(2,1)}, u32[]{:S(2)}, u32[]{:S(2)}) collective-permute-start(bf16[2,2,128,2048]{3,2,0,1:T(8,128)(2,1)} %bitcast.363), channel_id=1, source_target_pairs={{0,4},{4,0},{8,12},{12,8},{16,20},{20,16},{24,28},{28,24},{1,5},{5... | collective-permute-start | bytes 6291464 | tf_op jit(solution)/shard_map/ppermute | solution.py:662
  542.0 72.6 %collective-permute-start.70 = (bf16[2,2,128,2048]{3,2,1,0:T(8,128)(2,1)}, bf16[2,2,128,2048]{3,2,1,0:T(8,128)(2,1)}, u32[]{:S(2)}, u32[]{:S(2)}) collective-permute-start(bf16[2,2,128,2048]{3,2,1,0:T(8,128)(2,1)} %dynamic-slice_bitcast_fusion.1), channel_id=1, source_target_pairs={{0,4},{4,0},{8,12},{12,8},{16,20},{20,16},{24,28},{28,24},{1,5},{5... | collective-permute-start | bytes 6291464 | tf_op jit(solution)/shard_map/ppermute | solution.py:662
  572.1 298.0 %reduce-scatter.5.cloned.1.call-start = ((), (), s32[]{:S(2)}) async-start(), calls=%async_computation.3 | async-start | bytes 5242880 | tf_op jit(solution)/shard_map/reduce_scatter | solution.py:755
  595.3 61.7 %collective-permute-start.35 = (bf16[256,2048]{1,0:T(8,128)(2,1)}, bf16[256,2048]{1,0:T(8,128)(2,1)S(1)}, u32[]{:S(2)}, u32[]{:S(2)}) collective-permute-start(bf16[256,2048]{1,0:T(8,128)(2,1)} %collective-permute-done.34), channel_id=1, source_target_pairs={{0,1},{1,2},{2,3},{3,0},{4,5},{5,6},{6,7},{7,4},{8,9},{9,10},{10,1... | collective-permute-start | bytes 3145736 | tf_op jit(solution)/shard_map/ppermute | solution.py:648
  614.6 122.8 %collective-permute-start.74 = (bf16[2,128,2048]{2,1,0:T(8,128)(2,1)}, bf16[2,128,2048]{2,1,0:T(8,128)(2,1)}, u32[]{:S(2)}, u32[]{:S(2)}) collective-permute-start(bf16[2,128,2048]{2,1,0:T(8,128)(2,1)} %dynamic-slice_bitcast_fusion.4), channel_id=1, source_target_pairs={{0,8},{4,12},{8,0},{12,4},{16,24},{20,28},{24,16},{28,20},{1,9},{5... | collective-permute-start | bytes 3145736 | tf_op jit(solution)/shard_map/ppermute | solution.py:662
  618.6 122.6 %collective-permute-start.77 = (bf16[2,128,2048]{2,1,0:T(8,128)(2,1)}, bf16[2,128,2048]{2,1,0:T(8,128)(2,1)}, u32[]{:S(2)}, u32[]{:S(2)}) collective-permute-start(bf16[2,128,2048]{2,1,0:T(8,128)(2,1)} %dynamic-slice_bitcast_fusion.3), channel_id=1, source_target_pairs={{0,16},{4,20},{8,24},{12,28},{16,0},{20,4},{24,8},{28,12},{1,17},{... | collective-permute-start | bytes 3145736 | tf_op jit(solution)/shard_map/ppermute | solution.py:662
  625.0 124.6 %collective-permute-start.68 = (bf16[2,128,2048]{2,1,0:T(8,128)(2,1)}, bf16[2,128,2048]{2,1,0:T(8,128)(2,1)}, u32[]{:S(2)}, u32[]{:S(2)}) collective-permute-start(bf16[2,128,2048]{2,1,0:T(8,128)(2,1)} %dynamic-slice_bitcast_fusion.6), channel_id=1, source_target_pairs={{0,8},{4,12},{8,0},{12,4},{16,24},{20,28},{24,16},{28,20},{1,9},{5... | collective-permute-start | bytes 3145736 | tf_op jit(solution)/shard_map/ppermute | solution.py:662
  627.8 126.8 %collective-permute-start.71 = (bf16[2,128,2048]{2,1,0:T(8,128)(2,1)}, bf16[2,128,2048]{2,1,0:T(8,128)(2,1)}, u32[]{:S(2)}, u32[]{:S(2)}) collective-permute-start(bf16[2,128,2048]{2,1,0:T(8,128)(2,1)} %dynamic-slice_bitcast_fusion.5), channel_id=1, source_target_pairs={{0,16},{4,20},{8,24},{12,28},{16,0},{20,4},{24,8},{28,12},{1,17},{... | collective-permute-start | bytes 3145736 | tf_op jit(solution)/shard_map/ppermute | solution.py:662
  657.0 47.8 %collective-permute-start.36 = (bf16[256,2048]{1,0:T(8,128)(2,1)S(1)}, bf16[256,2048]{1,0:T(8,128)(2,1)S(1)}, u32[]{:S(2)}, u32[]{:S(2)}) collective-permute-start(bf16[256,2048]{1,0:T(8,128)(2,1)S(1)} %collective-permute-done.35), channel_id=1, source_target_pairs={{0,1},{1,2},{2,3},{3,0},{4,5},{5,6},{6,7},{7,4},{8,9},{9,10},{10,1... | collective-permute-start | bytes 3145736 | tf_op jit(solution)/shard_map/ppermute | solution.py:648
  704.8 53.3 %collective-permute-start.62 = (bf16[2,128,2048]{2,1,0:T(8,128)(2,1)}, bf16[2,128,2048]{2,1,0:T(8,128)(2,1)}, u32[]{:S(2)}, u32[]{:S(2)}) collective-permute-start(bf16[2,128,2048]{2,1,0:T(8,128)(2,1)} %dynamic-slice_bitcast_fusion.8), channel_id=1, source_target_pairs={{0,8},{4,12},{8,0},{12,4},{16,24},{20,28},{24,16},{28,20},{1,9},{5... | collective-permute-start | bytes 3145736 | tf_op jit(solution)/shard_map/ppermute | solution.py:662
  741.2 53.0 %collective-permute-start.75 = (bf16[128,2048]{1,0:T(8,128)(2,1)}, bf16[128,2048]{1,0:T(8,128)(2,1)}, u32[]{:S(2)}, u32[]{:S(2)}) collective-permute-start(bf16[128,2048]{1,0:T(8,128)(2,1)} %dynamic-slice_bitcast_fusion.10), channel_id=1, source_target_pairs={{0,16},{4,20},{8,24},{12,28},{16,0},{20,4},{24,8},{28,12},{1,17},{... | collective-permute-start | bytes 1572872 | tf_op jit(solution)/shard_map/ppermute | solution.py:662
  749.6 47.0 %collective-permute-start.78 = (bf16[128,2048]{1,0:T(8,128)(2,1)}, bf16[128,2048]{1,0:T(8,128)(2,1)}, u32[]{:S(2)}, u32[]{:S(2)}) collective-permute-start(bf16[128,2048]{1,0:T(8,128)(2,1)} %dynamic-slice_bitcast_fusion.9), channel_id=1, source_target_pairs={{0,8},{4,12},{8,0},{12,4},{16,24},{20,28},{24,16},{28,20},{1,9},{5... | collective-permute-start | bytes 1572872 | tf_op jit(solution)/shard_map/ppermute | solution.py:662
  (169 other events, 2192.2 us)
Sparse Core Ops, SparseCore 0:
  572.2 104.3 reduce-scatter.2
  794.3 75.7 reduce-scatter.4

commit v3 on v2

v3 whole, which is shorter than its diff:
```python
import functools

import jax
import jax.numpy as jnp
from jax import lax
from jax.experimental import pallas as pl
from jax.experimental.pallas import tpu as pltpu
from jax.sharding import PartitionSpec as P

rms_eps = 1e-06
NEG = -1e30
LOG2E = 1.4426950408889634


def split_two(x):
    high = x.astype(jnp.bfloat16)
    return high, (x - high.astype(jnp.float32)).astype(jnp.bfloat16)


def dot32(a, b, dims):
    return lax.dot_general(a, b, (dims, ((), ())), preferred_element_type=jnp.float32)


def dot_three(a, b, dims):
    ah, al = split_two(a)
    bh, bl = split_two(b)
    return dot32(ah, bh, dims) + dot32(ah, bl, dims) + dot32(al, bh, dims)


NN, NT, TN = ((1,), (0,)), ((1,), (1,)), ((0,), (0,))


def mapped(v):
    return jnp.where(v > 0, v + 1.0, jnp.exp(jnp.minimum(v, 0.0)))


def key_reach(first, rows, keys):
    return min(keys, max(keys // 2, first + rows))


def key_limit(first, rows, prefix, valid):
    row = first + lax.broadcasted_iota(jnp.int32, (1, rows), 1)
    return jnp.minimum(valid - 1, jnp.maximum(row, prefix - 1))


def backward_kernel(bounds, q_ref, k_ref, v_ref, gc_ref, mix_ref, lse_ref, mem_ref, norm_ref, gate_ref, dq_ref, dk_ref, dv_ref, dmem_ref, dnorm_ref, dgate_ref, dk_acc, dv_acc, *, block):
    keys, hd = k_ref.shape
    prefix, valid = bounds[0], bounds[1]
    scale = hd ** -0.5
    gate = jax.nn.sigmoid(gate_ref[0])
    memory = mem_ref[0]
    norm = norm_ref[0]
    dmem = jnp.zeros((hd, hd), jnp.float32)
    dnorm = jnp.zeros((1, hd), jnp.float32)
    dgate = jnp.zeros((1, hd), jnp.float32)
    for first in range(keys - block, -1, -block):
        reach = key_reach(first, block, keys)
        rows = slice(first, first + block)
        q = q_ref[rows, :]
        gc = gc_ref[rows, :].astype(jnp.float32)
        mixed = mix_ref[rows, :]
        qm = mapped(q.astype(jnp.float32))
        inverse = 1.0 / jnp.sum(qm * norm, axis=-1, keepdims=True)
        retrieved = dot_three(qm, memory, NN) * inverse
        dgate = dgate + jnp.sum(gc * (retrieved - mixed), axis=0, keepdims=True)
        gnum = gate * gc * inverse
        gden = -jnp.sum(gnum * retrieved, axis=-1, keepdims=True)
        dmem = dmem + dot_three(qm, gnum, TN)
        dnorm = dnorm + jnp.sum(gden * qm, axis=0, keepdims=True)
        dq_mem = (dot_three(gnum, memory, NT) + gden * norm) * jnp.minimum(qm, 1.0)
        low = ((1.0 - gate) * gc).astype(jnp.bfloat16)
        delta = jnp.sum((low.astype(jnp.float32) * mixed).T, axis=0, keepdims=True)
        s = dot32(k_ref[:reach, :], q, NT) * (scale * LOG2E)
        limit = key_limit(first, block, prefix, valid)
        s = jnp.where(lax.broadcasted_iota(jnp.int32, s.shape, 0) <= limit, s - lse_ref[0, :, rows], NEG)
        p = jnp.exp2(s)
        gp = dot32(v_ref[:reach, :], low, NT)
        gs = (p * (gp - delta)).astype(jnp.bfloat16)
        dv = dot32(p.astype(jnp.bfloat16), low, NN)
        dk = dot32(gs, q, NN)
        if first == keys - block:
            dv_acc[...] = dv
            dk_acc[...] = dk
        else:
            dv_acc[:reach, :] += dv
            dk_acc[:reach, :] += dk
        dq = dot32(k_ref[:reach, :], gs, TN).T * scale
        dq_ref[rows, :] = (dq + dq_mem).astype(jnp.bfloat16)
    dk_ref[...] = (dk_acc[...] * scale).astype(jnp.bfloat16)
    dv_ref[...] = dv_acc[...].astype(jnp.bfloat16)
    dmem_ref[0] = dmem
    dnorm_ref[0] = dnorm
    dgate_ref[0] = dgate * (gate * (1.0 - gate))


def head_specs(keys, hd):
    rows = pl.BlockSpec((keys, hd), lambda h: (0, h))
    square = pl.BlockSpec((1, hd, hd), lambda h: (h, 0, 0))
    line = pl.BlockSpec((1, 1, hd), lambda h: (h, 0, 0))
    long = pl.BlockSpec((1, 1, keys), lambda h: (h, 0, 0))
    return rows, square, line, long


def attend_back(bounds, qkv, gc, mix, lse, memory, norm, gate, block=256):
    keys = qkv.shape[0]
    heads, hd = memory.shape[:2]
    rows, square, line, long = head_specs(keys, hd)
    key_rows = pl.BlockSpec((keys, hd), lambda h: (0, heads + h))
    value_rows = pl.BlockSpec((keys, hd), lambda h: (0, 2 * heads + h))
    f32 = jnp.float32
    S = jax.ShapeDtypeStruct
    low = S(gc.shape, jnp.bfloat16)
    return pl.pallas_call(
        functools.partial(backward_kernel, block=block),
        grid=(heads,),
        in_specs=[pl.BlockSpec(memory_space=pltpu.SMEM), rows, key_rows, value_rows, rows, rows, long, square, line, line],
        out_specs=[rows, rows, rows, square, line, line],
        out_shape=[low, low, low, S((heads, hd, hd), f32), S((heads, 1, hd), f32), S((heads, 1, hd), f32)],
        scratch_shapes=[pltpu.VMEM((keys, hd), f32), pltpu.VMEM((keys, hd), f32)],
        compiler_params=pltpu.CompilerParams(vmem_limit_bytes=48 * 2**20),
        name="attend_backward",
    )(bounds, qkv, qkv, qkv, gc, mix, lse, memory, norm.reshape(heads, 1, hd), jnp.broadcast_to(gate[:, None, None], (heads, 1, hd)))


norm_eps = 1e-06
MESH = pl.DeviceIdType.MESH
RIGHT, LEFT = 0, 1


class Line:
    def __init__(self, size, send_sem, recv_sem):
        self.size, self.send_sem, self.recv_sem = size, send_sem, recv_sem
        self.here = lax.axis_index("tp")

    def copy(self, phase, way, slot, src, dst):
        to = self.here + 1 if way == RIGHT else self.here - 1
        return pltpu.make_async_remote_copy(
            src_ref=src,
            dst_ref=dst,
            send_sem=self.send_sem.at[phase, way, slot],
            recv_sem=self.recv_sem.at[phase, way, slot],
            device_id={"tp": to},
            device_id_type=MESH,
        )

    def arrived(self, phase, way, slot, dst):
        self.copy(phase, way, slot, dst, dst).wait_recv()

    def scatter_step(self, phase, k, part, land_right, land_left):
        n, t = self.size, self.here
        far, near = n - 1 - k, k

        def pass_on(way, shard, land, first):
            @pl.when(jnp.logical_not(first))
            def _():
                self.arrived(phase, way, k, land)
                part[shard] = (part[shard].astype(jnp.float32) + land[...].astype(jnp.float32)).astype(part.dtype)

            self.copy(phase, way, k, part.at[shard], land).start()

        @pl.when(t < far)
        def _():
            pass_on(RIGHT, far, land_right.at[far - 1], t == 0)

        @pl.when(t > near)
        def _():
            pass_on(LEFT, near, land_left.at[near], t == n - 1)

    def scatter_end(self, phase, part, land_right, land_left, total):
        n, t = self.size, self.here
        total[...] = part[t].astype(jnp.float32)

        @pl.when(t > 0)
        def _():
            self.arrived(phase, RIGHT, n - 1 - t, land_right.at[t - 1])
            total[...] += land_right[t - 1].astype(jnp.float32)

        @pl.when(t < n - 1)
        def _():
            self.arrived(phase, LEFT, t, land_left.at[t])
            total[...] += land_left[t].astype(jnp.float32)

    def scatter_sent(self, phase, part, land_right, land_left):
        n, t = self.size, self.here
        for k in range(n - 1):
            far, near = n - 1 - k, k

            @pl.when(t < far)
            def _():
                self.copy(phase, RIGHT, k, part.at[far], land_right.at[far - 1]).wait_send()

            @pl.when(t > near)
            def _():
                self.copy(phase, LEFT, k, part.at[near], land_left.at[near]).wait_send()

    def gather_step(self, phase, k, shard_at):
        n, t = self.size, self.here

        @pl.when(t >= k)
        def _():
            shard = shard_at(t - k)
            if k > 0:
                self.arrived(phase, RIGHT, k - 1, shard)
            if k < n - 1:
                @pl.when(t < n - 1)
                def _():
                    self.copy(phase, RIGHT, k, shard, shard).start()

        @pl.when(t + k <= n - 1)
        def _():
            shard = shard_at(t + k)
            if k > 0:
                self.arrived(phase, LEFT, k - 1, shard)
            if k < n - 1:
                @pl.when(t > 0)
                def _():
                    self.copy(phase, LEFT, k, shard, shard).start()

    def gather_sent(self, phase, shard_at):
        n, t = self.size, self.here
        for k in range(n - 1):
            @pl.when((t >= k) & (t < n - 1))
            def _():
                self.copy(phase, RIGHT, k, shard_at(t - k), shard_at(t - k)).wait_send()

            @pl.when((t + k <= n - 1) & (t > 0))
            def _():
                self.copy(phase, LEFT, k, shard_at(t + k), shard_at(t + k)).wait_send()


class Cube:
    def __init__(self, size, send_sem, recv_sem):
        self.size, self.send_sem, self.recv_sem = size, send_sem, recv_sem
        self.here = lax.axis_index("fsdp")
        self.levels = size.bit_length() - 1
        ups = [1 << b for b in range(1, self.levels)]
        self.orders = [ups[::-1] + [1], ups + [1]]

    def peer(self, bit):
        return lax.bitwise_xor(self.here, bit)

    def held(self, half, stage):
        masks = [0]
        for bit in self.orders[half][:stage]:
            masks += [mask ^ bit for mask in masks]
        return masks

    def copy(self, item, half, mask, bit, block_at):
        owner = self.peer(mask) if mask else self.here
        block = block_at(owner, half)
        return pltpu.make_async_remote_copy(
            src_ref=block,
            dst_ref=block,
            send_sem=self.send_sem.at[item, half, mask ^ bit],
            recv_sem=self.recv_sem.at[item, half, mask ^ bit],
            device_id={"fsdp": self.peer(bit)},
            device_id_type=MESH,
        )

    def await_stage(self, item, stage, block_at):
        for half in range(2):
            bit = self.orders[half][stage]
            for mask in self.held(half, stage):
                block = block_at(self.peer(mask ^ bit), half)
                pltpu.make_async_remote_copy(
                    src_ref=block,
                    dst_ref=block,
                    send_sem=self.send_sem.at[item, half, mask ^ bit],
                    recv_sem=self.recv_sem.at[item, half, mask ^ bit],
                    device_id={"fsdp": self.peer(bit)},
                    device_id_type=MESH,
                ).wait_recv()

    def stage(self, item, stage, block_at):
        if stage > 0:
            self.await_stage(item, stage - 1, block_at)
        if stage == self.levels:
            return
        for half in range(2):
            bit = self.orders[half][stage]
            for mask in self.held(half, stage):
                self.copy(item, half, mask, bit, block_at).start()

    def sent(self, item, block_at):
        for stage in range(self.levels):
            for half in range(2):
                bit = self.orders[half][stage]
                for mask in self.held(half, stage):
                    self.copy(item, half, mask, bit, block_at).wait_send()


GELU_A, GELU_B = 0.7978845608028654, 0.044715


def gelu_pair(v):
    square = v * v
    curve = jnp.tanh(v * (GELU_A + GELU_A * GELU_B * square))
    half = 0.5 + 0.5 * curve
    slope = half + (0.5 * v) * (1.0 - curve * curve) * (GELU_A + 3.0 * GELU_A * GELU_B * square)
    return v * half, slope


def inverse_rms(v):
    return lax.rsqrt(jnp.mean(v * v, axis=-1, keepdims=True) + norm_eps)


def layer_kernel(
    bounds, gain_in, live_ref, mem_ref, norm_ref, gate_ref,
    stream_hbm, cot_hbm, wq_hbm, wk_hbm, wv_hbm, wo_hbm, wg_hbm, wu_hbm, wd_hbm,
    mlp_hbm, attn_out, one_out, qkv_out, comb_out, mix_out, cot_all, x_out, hid_out, gl_out, ul_out, terms_hbm,
    result_out, gmid_out, branch_out, kept_out, land,
    ggain_ref, stat_ref, lse_ref, memo_ref, normo_ref, gain,
    w_three, x, cot, hid, gl, ul, part, land_r, land_l, stream, mid, total,
    own_sem, load_sem, out_sem, term_sem, grad_sem, trade_send, trade_recv, gain_send, gain_recv, cube_send, cube_recv, line_send, line_recv,
    *, chunks, tp_size, fsdp_size, tile,
):
    n = tp_size
    bf16, f32 = jnp.bfloat16, jnp.float32
    t, f = lax.axis_index("tp"), lax.axis_index("fsdp")
    c_rows, width = x.shape[2], x.shape[3]
    units = hid.shape[1]
    rows_dev = stream.shape[0]
    length = rows_dev * n
    heads, hd = mem_ref.shape[0], mem_ref.shape[2]
    inner = heads * hd
    shard = width // fsdp_size
    line = Line(n, line_send, line_recv)
    cube = Cube(fsdp_size, cube_send, cube_recv)
    bits = [1 << b for b in range(cube.levels)]
    AG1 = 0

    def ph(kind, c):
        return 1 + kind * chunks + c

    COT, RS1, AG2, RS3, AG4, RS2 = range(6)

    attn_w = w_three.at[0]
    qkv = w_three.at[1]
    flat_one = w_three.at[2]

    def stream_at(s):
        return w_three.at[2, pl.ds(pl.multiple_of(length + s * rows_dev, rows_dev), rows_dev), :]

    def x_at(c):
        return lambda s: x.at[c, s]

    def cot_at(c):
        return lambda s: cot_all.at[c, s]

    def lands(c):
        return part.at[c], land_r.at[c], land_l.at[c]

    def block_of(item):
        whole = attn_w if item == 0 else mlp_hbm.at[item - 1]

        def at(owner, half):
            rows = shard // 2
            return whole.at[pl.ds(pl.multiple_of(owner * shard + half * rows, rows), rows), :]

        return at

    def push(item, stage):
        cube.stage(item, stage, block_of(item))

    own_rows = pl.ds(pl.multiple_of(f * shard, shard), shard)
    own = [
        pltpu.make_async_copy(w, w_three.at[0, own_rows, p * inner : (p + 1) * inner], own_sem.at[p])
        for p, w in enumerate((wq_hbm, wk_hbm, wv_hbm, wo_hbm))
    ]
    own += [pltpu.make_async_copy(stream_hbm, stream_at(t), own_sem.at[4]), pltpu.make_async_copy(stream_hbm, stream, own_sem.at[5])]
    homes = [hid.at[0:shard, :], hid.at[shard : 2 * shard, :], gl.at[0:shard, :]]
    own += [pltpu.make_async_copy(w, homes[m], own_sem.at[6 + m]) for m, w in enumerate((wg_hbm, wu_hbm, wd_hbm))]
    own.append(pltpu.make_async_copy(cot_hbm, ul.at[0:rows_dev, :], own_sem.at[9]))
    placed = [pltpu.make_async_copy(homes[m], mlp_hbm.at[m, own_rows, :], own_sem.at[6 + m]) for m in range(3)]
    placed += [
        pltpu.make_async_copy(ul.at[c * c_rows : (c + 1) * c_rows, :], cot_all.at[c, t], own_sem.at[9 + c])
        for c in range(chunks)
    ]
    for item in own:
        item.start()
    gain[...] = gain_in[...]
    ggain_ref[...] = jnp.zeros_like(ggain_ref)
    stat_ref[...] = jnp.zeros_like(stat_ref)

    barrier = pltpu.get_barrier_semaphore()

    @pl.when(t > 0)
    def _():
        pl.semaphore_signal(barrier, inc=1, device_id={"tp": t - 1}, device_id_type=MESH)

    @pl.when(t < n - 1)
    def _():
        pl.semaphore_signal(barrier, inc=1, device_id={"tp": t + 1}, device_id_type=MESH)

    for bit in bits:
        pl.semaphore_signal(barrier, inc=1, device_id={"fsdp": cube.peer(bit)}, device_id_type=MESH)
    peers = (t > 0).astype(jnp.int32) + (t < n - 1).astype(jnp.int32) + len(bits)
    pl.semaphore_wait(barrier, peers)

    for item in own[:6]:
        item.wait()
    push(0, 0)
    line.gather_step(AG1, 0, stream_at)
    for item in own[6:]:
        item.wait()
    for item in placed:
        item.start()
    for level, bit in enumerate(bits):
        trade = pltpu.make_async_remote_copy(
            src_ref=gain,
            dst_ref=total.at[8 * level : 8 * level + 8, :],
            send_sem=gain_send.at[level],
            recv_sem=gain_recv.at[level],
            device_id={"fsdp": cube.peer(bit)},
            device_id_type=MESH,
        )
        trade.start()
        trade.wait()
        gain[...] += total[8 * level : 8 * level + 8, :]
    for item in placed:
        item.wait()

    def norm_one(s):
        v = stream_at(s)[...].astype(f32)
        flat_one[pl.ds(pl.multiple_of(s * rows_dev, rows_dev), rows_dev), :] = (
            v * inverse_rms(v) * gain[0:1, :]
        ).astype(bf16)

    def project_one(s):
        rows = pl.ds(pl.multiple_of(s * rows_dev, rows_dev), rows_dev)

        @pl.loop(0, 3)
        def _(p):
            cols = pl.ds(pl.multiple_of(p * inner, inner), inner)
            qkv[rows, cols] = dot32(flat_one[rows, :], attn_w[:, cols], NN).astype(bf16)

    def arrived_pair(k, work):
        @pl.when(t >= k)
        def _():
            work(t - k)

        @pl.when(t + k <= n - 1)
        def _():
            work(t + k)

    norm_one(t)
    push(0, 1)
    push(1, 0)
    line.gather_step(AG1, 1, stream_at)
    for stage in range(2, cube.levels):
        push(0, stage)
    arrived_pair(1, norm_one)
    push(0, cube.levels)
    attn_save = pltpu.make_async_copy(attn_w, attn_out, out_sem.at[0])
    attn_save.start()
    project_one(t)
    push(1, 1)
    push(2, 0)
    line.gather_step(AG1, 2, stream_at)
    arrived_pair(1, project_one)

    def both(s):
        norm_one(s)
        project_one(s)

    for k in range(2, n):
        if k > 2:
            line.gather_step(AG1, k, stream_at)
        if k == n - 1:
            for c in range(chunks):
                line.gather_step(ph(COT, c), 0, cot_at(c))
        arrived_pair(k, both)
    one_save = pltpu.make_async_copy(flat_one.at[0:length, :], one_out, out_sem.at[1])
    one_save.start()
    qkv_save = pltpu.make_async_copy(qkv.at[0:length, 0 : 3 * inner], qkv_out, out_sem.at[2])
    qkv_save.start()
    for stage in range(2, cube.levels):
        push(1, stage)
    push(2, 1)
    push(3, 0)
    push(1, cube.levels)

    prefix, valid = bounds[0], bounds[1]
    score_scale = hd ** -0.5 * LOG2E

    def attend_rows(s):
        first = s * rows_dev
        reach = key_reach(first, rows_dev, length)
        limit = key_limit(first, rows_dev, prefix, valid)

        @pl.loop(0, heads)
        def _(h):
            def lanes(group):
                return pl.ds(pl.multiple_of(group * inner + h * hd, hd), hd)

            q = qkv[first : first + rows_dev, lanes(0)]
            scores = dot32(qkv[0:reach, lanes(1)], q, NT) * score_scale
            scores = jnp.where(lax.broadcasted_iota(jnp.int32, scores.shape, 0) <= limit, scores, NEG)
            top = jnp.max(scores, axis=0, keepdims=True)
            probs = jnp.exp2(scores - top)
            row_total = jnp.sum(probs, axis=0, keepdims=True)
            mixed = (dot32(qkv[0:reach, lanes(2)], probs.astype(bf16), TN) / row_total).T
            lse_ref[h, :, first : first + rows_dev] = top + jnp.log2(row_total)
            gate = jax.nn.sigmoid(gate_ref[h])
            qm = mapped(q.astype(f32))
            denominator = jnp.sum(qm * norm_ref[h], axis=-1, keepdims=True)
            retrieved = dot_three(qm, mem_ref[h], NN) / denominator
            mid[:, pl.ds(pl.multiple_of(s * inner + h * hd, hd), hd)] = mixed
            both_mix = (gate * retrieved + (1.0 - gate) * mixed).astype(bf16)
            for c in range(chunks):
                hid[s * c_rows : (s + 1) * c_rows, pl.ds(pl.multiple_of(c * inner + h * hd, hd), hd)] = both_mix[
                    c * c_rows : (c + 1) * c_rows
                ]

    def update_memory():
        @pl.loop(0, heads)
        def _(h):
            km = mapped(qkv[0:length, pl.ds(pl.multiple_of(inner + h * hd, hd), hd)].astype(f32))
            km = jnp.where(lax.broadcasted_iota(jnp.int32, km.shape, 0) < valid, km, 0.0)
            kh, kl = split_two(km)
            values = qkv[0:length, pl.ds(pl.multiple_of(2 * inner + h * hd, hd), hd)]
            memo_ref[h] = mem_ref[h] + dot32(kh, values, TN) + dot32(kl, values, TN)
            normo_ref[h] = norm_ref[h] + jnp.sum(km, axis=0, keepdims=True)

    for s in range(n):
        attend_rows(s)
    for stage in range(2, cube.levels):
        push(2, stage)
    comb_saves = []
    for s in range(n):
        comb_saves.append(
            pltpu.make_async_copy(mid.at[:, s * inner : (s + 1) * inner], mix_out.at[s * rows_dev : (s + 1) * rows_dev, :], out_sem.at[3 + s])
        )
        for c in range(chunks):
            comb_saves.append(
                pltpu.make_async_copy(
                    hid.at[s * c_rows : (s + 1) * c_rows, c * inner : (c + 1) * inner],
                    comb_out.at[s, c],
                    out_sem.at[3 + n + s * chunks + c],
                )
            )
    for item in comb_saves:
        item.start()

    def project(c):
        flat = part.at[c].reshape(n * c_rows, width)

        @pl.loop(0, width // tile)
        def _(j):
            cols = pl.ds(pl.multiple_of(j * tile, tile), tile)
            flat[:, cols] = dot32(
                hid[:, c * inner : (c + 1) * inner], attn_w[cols, 3 * inner : 4 * inner], NT
            ).astype(bf16)

    def norm_two(c):
        rows = slice(c * c_rows, (c + 1) * c_rows)
        branch = total[...]
        live = live_ref[rows, :]
        stat_ref[0:1, :] += jnp.sum(jnp.sum(branch * branch, axis=-1, keepdims=True) * live, axis=0, keepdims=True)
        m = stream[rows, :].astype(f32) + branch
        mid[rows, :] = m
        x[c, t] = (m * inverse_rms(m) * gain[1:2, :]).astype(bf16)

    def first_half(c, service):
        flat = x.at[c].reshape(n * c_rows, width)
        cot_flat = cot.reshape(n * c_rows, width)

        @pl.loop(0, units // tile)
        def _(j):
            cols = pl.ds(pl.multiple_of(j * tile, tile), tile)
            gate_pre = dot32(flat[...], w_three[0, :, cols], NN)
            up_pre = dot32(flat[...], w_three[1, :, cols], NN)
            grad_hidden = dot32(cot_flat[...], w_three[2, :, cols], NN)
            value, slope = gelu_pair(gate_pre)
            hid[:, cols] = (value * up_pre).astype(bf16)
            ul[:, cols] = (grad_hidden * value).astype(bf16)
            gl[:, cols] = (grad_hidden * up_pre * slope).astype(bf16)
            service(j)

    def second_half(c):
        flat = part.at[c].reshape(n * c_rows, width)

        @pl.loop(0, width // tile)
        def _(j):
            cols = pl.ds(pl.multiple_of(j * tile, tile), tile)
            terms = dot32(gl[...], w_three[0, cols, :], NT) + dot32(ul[...], w_three[1, cols, :], NT)
            flat[:, cols] = terms.astype(bf16)

    def branch_terms(c):
        @pl.loop(0, width // tile)
        def _(j):
            cols = pl.ds(pl.multiple_of(j * tile, tile), tile)
            ul[:, cols] = dot32(hid[...], w_three[2, cols, :], NT).astype(bf16)

    def norm_back(c):
        rows = slice(c * c_rows, (c + 1) * c_rows)
        m = mid[rows, :]
        inv = inverse_rms(m)
        u = m * inv
        gn = total[...]
        e = gn * gain[1:2, :]
        ggain_ref[...] += jnp.sum(gn * u, axis=0, keepdims=True)
        gm = stream[rows, :].astype(f32) + inv * (e - u * jnp.mean(e * u, axis=-1, keepdims=True))
        total[...] = gm
        x[c, t] = gm.astype(bf16)

    def scatter(kind, c, k):
        line.scatter_step(ph(kind, c), k, *lands(c))

    def gather(kind, c, k):
        line.gather_step(ph(kind, c), k, x_at(c) if kind != COT else cot_at(c))

    project(0)
    scatter(RS1, 0, 0)
    project(1)
    scatter(RS1, 1, 0)
    attn_save.wait()
    cube.sent(0, block_of(0))
    gate_load = pltpu.make_async_copy(mlp_hbm.at[0], w_three.at[0], load_sem.at[0])
    gate_load.start()
    gather(COT, 0, 1)
    gather(COT, 1, 1)
    update_memory()
    scatter(RS1, 0, 1)
    push(2, cube.levels)
    push(3, 1)
    one_save.wait()
    qkv_save.wait()
    up_load = pltpu.make_async_copy(mlp_hbm.at[1], w_three.at[1], load_sem.at[1])
    up_load.start()
    gather(COT, 0, 2)
    for k in range(2, n - 1):
        scatter(RS1, 0, k)
    for item in comb_saves:
        item.wait()
    line.scatter_end(ph(RS1, 0), *lands(0), total)
    norm_two(0)
    gather(AG2, 0, 0)
    scatter(RS1, 1, 1)
    gather(COT, 1, 2)
    for stage in range(2, cube.levels):
        push(3, stage)
    for k in range(1, n - 1):
        gather(AG2, 0, k)
        if k + 1 < n - 1:
            scatter(RS1, 1, k + 1)
    gather(COT, 0, 3)
    cot_loads = [pltpu.make_async_copy(cot_all.at[c], cot, load_sem.at[3 + c]) for c in range(chunks)]
    cot_loads[0].start()
    push(3, cube.levels)
    line.gather_sent(AG1, stream_at)
    down_load = pltpu.make_async_copy(mlp_hbm.at[2], w_three.at[2], load_sem.at[2])
    down_load.start()
    line.scatter_end(ph(RS1, 1), *lands(1), total)
    norm_two(1)
    cot_own = pltpu.make_async_copy(cot_hbm, stream, own_sem.at[5])
    cot_own.start()
    gather(AG2, 1, 0)
    gather(AG2, 0, n - 1)
    gather(COT, 1, 3)
    gate_load.wait()
    up_load.wait()
    down_load.wait()
    cot_own.wait()
    outs = {}

    def send_out(name, c, src, dst, sem):
        outs[name, c] = pltpu.make_async_copy(src, dst, out_sem.at[sem])
        outs[name, c].start()

    def save_terms(c):
        for s in range(n):
            outs[("terms", s), c] = pltpu.make_async_copy(
                ul.at[s * c_rows : (s + 1) * c_rows, :], terms_hbm.at[c, s], term_sem.at[c * n + s]
            )
            outs[("terms", s), c].start()

    def await_terms(c):
        for s in range(n):
            outs[("terms", s), c].wait()

    def rows_of(ref, c):
        return ref.at[pl.ds(c * c_rows, c_rows), :]

    def save_chunk(c):
        send_out("x", c, x.at[c], x_out.at[c], 0)
        send_out("hid", c, hid, hid_out.at[c], 1)
        send_out("gl", c, gl, gl_out.at[c], 2)
        send_out("ul", c, ul, ul_out.at[c], 3)

    def finish_back(c):
        line.scatter_end(ph(RS3, c), *lands(c), total)
        norm_back(c)
        send_out("gmid", c, total, rows_of(gmid_out, c), 5)
        gather(AG4, c, 0)
        outs["gmid", c].wait()

    def start_branch(c):
        line.scatter_sent(ph(RS3, c), *lands(c))
        load = pltpu.make_async_copy(terms_hbm.at[c], part.at[c], load_sem.at[5])
        load.start()
        load.wait()
        scatter(RS2, c, 0)

    def finish_branch(c):
        rows = slice(c * c_rows, (c + 1) * c_rows)
        line.scatter_end(ph(RS2, c), *lands(c), total)
        branch = total[...]
        result = mid[rows, :] + branch
        live = live_ref[rows, :]
        stat_ref[1:2, :] += jnp.sum(jnp.sum(result * result, axis=-1, keepdims=True) * live, axis=0, keepdims=True)
        stat_ref[2:3, :] += jnp.sum(jnp.sum(branch * branch, axis=-1, keepdims=True) * live, axis=0, keepdims=True)
        part[c, t] = result.astype(bf16)
        send_out("result", c, part.at[c, t], rows_of(result_out, c), 6)
        outs["result", c].wait()

    def during(*steps):
        def service(j):
            for at, step in enumerate(steps):
                @pl.when(j == at)
                def _():
                    step()

        return service

    half_rows = shard // 2
    flat_w = w_three.reshape(3 * width, units)
    cot_flat = cot.reshape(n * c_rows, width)
    trade_orders = [[1] + [1 << b for b in range(1, cube.levels)], [1] + [1 << b for b in range(cube.levels - 1, 0, -1)]]
    spare = width // 2
    sources = ((x_out, gl_out), (x_out, ul_out), (cot_all, hid_out))

    def grad_loads(g):
        left, right = sources[g]
        loads = [
            pltpu.make_async_copy(right.at[0], hid, grad_sem.at[0]),
            pltpu.make_async_copy(right.at[1], gl, grad_sem.at[1]),
            pltpu.make_async_copy(left.at[1], cot, grad_sem.at[2]),
        ]
        for s in range(n):
            loads.append(pltpu.make_async_copy(left.at[0, s], ul.at[s * c_rows : (s + 1) * c_rows, :], grad_sem.at[8 + s]))
        return loads

    def weight_grad(g, service=lambda j: None, wide=256):
        for item in grad_loads(g):
            item.start()
        for item in grad_loads(g):
            item.wait()
        if g > 0:
            first_trade(g - 1).wait_send()

        @pl.loop(0, width // wide)
        def _(j):
            cols = pl.ds(pl.multiple_of(j * wide, wide), wide)
            for first in range(0, units, units // 2):
                span = slice(first, first + units // 2)
                terms = dot32(ul[:, cols], hid[:, span], TN) + dot32(cot_flat[:, cols], gl[:, span], TN)
                for q in range(wide // shard):
                    mask = lax.bitwise_xor(j * (wide // shard) + q, f)
                    row = lax.rem(mask, 2) * spare + (1 - lax.rem(mask, 2)) * (g * width) + (mask // 2) * shard
                    flat_w[pl.ds(pl.multiple_of(row, shard), shard), span] = terms[q * shard : (q + 1) * shard].astype(bf16)
            service(j)

        first_trade(g).start()

    def first_trade(g):
        return pltpu.make_async_remote_copy(
            src_ref=flat_w.at[spare : 2 * spare, :],
            dst_ref=land.at[g, 0],
            send_sem=trade_send.at[g, 0, 0, 0],
            recv_sem=trade_recv.at[g, 0, 0, 0],
            device_id={"fsdp": cube.peer(1)},
            device_id_type=MESH,
        )

    def trades(g, i):
        for half in range(2):
            order = trade_orders[half]
            bit = order[i]
            for mask in range(fsdp_size):
                if all(mask & b == 0 for b in order[: i + 1]):
                    there = pl.ds((mask // 2) * shard + half * half_rows, half_rows)
                    here = pl.ds(g * width + ((mask ^ bit) // 2) * shard + half * half_rows, half_rows)
                    yield mask, half, pltpu.make_async_remote_copy(
                        src_ref=flat_w.at[here, :],
                        dst_ref=land.at[g, i, there, :],
                        send_sem=trade_send.at[g, i, half, mask // 2],
                        recv_sem=trade_recv.at[g, i, half, mask // 2],
                        device_id={"fsdp": cube.peer(bit)},
                        device_id_type=MESH,
                    )

    def trade_start(g, i):
        for _, _, item in trades(g, i):
            item.start()

    def add_first(g):
        first_trade(g).wait_recv()
        load = pltpu.make_async_copy(land.at[g, 0], flat_w.at[width + spare : width + 2 * spare, :], grad_sem.at[3])
        load.start()
        load.wait()

        @pl.loop(0, spare // half_rows)
        def _(r):
            mine = pl.ds(pl.multiple_of(g * width + r * half_rows, half_rows), half_rows)
            came = pl.ds(pl.multiple_of(width + spare + r * half_rows, half_rows), half_rows)
            flat_w[mine, :] = (flat_w[mine, :].astype(f32) + flat_w[came, :].astype(f32)).astype(bf16)

        trade_start(g, 1)

    def add_next(g, i):
        places = []
        for mask, half, item in trades(g, i):
            item.wait_recv()
            places.append((mask // 2) * shard + half * half_rows)
        loads = [
            pltpu.make_async_copy(
                land.at[g, i, place : place + half_rows, :],
                flat_w.at[2 * width + spare + place : 2 * width + spare + place + half_rows, :],
                grad_sem.at[4 + at % 4],
            )
            for at, place in enumerate(places)
        ]
        for base in range(0, len(loads), 4):
            for item in loads[base : base + 4]:
                item.start()
            for item in loads[base : base + 4]:
                item.wait()
        for place in places:
            mine = slice(g * width + place, g * width + place + half_rows)
            came = slice(2 * width + spare + place, 2 * width + spare + place + half_rows)
            flat_w[mine, :] = (flat_w[mine, :].astype(f32) + flat_w[came, :].astype(f32)).astype(bf16)
        trade_start(g, i + 1)
        if i + 1 == cube.levels - 1:
            send_out("kept", g, flat_w.at[g * width : g * width + shard, :], kept_out.at[g], 8 + g)

    def trade_end(g):
        for _, _, item in trades(g, cube.levels - 1):
            item.wait_recv()
        outs["kept", g].wait()

    def trade_sent(g):
        for i in range(1, cube.levels):
            for _, _, item in trades(g, i):
                item.wait_send()

    cot_loads[0].wait()
    first_half(0, during(*[functools.partial(gather, AG2, 1, k) for k in range(1, n)]))
    cot_loads[1].start()
    save_chunk(0)
    line.scatter_sent(ph(RS1, 0), *lands(0))
    second_half(0)
    line.gather_sent(ph(AG2, 0), x_at(0))
    outs["x", 0].wait()
    outs["ul", 0].wait()
    scatter(RS3, 0, 0)
    branch_terms(0)
    save_terms(0)
    outs["hid", 0].wait()
    outs["gl", 0].wait()
    await_terms(0)
    cot_loads[1].wait()
    first_half(1, during(lambda: None, *[functools.partial(scatter, RS3, 0, k) for k in range(1, n - 1)]))
    save_chunk(1)
    line.scatter_sent(ph(RS1, 1), *lands(1))
    second_half(1)
    line.gather_sent(ph(AG2, 1), x_at(1))
    outs["x", 1].wait()
    outs["ul", 1].wait()
    scatter(RS3, 1, 0)
    finish_back(0)
    branch_terms(1)
    save_terms(1)
    outs["hid", 1].wait()
    outs["gl", 1].wait()
    for item in range(1, 4):
        cube.sent(item, block_of(item))
    scatter(RS3, 1, 1)
    gather(AG4, 0, 1)
    start_branch(0)
    await_terms(1)

    def skip():
        pass

    def z_one():
        for k in range(2, n - 1):
            scatter(RS3, 1, k)
        gather(AG4, 0, 2)

    weight_grad(0, during(*[skip] * 6, z_one))
    scatter(RS2, 0, 1)
    weight_grad(1)
    finish_back(1)
    for k in range(3, n):
        gather(AG4, 0, k)
    send_out("branch", 0, x.at[0], branch_out.at[:, 0], 0)
    for k in range(2, n - 1):
        scatter(RS2, 0, k)
    add_first(0)
    gather(AG4, 1, 1)
    start_branch(1)
    weight_grad(2)
    finish_branch(0)
    gather(AG4, 1, 2)
    scatter(RS2, 1, 1)
    add_first(1)
    for i in range(1, cube.levels - 1):
        add_next(0, i)
    for k in range(3, n):
        gather(AG4, 1, k)
    send_out("branch", 1, x.at[1], branch_out.at[:, 1], 7)
    for k in range(2, n - 1):
        scatter(RS2, 1, k)
    add_first(2)
    finish_branch(1)
    for g in (1, 2):
        for i in range(1, cube.levels - 1):
            add_next(g, i)
    for g in range(3):
        trade_end(g)
        trade_sent(g)
    first_trade(2).wait_send()
    for c in range(chunks):
        outs["branch", c].wait()
    for c in range(chunks):
        line.gather_sent(ph(COT, c), cot_at(c))
        line.gather_sent(ph(AG4, c), x_at(c))
        line.scatter_sent(ph(RS2, c), *lands(c))


def whole_layer(bounds, gains, live, memory, norm, gate, stream, cot, attn_weights, mlp_weights, tp_size, fsdp_size, collective_id, tile=512):
    chunks = 2
    rows, width = stream.shape
    inner = attn_weights[0].shape[1]
    units = mlp_weights[0].shape[1]
    heads, hd = memory.shape[:2]
    length = rows * tp_size
    c_rows = rows // chunks
    bf, f32 = jnp.bfloat16, jnp.float32
    S = jax.ShapeDtypeStruct
    any_space = pl.BlockSpec(memory_space=pl.ANY)
    vmem = pl.BlockSpec(memory_space=pltpu.VMEM)
    smem = pl.BlockSpec(memory_space=pltpu.SMEM)
    grid_rows = (chunks, tp_size, c_rows)
    flat_rows = (chunks, tp_size * c_rows)
    levels = fsdp_size.bit_length() - 1
    V, DMA = pltpu.VMEM, pltpu.SemaphoreType.DMA
    return pl.pallas_call(
        functools.partial(layer_kernel, chunks=chunks, tp_size=tp_size, fsdp_size=fsdp_size, tile=tile),
        in_specs=[smem] + [vmem] * 5 + [any_space] * 9,
        out_specs=[any_space] * 17 + [vmem] * 6,
        out_shape=[
            S((3, width, units), bf),
            S((width, 4 * inner), bf),
            S((length, width), bf),
            S((length, 3 * inner), bf),
            S((tp_size, chunks, c_rows, inner), bf),
            S((length, inner), f32),
            S(grid_rows + (width,), bf),
            S(grid_rows + (width,), bf),
            S(flat_rows + (units,), bf), S(flat_rows + (units,), bf), S(flat_rows + (units,), bf),
            S(grid_rows + (width,), bf),
            S((rows, width), bf),
            S((rows, width), f32),
            S((tp_size, chunks, c_rows, width), bf),
            S((3, width // fsdp_size, units), bf),
            S((3, levels, width // 2, units), bf),
            S((1, width), f32), S((8, 128), f32), S((heads, 1, length), f32), S((heads, hd, hd), f32), S((heads, 1, hd), f32), S((8, width), f32),
        ],
        scratch_shapes=[
            V((3, width, units), bf),
            V(grid_rows + (width,), bf),
            V((tp_size, c_rows, width), bf),
            V(flat_rows[1:] + (units,), bf), V(flat_rows[1:] + (units,), bf), V(flat_rows[1:] + (units,), bf),
            V(grid_rows + (width,), bf),
            V((chunks, tp_size - 1, c_rows, width), bf), V((chunks, tp_size - 1, c_rows, width), bf),
            V((rows, width), bf),
            V((rows, width), f32), V((c_rows, width), f32),
            DMA((9 + chunks,)), DMA((6,)), DMA((3 + tp_size + tp_size * chunks,)),
            DMA((2 * tp_size,)), DMA((8 + tp_size,)),
            DMA((3, levels, 2, fsdp_size // 2)), DMA((3, levels, 2, fsdp_size // 2)),
            DMA((levels,)), DMA((levels,)),
            DMA((4, 2, fsdp_size)), DMA((4, 2, fsdp_size)),
            DMA((1 + 6 * chunks, 2, tp_size - 1)), DMA((1 + 6 * chunks, 2, tp_size - 1)),
        ],
        compiler_params=pltpu.CompilerParams(
            collective_id=collective_id, has_side_effects=True, vmem_limit_bytes=60 * 2**20
        ),
        name="layer_kernel",
    )(
        bounds, gains, live, memory, norm.reshape(heads, 1, hd), jnp.broadcast_to(gate[:, None, None], (heads, 1, hd)),
        stream, cot, *attn_weights, *mlp_weights,
    )


def contract_rows(first_mat, second_mat):
    return lax.dot_general(
        first_mat, second_mat, (((0,), (0,)), ((), ())), preferred_element_type=jnp.float32
    )


def times_transpose(first_mat, second_mat):
    return lax.dot_general(
        first_mat, second_mat, (((1,), (1,)), ((), ())), preferred_element_type=jnp.float32
    )


def halve(terms, axis, bits):
    size = lax.axis_size(axis)
    here = lax.axis_index(axis)
    left = [1 << b for b in range(size.bit_length() - 2, -1, -1)]
    for bit in bits:
        at = left.index(bit)
        mine = lax.rem(here // bit, 2)
        kept = lax.dynamic_index_in_dim(terms, mine, at, keepdims=False)
        sent = lax.dynamic_index_in_dim(terms, 1 - mine, at, keepdims=False)
        came = lax.ppermute(sent, axis, [(i, i ^ bit) for i in range(size)])
        total = kept.astype(jnp.float32) + came.astype(jnp.float32)
        left.pop(at)
        terms = total if not left else total.astype(jnp.bfloat16)
    return terms


def scatter_blocks(grad, axis):
    size = lax.axis_size(axis)
    levels = size.bit_length() - 1
    ups = [1 << b for b in range(1, levels)]
    rows = grad.shape[0] // size
    split = grad.reshape((2,) * levels + (2, rows // 2, grad.shape[1]))
    first = halve(lax.index_in_dim(split, 0, levels, keepdims=False), axis, [1] + ups)
    second = halve(lax.index_in_dim(split, 1, levels, keepdims=False), axis, [1] + ups[::-1])
    return jnp.concatenate([first, second], axis=0)


def on_device(
    stream,
    attn_gain,
    w_query,
    w_key,
    w_value,
    w_out,
    mem_gate,
    mlp_gain,
    w_gate,
    w_up,
    w_down,
    memory,
    normalizer,
    prefix,
    valid,
    cotangent,
):
    f32, bf16 = jnp.float32, jnp.bfloat16
    len_dev, width = (stream.shape[1], stream.shape[2])
    tp_size, fsdp_size = lax.axis_size("tp"), lax.axis_size("fsdp")
    tp_here, seq_here = lax.axis_index("tp"), lax.axis_index("fsdp")
    seq_len = len_dev * tp_size
    heads_here = mem_gate.shape[0]
    prefix_len = prefix[seq_here]
    valid_len = valid[seq_here]
    stream, cotangent = stream[0], cotangent[0]

    shard = width // fsdp_size
    gains = jnp.zeros((8, width), f32)
    gains = lax.dynamic_update_slice(
        gains, jnp.stack([attn_gain, mlp_gain]).astype(f32), (0, seq_here * shard)
    )
    bounds = jnp.stack([prefix_len, valid_len])
    local_position = tp_here * len_dev + jnp.arange(len_dev, dtype=jnp.int32)
    live_here = (local_position < valid_len).astype(f32)[:, None]
    (
        _, attn_full, flat_one, qkv_rows, combined, local_mix, _, _, _, _, _, _,
        stream_out, grad_middle, branch_low, kept, landed, gain_two_terms, stats, log_total, memory_next, normalizer_next, gains,
    ) = whole_layer(
        bounds, gains, live_here, memory[0], normalizer[0], mem_gate, stream, cotangent,
        (w_query, w_key, w_value, w_out), (w_gate, w_up, w_down), tp_size, fsdp_size, 1,
    )
    inner = w_query.shape[1]
    combined = combined.reshape(seq_len, inner)
    branch_low = branch_low.reshape(seq_len, width)
    query_full, key_full, value_full, out_full = (attn_full[:, p * inner : (p + 1) * inner] for p in range(4))

    gate_grad, up_grad, down_grad = (
        kept[g].astype(f32) + landed[g, -1, :shard].astype(f32) for g in range(3)
    )
    out_grad = scatter_blocks(contract_rows(branch_low, combined).astype(bf16), "fsdp")
    grad_combined = jnp.dot(branch_low, out_full, preferred_element_type=f32)
    query_low, key_low, value_low, grad_memory, grad_normalizer, gate_parts = attend_back(
        bounds, qkv_rows, grad_combined, local_mix, log_total,
        memory[0], normalizer[0], mem_gate,
    )
    one_terms = (
        times_transpose(query_low, query_full)
        + times_transpose(key_low, key_full)
        + times_transpose(value_low, value_full)
    )
    grad_normed_one = lax.psum_scatter(one_terms.astype(bf16), "tp", scatter_dimension=0, tiled=True).astype(f32)
    query_grad = scatter_blocks(contract_rows(flat_one, query_low).astype(bf16), "fsdp")
    key_grad = scatter_blocks(contract_rows(flat_one, key_low).astype(bf16), "fsdp")
    value_grad = scatter_blocks(contract_rows(flat_one, value_low).astype(bf16), "fsdp")

    stream_f = stream.astype(f32)
    inverse = lax.rsqrt(jnp.mean(stream_f * stream_f, axis=-1, keepdims=True) + norm_eps)
    unit = stream_f * inverse
    gain_one_terms = jnp.sum(grad_normed_one * unit, axis=0)
    scaled = grad_normed_one * gains[0]
    stream_grad = grad_middle + inverse * (scaled - unit * jnp.mean(scaled * unit, axis=-1, keepdims=True))

    gate_terms = jnp.zeros((tp_size, heads_here), f32).at[tp_here].set(jnp.sum(gate_parts, axis=(1, 2)))
    stat_terms = jnp.zeros((fsdp_size, 3), f32).at[seq_here].set(jnp.stack([stats[1, 0], stats[0, 0], stats[2, 0]]))
    joined = lax.psum(
        jnp.concatenate([gain_one_terms, gain_two_terms[0], gate_terms.reshape(-1), stat_terms.reshape(-1)]),
        ("fsdp", "tp"),
    )
    gain_one_grad = lax.dynamic_slice_in_dim(joined[:width], seq_here * shard, shard)
    gain_two_grad = lax.dynamic_slice_in_dim(joined[width : 2 * width], seq_here * shard, shard)
    gates = joined[2 * width : 2 * width + tp_size * heads_here].reshape(tp_size, heads_here)
    sums = joined[2 * width + tp_size * heads_here :].reshape(fsdp_size, 3)
    gate_grad_logit = lax.dynamic_index_in_dim(gates, tp_here, 0, keepdims=False)
    stat_sums = lax.dynamic_index_in_dim(sums, seq_here, 0)
    token_count = valid_len.astype(f32) * width
    rms_stats = jnp.sqrt(stat_sums / token_count + rms_eps)
    return (
        stream_out[None],
        stream_grad[None],
        gain_one_grad,
        query_grad,
        key_grad,
        value_grad,
        out_grad,
        gate_grad_logit,
        gain_two_grad,
        gate_grad,
        up_grad,
        down_grad,
        memory_next[None],
        normalizer_next[:, 0][None],
        grad_memory[None],
        grad_normalizer[:, 0][None],
        rms_stats,
    )


def solution(mesh):
    placed = (
        P("fsdp", "tp", None),
        P("fsdp"),
        P("fsdp", "tp"),
        P("fsdp", "tp"),
        P("fsdp", "tp"),
        P("fsdp", "tp"),
        P("tp"),
        P("fsdp"),
        P("fsdp", "tp"),
        P("fsdp", "tp"),
        P("fsdp", "tp"),
        P("fsdp", "tp", None, None),
        P("fsdp", "tp", None),
        P(),
        P(),
        P("fsdp", "tp", None),
    )
    return jax.shard_map(
        on_device,
        mesh=mesh,
        in_specs=placed,
        out_specs=(
            P("fsdp", "tp", None),
            P("fsdp", "tp", None),
            P("fsdp"),
            P("fsdp", "tp"),
            P("fsdp", "tp"),
            P("fsdp", "tp"),
            P("fsdp", "tp"),
            P("tp"),
            P("fsdp"),
            P("fsdp", "tp"),
            P("fsdp", "tp"),
            P("fsdp", "tp"),
            P("fsdp", "tp", None, None),
            P("fsdp", "tp", None),
            P("fsdp", "tp", None, None),
            P("fsdp", "tp", None),
            P("fsdp", None),
        ),
        check_vma=False,
    )
```

time: 932 us -> 809 us (0.87)
  Pallas kernels: 303 us -> 576 us
  waiting for transfers between devices: 220 us -> 52.5 us
  starting transfers between devices: 102 us -> 18.9 us
  local copies, waits for them, and re-layouts: 105 us -> 32 us
  matrix products: 65.5 us -> 32.1 us
  other arithmetic: 64 us -> 30.9 us
    pallas_call x3 -> x1, Pallas kernels: 288 us -> 562 us  [whole_layer(): pl.pallas_call(functools.partial(layer_kernel, chunks=chunks, tp_size=tp_...]
    ppermute x37 -> x0, waiting for transfers between devices: 193 us -> none  [the longest x9 125 us: ring_gather(): lax.ppermute(moving, axis, [(i, (i + 1) % size) for i in range(size)])]
    ppermute x37 -> x0, starting transfers between devices: 67.3 us -> none  [the longest x9 52 us: ring_gather(): lax.ppermute(moving, axis, [(i, (i + 1) % size) for i in range(size)])]
    dot_general x7 -> x4, matrix products: 42.8 us -> 9.72 us  [contract_rows(): lax.dot_general(first_mat, second_mat, (((0,), (0,)), ((), ())), preferre...]
    unnamed x231 -> x65, local copies, waits for them, and re-layouts: 32.5 us -> 9.56 us
    reduce_scatter x1, waiting for transfers between devices: 14.1 us -> 35.7 us  [on_device(): lax.psum_scatter(one_terms.astype(bf16), 'tp', scatter_dimension=0, tiled...]
    squeeze x35 -> x20, local copies, waits for them, and re-layouts: 21.7 us -> 3.73 us  [halve(): sent = lax.dynamic_index_in_dim(terms, 1 - mine, at, keepdims=False)]
    ppermute x42 -> x24, starting transfers between devices: 34.9 us -> 18.8 us  [halve(): came = lax.ppermute(sent, axis, [(i, i ^ bit) for i in range(size)])]
  transfers between devices with their start and end apart: 81 -> 25, of which waited for: 23 -> 12; matrix products, arithmetic and copies ran while one was open for 18% -> 7% of each run, Pallas kernels for 4% -> 0%
where the time goes in v3:
time: 809 us; the launch traced here: 800 us
  Pallas kernels  576 us (71%)
  waiting for transfers between devices  52.5 us (6%)
  blocking collectives  40.9 us (5%)
  matrix products  32.1 us (4%)
  local copies, waits for them, and re-layouts  32 us (4%)
  other arithmetic  30.9 us (4%)
  starting transfers between devices  18.9 us (2%)
  between operations  15.8 us (2%)
    pallas_call x1, Pallas kernels, whole_layer(): pl.pallas_call(functools.partial(layer_kernel, chunks=chunks, tp_size=tp_...  562 us
    psum x1, blocking collectives, on_device(): lax.psum(jnp.concatenate([gain_one_terms, gain_two_terms[0], gate_terms.r...  40.9 us
    reduce_scatter x1, waiting for transfers between devices, on_device(): lax.psum_scatter(one_terms.astype(bf16), 'tp', scatter_dimension=0, tiled...  35.7 us
    ppermute x24, starting transfers between devices, halve(): came = lax.ppermute(sent, axis, [(i, i ^ bit) for i in range(size)])  18.8 us
    dot_general x3, matrix products, times_transpose(): lax.dot_general(first_mat, second_mat, (((1,), (1,)), ((), ())), preferre...  17.2 us
    ppermute x24, waiting for transfers between devices, halve(): came = lax.ppermute(sent, axis, [(i, i ^ bit) for i in range(size)])  16.8 us
  transfers between devices with their start and end apart: 25, of which 12 were waited for; matrix products, arithmetic and copies ran while one was open for 7% of the time, Pallas kernels for 0%

profile of v3, /device:TPU:0, one launch (start us, length us, event | category | flops | bytes accessed | tf_op | source)
XLA Modules:
  0.0 799.6 jit_solution(17469755464301779520)
XLA Ops:
  11.0 1.9 pad_add_fusion.2.bounds
  15.6 561.5 %layer_kernel.1 = (bf16[3,2048,2048]{2,1,0:T(8,128)(2,1)}, bf16[2048,2048]{1,0:T(8,128)(2,1)}, bf16[1024,2048]{1,0:T(8,128)(2,1)}, bf16[1024,1536]{1,0:T(8,128)(...) custom-call(s32[2]{0:T(128)} %pad_add_fusion.2.bounds, ...), custom_call_target="tpu_custom_call" | custom-call | tf_op jit(solution)/shard_map/layer_kernel/pallas_call | solution.py:949
  577.2 5.3 fusion.14.gc_ref
  582.5 14.8 %attend_backward.1 = (bf16[1024,512]{1,0:T(8,128)(2,1)S(1)}, bf16[1024,512]{1,0:T(8,128)(2,1)S(1)}, bf16[1024,512]{1,0:T(8,128)(2,1)S(1)}, f32[4,128,128]{2,1,0:...) custom-call(s32[2]{0:T(128)S(1)} %copy-done.4, bf16[1024,1536]{1,0:T(8,128)(2,1)} %get-tuple-element.65.q_ref.k_ref.v_ref, ...), custom_call_target="tpu_custom_call" | custom-call | tf_op jit(solution)/shard_map/attend_backward/pallas_call | solution.py:113
  597.3 2.5 convolution_convert_fusion
  602.8 2.4 bitcast_convert_fusion
  606.7 2.8 constant_dynamic-slice_fusion.3
  613.9 2.4 convolution_convert_fusion.1
  617.4 2.4 convolution_convert_fusion.2
  623.0 2.7 fusion.10
  625.7 5.7 fusion.12
  631.3 8.8 %add_convert_fusion = bf16[1024,2048]{1,0:T(8,128)(2,1)} fusion(f32[1024,2048]{1,0:T(8,128)} %fusion.12, f32[1024,2048]{1,0:T(8,128)S(1)} %fusion.10, bf16[1024,512]{1,0:T(8,128)(2,1)S(1)} %get-tuple-element.72, bf16[2048,2048]{1,0:T(8,128)(2,1)} %get-tuple-element.67), kind=kOutput, calls=%fused_computation | convolution fusion | flops 2153775104 | bytes 24117248 | tf_op jit(solution)/shard_map/dot_general | solution.py:1004
  644.6 6.1 convert_add_fusion
  652.3 2.7 broadcast_select_fusion
  655.6 1.9 copy.106
  674.1 4.5 collective-permute-done.13
  682.1 2.1 collective-permute-done.7
  687.7 2.1 collective-permute-done.1
  693.3 1.6 collective-permute-done.20
  698.9 1.7 collective-permute-done.8
  704.9 35.7 %reduce-scatter.2.cloned.1.call-done = bf16[256,2048]{1,0:T(8,128)(2,1)} async-done(((bf16[1024,2048]{1,0:T(8,128)(2,1)}), bf16[256,2048]{1,0:T(8,128)(2,1)}) %reduce-scatter.2.cloned.1.call-update) | async-done | bytes 1048592 | tf_op jit(solution)/shard_map/reduce_scatter | solution.py:1098
  740.6 2.2 fusion.8
  742.8 40.9 %psum.7 = f32[4136]{0:T(1024)S(1)} all-reduce(f32[4136]{0:T(1024)S(1)} %concatenate.30), channel_id=1, replica_groups=mesh['fsdp'=8,'tp'=4] {'fsdp','tp'}, use_global_device_ids=true, to_apply=%region_7.8 | all-reduce | flops 4136 | bytes 33088 | tf_op jit(solution)/shard_map/psum | solution.py:1112
  786.3 3.6 fusion.5
  (195 shorter events, 65.5 us)
Async XLA Ops:
  7.2 733.4 %reduce-scatter.2.cloned.1.call-start = ((), (), s32[]{:S(2)}) async-start(), calls=%async_computation.1 | async-start | bytes 5242880 | tf_op jit(solution)/shard_map/reduce_scatter | solution.py:1098
  610.4 48.2 %collective-permute-start.18 = (bf16[2,2,128,512]{3,2,0,1:T(8,128)(2,1)}, bf16[2,2,128,512]{3,2,0,1:T(8,128)(2,1)}, u32[]{:S(2)}, u32[]{:S(2)}) collective-permute-start(bf16[2,2,128,512]{3,2,0,1:T(8,128)(2,1)} %bitcast.207), channel_id=1, source_target_pairs={{0,4},{4,0},{8,12},{12,8},{16,20},{20,16},{24,28},{28,24},{1,5},{5... | collective-permute-start | bytes 1572872 | tf_op jit(solution)/shard_map/ppermute | solution.py:1018
  611.2 49.3 %collective-permute-start.21 = (bf16[2,2,128,512]{3,2,1,0:T(8,128)(2,1)}, bf16[2,2,128,512]{3,2,1,0:T(8,128)(2,1)}, u32[]{:S(2)}, u32[]{:S(2)}) collective-permute-start(bf16[2,2,128,512]{3,2,1,0:T(8,128)(2,1)} %dynamic-slice_bitcast_fusion), channel_id=1, source_target_pairs={{0,4},{4,0},{8,12},{12,8},{16,20},{20,16},{24,28},{28,24},{1,5},{5... | collective-permute-start | bytes 1572872 | tf_op jit(solution)/shard_map/ppermute | solution.py:1018
  612.6 49.6 %collective-permute-start.12 = (bf16[2,2,128,512]{3,2,0,1:T(8,128)(2,1)}, bf16[2,2,128,512]{3,2,0,1:T(8,128)(2,1)}, u32[]{:S(2)}, u32[]{:S(2)}) collective-permute-start(bf16[2,2,128,512]{3,2,0,1:T(8,128)(2,1)} %bitcast.208), channel_id=1, source_target_pairs={{0,4},{4,0},{8,12},{12,8},{16,20},{20,16},{24,28},{28,24},{1,5},{5... | collective-permute-start | bytes 1572872 | tf_op jit(solution)/shard_map/ppermute | solution.py:1018
  613.4 52.6 %collective-permute-start.15 = (bf16[2,2,128,512]{3,2,1,0:T(8,128)(2,1)}, bf16[2,2,128,512]{3,2,1,0:T(8,128)(2,1)}, u32[]{:S(2)}, u32[]{:S(2)}) collective-permute-start(bf16[2,2,128,512]{3,2,1,0:T(8,128)(2,1)} %dynamic-slice_bitcast_fusion.1), channel_id=1, source_target_pairs={{0,4},{4,0},{8,12},{12,8},{16,20},{20,16},{24,28},{28,24},{1,5},{5... | collective-permute-start | bytes 1572872 | tf_op jit(solution)/shard_map/ppermute | solution.py:1018
  623.0 40.8 %collective-permute-start.6 = (bf16[2,2,128,512]{3,2,0,1:T(8,128)(2,1)}, bf16[2,2,128,512]{3,2,0,1:T(8,128)(2,1)}, u32[]{:S(2)}, u32[]{:S(2)}) collective-permute-start(bf16[2,2,128,512]{3,2,0,1:T(8,128)(2,1)} %bitcast.209), channel_id=1, source_target_pairs={{0,4},{4,0},{8,12},{12,8},{16,20},{20,16},{24,28},{28,24},{1,5},{5... | collective-permute-start | bytes 1572872 | tf_op jit(solution)/shard_map/ppermute | solution.py:1018
  658.5 9.9 %collective-permute-start.9 = (bf16[2,2,128,512]{3,2,1,0:T(8,128)(2,1)}, bf16[2,2,128,512]{3,2,1,0:T(8,128)(2,1)S(1)}, u32[]{:S(2)}, u32[]{:S(2)}) collective-permute-start(bf16[2,2,128,512]{3,2,1,0:T(8,128)(2,1)} %dynamic-slice_bitcast_fusion.2), channel_id=1, source_target_pairs={{0,4},{4,0},{8,12},{12,8},{16,20},{20,16},{24,28},{28,24},{1,5},{5... | collective-permute-start | bytes 1572872 | tf_op jit(solution)/shard_map/ppermute | solution.py:1018
  660.5 10.4 %collective-permute-start = (bf16[2,2,128,512]{3,2,0,1:T(8,128)(2,1)}, bf16[2,2,128,512]{3,2,0,1:T(8,128)(2,1)S(1)}, u32[]{:S(2)}, u32[]{:S(2)}) collective-permute-start(bf16[2,2,128,512]{3,2,0,1:T(8,128)(2,1)} %bitcast.224), channel_id=1, source_target_pairs={{0,4},{4,0},{8,12},{12,8},{16,20},{20,16},{24,28},{28,24},{1,5},{5... | collective-permute-start | bytes 1572872 | tf_op jit(solution)/shard_map/ppermute | solution.py:1018
  662.1 7.5 collective-permute-start.3
  663.8 9.2 %collective-permute-start.19 = (bf16[2,128,512]{2,1,0:T(8,128)(2,1)S(1)}, bf16[2,128,512]{2,1,0:T(8,128)(2,1)S(1)}, u32[]{:S(2)}, u32[]{:S(2)}) collective-permute-start(bf16[2,128,512]{2,1,0:T(8,128)(2,1)S(1)} %dynamic-slice_bitcast_fusion.5), channel_id=1, source_target_pairs={{0,8},{4,12},{8,0},{12,4},{16,24},{20,28},{24,16},{28,20},{1,9},{5... | collective-permute-start | bytes 786440 | tf_op jit(solution)/shard_map/ppermute | solution.py:1018
  666.1 13.7 %collective-permute-start.22 = (bf16[2,128,512]{2,1,0:T(8,128)(2,1)S(1)}, bf16[2,128,512]{2,1,0:T(8,128)(2,1)S(1)}, u32[]{:S(2)}, u32[]{:S(2)}) collective-permute-start(bf16[2,128,512]{2,1,0:T(8,128)(2,1)S(1)} %dynamic-slice_bitcast_fusion.4), channel_id=1, source_target_pairs={{0,16},{4,20},{8,24},{12,28},{16,0},{20,4},{24,8},{28,12},{1,17},{... | collective-permute-start | bytes 786440 | tf_op jit(solution)/shard_map/ppermute | solution.py:1018
  668.5 10.2 %collective-permute-start.13 = (bf16[2,128,512]{2,1,0:T(8,128)(2,1)S(1)}, bf16[2,128,512]{2,1,0:T(8,128)(2,1)S(1)}, u32[]{:S(2)}, u32[]{:S(2)}) collective-permute-start(bf16[2,128,512]{2,1,0:T(8,128)(2,1)S(1)} %dynamic-slice_bitcast_fusion.7), channel_id=1, source_target_pairs={{0,8},{4,12},{8,0},{12,4},{16,24},{20,28},{24,16},{28,20},{1,9},{5... | collective-permute-start | bytes 786440 | tf_op jit(solution)/shard_map/ppermute | solution.py:1018
  669.7 11.2 %collective-permute-start.16 = (bf16[2,128,512]{2,1,0:T(8,128)(2,1)S(1)}, bf16[2,128,512]{2,1,0:T(8,128)(2,1)S(1)}, u32[]{:S(2)}, u32[]{:S(2)}) collective-permute-start(bf16[2,128,512]{2,1,0:T(8,128)(2,1)S(1)} %dynamic-slice_bitcast_fusion.6), channel_id=1, source_target_pairs={{0,16},{4,20},{8,24},{12,28},{16,0},{20,4},{24,8},{28,12},{1,17},{... | collective-permute-start | bytes 786440 | tf_op jit(solution)/shard_map/ppermute | solution.py:1018
  670.9 13.3 %collective-permute-start.7 = (bf16[2,128,512]{2,1,0:T(8,128)(2,1)S(1)}, bf16[2,128,512]{2,1,0:T(8,128)(2,1)S(1)}, u32[]{:S(2)}, u32[]{:S(2)}) collective-permute-start(bf16[2,128,512]{2,1,0:T(8,128)(2,1)S(1)} %dynamic-slice_bitcast_fusion.9), channel_id=1, source_target_pairs={{0,8},{4,12},{8,0},{12,4},{16,24},{20,28},{24,16},{28,20},{1,9},{5... | collective-permute-start | bytes 786440 | tf_op jit(solution)/shard_map/ppermute | solution.py:1018
  673.0 13.5 %collective-permute-start.10 = (bf16[2,128,512]{2,1,0:T(8,128)(2,1)S(1)}, bf16[2,128,512]{2,1,0:T(8,128)(2,1)S(1)}, u32[]{:S(2)}, u32[]{:S(2)}) collective-permute-start(bf16[2,128,512]{2,1,0:T(8,128)(2,1)S(1)} %dynamic-slice_bitcast_fusion.8), channel_id=1, source_target_pairs={{0,16},{4,20},{8,24},{12,28},{16,0},{20,4},{24,8},{28,12},{1,17},{... | collective-permute-start | bytes 786440 | tf_op jit(solution)/shard_map/ppermute | solution.py:1018
  678.7 11.2 %collective-permute-start.1 = (bf16[2,128,512]{2,1,0:T(8,128)(2,1)S(1)}, bf16[2,128,512]{2,1,0:T(8,128)(2,1)S(1)}, u32[]{:S(2)}, u32[]{:S(2)}) collective-permute-start(bf16[2,128,512]{2,1,0:T(8,128)(2,1)S(1)} %dynamic-slice_bitcast_fusion.11), channel_id=1, source_target_pairs={{0,8},{4,12},{8,0},{12,4},{16,24},{20,28},{24,16},{28,20},{1,9},{5... | collective-permute-start | bytes 786440 | tf_op jit(solution)/shard_map/ppermute | solution.py:1018
  679.7 12.4 %collective-permute-start.4 = (bf16[2,128,512]{2,1,0:T(8,128)(2,1)S(1)}, bf16[2,128,512]{2,1,0:T(8,128)(2,1)S(1)}, u32[]{:S(2)}, u32[]{:S(2)}) collective-permute-start(bf16[2,128,512]{2,1,0:T(8,128)(2,1)S(1)} %dynamic-slice_bitcast_fusion.10), channel_id=1, source_target_pairs={{0,16},{4,20},{8,24},{12,28},{16,0},{20,4},{24,8},{28,12},{1,17},{... | collective-permute-start | bytes 786440 | tf_op jit(solution)/shard_map/ppermute | solution.py:1018
  680.9 14.0 %collective-permute-start.20 = (bf16[128,512]{1,0:T(8,128)(2,1)S(1)}, bf16[128,512]{1,0:T(8,128)(2,1)S(1)}, u32[]{:S(2)}, u32[]{:S(2)}) collective-permute-start(bf16[128,512]{1,0:T(8,128)(2,1)S(1)} %dynamic-slice_bitcast_fusion.13), channel_id=1, source_target_pairs={{0,16},{4,20},{8,24},{12,28},{16,0},{20,4},{24,8},{28,12},{1,17},{... | collective-permute-start | bytes 393224 | tf_op jit(solution)/shard_map/ppermute | solution.py:1018
  684.3 11.8 %collective-permute-start.23 = (bf16[128,512]{1,0:T(8,128)(2,1)S(1)}, bf16[128,512]{1,0:T(8,128)(2,1)S(1)}, u32[]{:S(2)}, u32[]{:S(2)}) collective-permute-start(bf16[128,512]{1,0:T(8,128)(2,1)S(1)} %dynamic-slice_bitcast_fusion.12), channel_id=1, source_target_pairs={{0,8},{4,12},{8,0},{12,4},{16,24},{20,28},{24,16},{28,20},{1,9},{5... | collective-permute-start | bytes 393224 | tf_op jit(solution)/shard_map/ppermute | solution.py:1018
  686.5 11.2 %collective-permute-start.14 = (bf16[128,512]{1,0:T(8,128)(2,1)S(1)}, bf16[128,512]{1,0:T(8,128)(2,1)S(1)}, u32[]{:S(2)}, u32[]{:S(2)}) collective-permute-start(bf16[128,512]{1,0:T(8,128)(2,1)S(1)} %dynamic-slice_bitcast_fusion.15), channel_id=1, source_target_pairs={{0,16},{4,20},{8,24},{12,28},{16,0},{20,4},{24,8},{28,12},{1,17},{... | collective-permute-start | bytes 393224 | tf_op jit(solution)/shard_map/ppermute | solution.py:1018
  689.9 9.0 %collective-permute-start.17 = (bf16[128,512]{1,0:T(8,128)(2,1)S(1)}, bf16[128,512]{1,0:T(8,128)(2,1)S(1)}, u32[]{:S(2)}, u32[]{:S(2)}) collective-permute-start(bf16[128,512]{1,0:T(8,128)(2,1)S(1)} %dynamic-slice_bitcast_fusion.14), channel_id=1, source_target_pairs={{0,8},{4,12},{8,0},{12,4},{16,24},{20,28},{24,16},{28,20},{1,9},{5... | collective-permute-start | bytes 393224 | tf_op jit(solution)/shard_map/ppermute | solution.py:1018
  692.2 8.4 %collective-permute-start.8 = (bf16[128,512]{1,0:T(8,128)(2,1)S(1)}, bf16[128,512]{1,0:T(8,128)(2,1)S(1)}, u32[]{:S(2)}, u32[]{:S(2)}) collective-permute-start(bf16[128,512]{1,0:T(8,128)(2,1)S(1)} %dynamic-slice_bitcast_fusion.17), channel_id=1, source_target_pairs={{0,16},{4,20},{8,24},{12,28},{16,0},{20,4},{24,8},{28,12},{1,17},{... | collective-permute-start | bytes 393224 | tf_op jit(solution)/shard_map/ppermute | solution.py:1018
  696.1 6.2 collective-permute-start.2
  697.8 6.2 collective-permute-start.5
  (30 other events, 209.4 us)
Sparse Core Ops, SparseCore 0:
  640.3 100.2 reduce-scatter.1

commit v4 on v3

--- a/solution.py
+++ b/solution.py
@@ -41,85 +41,6 @@
 def key_limit(first, rows, prefix, valid):
     row = first + lax.broadcasted_iota(jnp.int32, (1, rows), 1)
     return jnp.minimum(valid - 1, jnp.maximum(row, prefix - 1))
-
-
-def backward_kernel(bounds, q_ref, k_ref, v_ref, gc_ref, mix_ref, lse_ref, mem_ref, norm_ref, gate_ref, dq_ref, dk_ref, dv_ref, dmem_ref, dnorm_ref, dgate_ref, dk_acc, dv_acc, *, block):
-    keys, hd = k_ref.shape
-    prefix, valid = bounds[0], bounds[1]
-    scale = hd ** -0.5
-    gate = jax.nn.sigmoid(gate_ref[0])
-    memory = mem_ref[0]
-    norm = norm_ref[0]
-    dmem = jnp.zeros((hd, hd), jnp.float32)
-    dnorm = jnp.zeros((1, hd), jnp.float32)
-    dgate = jnp.zeros((1, hd), jnp.float32)
-    for first in range(keys - block, -1, -block):
-        reach = key_reach(first, block, keys)
-        rows = slice(first, first + block)
-        q = q_ref[rows, :]
-        gc = gc_ref[rows, :].astype(jnp.float32)
-        mixed = mix_ref[rows, :]
-        qm = mapped(q.astype(jnp.float32))
-        inverse = 1.0 / jnp.sum(qm * norm, axis=-1, keepdims=True)
-        retrieved = dot_three(qm, memory, NN) * inverse
-        dgate = dgate + jnp.sum(gc * (retrieved - mixed), axis=0, keepdims=True)
-        gnum = gate * gc * inverse
-        gden = -jnp.sum(gnum * retrieved, axis=-1, keepdims=True)
-        dmem = dmem + dot_three(qm, gnum, TN)
-        dnorm = dnorm + jnp.sum(gden * qm, axis=0, keepdims=True)
-        dq_mem = (dot_three(gnum, memory, NT) + gden * norm) * jnp.minimum(qm, 1.0)
-        low = ((1.0 - gate) * gc).astype(jnp.bfloat16)
-        delta = jnp.sum((low.astype(jnp.float32) * mixed).T, axis=0, keepdims=True)
-        s = dot32(k_ref[:reach, :], q, NT) * (scale * LOG2E)
-        limit = key_limit(first, block, prefix, valid)
-        s = jnp.where(lax.broadcasted_iota(jnp.int32, s.shape, 0) <= limit, s - lse_ref[0, :, rows], NEG)
-        p = jnp.exp2(s)
-        gp = dot32(v_ref[:reach, :], low, NT)
-        gs = (p * (gp - delta)).astype(jnp.bfloat16)
-        dv = dot32(p.astype(jnp.bfloat16), low, NN)
-        dk = dot32(gs, q, NN)
-        if first == keys - block:
-            dv_acc[...] = dv
-            dk_acc[...] = dk
-        else:
-            dv_acc[:reach, :] += dv
-            dk_acc[:reach, :] += dk
-        dq = dot32(k_ref[:reach, :], gs, TN).T * scale
-        dq_ref[rows, :] = (dq + dq_mem).astype(jnp.bfloat16)
-    dk_ref[...] = (dk_acc[...] * scale).astype(jnp.bfloat16)
-    dv_ref[...] = dv_acc[...].astype(jnp.bfloat16)
-    dmem_ref[0] = dmem
-    dnorm_ref[0] = dnorm
-    dgate_ref[0] = dgate * (gate * (1.0 - gate))
-
-
-def head_specs(keys, hd):
-    rows = pl.BlockSpec((keys, hd), lambda h: (0, h))
-    square = pl.BlockSpec((1, hd, hd), lambda h: (h, 0, 0))
-    line = pl.BlockSpec((1, 1, hd), lambda h: (h, 0, 0))
-    long = pl.BlockSpec((1, 1, keys), lambda h: (h, 0, 0))
-    return rows, square, line, long
-
-
-def attend_back(bounds, qkv, gc, mix, lse, memory, norm, gate, block=256):
-    keys = qkv.shape[0]
-    heads, hd = memory.shape[:2]
-    rows, square, line, long = head_specs(keys, hd)
-    key_rows = pl.BlockSpec((keys, hd), lambda h: (0, heads + h))
-    value_rows = pl.BlockSpec((keys, hd), lambda h: (0, 2 * heads + h))
-    f32 = jnp.float32
-    S = jax.ShapeDtypeStruct
-    low = S(gc.shape, jnp.bfloat16)
-    return pl.pallas_call(
-        functools.partial(backward_kernel, block=block),
-        grid=(heads,),
-        in_specs=[pl.BlockSpec(memory_space=pltpu.SMEM), rows, key_rows, value_rows, rows, rows, long, square, line, line],
-        out_specs=[rows, rows, rows, square, line, line],
-        out_shape=[low, low, low, S((heads, hd, hd), f32), S((heads, 1, hd), f32), S((heads, 1, hd), f32)],
-        scratch_shapes=[pltpu.VMEM((keys, hd), f32), pltpu.VMEM((keys, hd), f32)],
-        compiler_params=pltpu.CompilerParams(vmem_limit_bytes=48 * 2**20),
-        name="attend_backward",
-    )(bounds, qkv, qkv, qkv, gc, mix, lse, memory, norm.reshape(heads, 1, hd), jnp.broadcast_to(gate[:, None, None], (heads, 1, hd)))
 
 
 norm_eps = 1e-06
@@ -308,7 +229,7 @@
     bounds, gain_in, live_ref, mem_ref, norm_ref, gate_ref,
     stream_hbm, cot_hbm, wq_hbm, wk_hbm, wv_hbm, wo_hbm, wg_hbm, wu_hbm, wd_hbm,
     mlp_hbm, attn_out, one_out, qkv_out, comb_out, mix_out, cot_all, x_out, hid_out, gl_out, ul_out, terms_hbm,
-    result_out, gmid_out, branch_out, kept_out, land,
+    result_out, gmid_out, branch_out, kept_out, land, all_out, mid_out, to_send,
     ggain_ref, stat_ref, lse_ref, memo_ref, normo_ref, gain,
     w_three, x, cot, hid, gl, ul, part, land_r, land_l, stream, mid, total,
     own_sem, load_sem, out_sem, term_sem, grad_sem, trade_send, trade_recv, gain_send, gain_recv, cube_send, cube_recv, line_send, line_recv,
@@ -472,6 +393,8 @@
         arrived_pair(k, both)
     one_save = pltpu.make_async_copy(flat_one.at[0:length, :], one_out, out_sem.at[1])
     one_save.start()
+    all_save = pltpu.make_async_copy(flat_one.at[length : 2 * length, :], all_out, own_sem.at[4])
+    all_save.start()
     qkv_save = pltpu.make_async_copy(qkv.at[0:length, 0 : 3 * inner], qkv_out, out_sem.at[2])
     qkv_save.start()
     for stage in range(2, cube.levels):
@@ -625,6 +548,7 @@
     push(2, cube.levels)
     push(3, 1)
     one_save.wait()
+    all_save.wait()
     qkv_save.wait()
     up_load = pltpu.make_async_copy(mlp_hbm.at[1], w_three.at[1], load_sem.at[1])
     up_load.start()
@@ -711,7 +635,7 @@
         stat_ref[1:2, :] += jnp.sum(jnp.sum(result * result, axis=-1, keepdims=True) * live, axis=0, keepdims=True)
         stat_ref[2:3, :] += jnp.sum(jnp.sum(branch * branch, axis=-1, keepdims=True) * live, axis=0, keepdims=True)
         part[c, t] = result.astype(bf16)
-        send_out("result", c, part.at[c, t], rows_of(result_out, c), 6)
+        send_out("result", c, part.at[c, t], result_out, 6)
         outs["result", c].wait()
 
     def during(*steps):
@@ -807,6 +731,12 @@
             flat_w[mine, :] = (flat_w[mine, :].astype(f32) + flat_w[came, :].astype(f32)).astype(bf16)
 
         trade_start(g, 1)
+
+    def save_last(g):
+        send_out("kept", g, flat_w.at[g * width : g * width + shard, :], kept_out.at[g], 8 + 3 * g)
+        for half in range(2):
+            row = g * width + (trade_orders[half][-1] // 2) * shard + half * half_rows
+            send_out(("last", half), g, flat_w.at[row : row + half_rows, :], to_send.at[g, half], 9 + 3 * g + half)
 
     def add_next(g, i):
         places = []
@@ -830,17 +760,18 @@
             mine = slice(g * width + place, g * width + place + half_rows)
             came = slice(2 * width + spare + place, 2 * width + spare + place + half_rows)
             flat_w[mine, :] = (flat_w[mine, :].astype(f32) + flat_w[came, :].astype(f32)).astype(bf16)
-        trade_start(g, i + 1)
-        if i + 1 == cube.levels - 1:
-            send_out("kept", g, flat_w.at[g * width : g * width + shard, :], kept_out.at[g], 8 + g)
+        if i + 1 < cube.levels - 1:
+            trade_start(g, i + 1)
+        else:
+            save_last(g)
 
     def trade_end(g):
-        for _, _, item in trades(g, cube.levels - 1):
-            item.wait_recv()
         outs["kept", g].wait()
+        for half in range(2):
+            outs[("last", half), g].wait()
 
     def trade_sent(g):
-        for i in range(1, cube.levels):
+        for i in range(1, cube.levels - 1):
             for _, _, item in trades(g, i):
                 item.wait_send()
 
@@ -892,6 +823,8 @@
     scatter(RS2, 0, 1)
     weight_grad(1)
     finish_back(1)
+    mid_save = pltpu.make_async_copy(mid, mid_out, own_sem.at[5])
+    mid_save.start()
     for k in range(3, n):
         gather(AG4, 0, k)
     send_out("branch", 0, x.at[0], branch_out.at[:, 0], 0)
@@ -899,21 +832,16 @@
         scatter(RS2, 0, k)
     add_first(0)
     gather(AG4, 1, 1)
-    start_branch(1)
     weight_grad(2)
     finish_branch(0)
+    add_first(1)
     gather(AG4, 1, 2)
-    scatter(RS2, 1, 1)
-    add_first(1)
+    add_first(2)
     for i in range(1, cube.levels - 1):
         add_next(0, i)
     for k in range(3, n):
         gather(AG4, 1, k)
     send_out("branch", 1, x.at[1], branch_out.at[:, 1], 7)
-    for k in range(2, n - 1):
-        scatter(RS2, 1, k)
-    add_first(2)
-    finish_branch(1)
     for g in (1, 2):
         for i in range(1, cube.levels - 1):
             add_next(g, i)
@@ -921,12 +849,15 @@
         trade_end(g)
         trade_sent(g)
     first_trade(2).wait_send()
+    mid_save.wait()
+    line.scatter_sent(ph(RS3, 1), *lands(1))
     for c in range(chunks):
         outs["branch", c].wait()
     for c in range(chunks):
         line.gather_sent(ph(COT, c), cot_at(c))
         line.gather_sent(ph(AG4, c), x_at(c))
-        line.scatter_sent(ph(RS2, c), *lands(c))
+        if c == 0:
+            line.scatter_sent(ph(RS2, c), *lands(c))
 
 
 def whole_layer(bounds, gains, live, memory, norm, gate, stream, cot, attn_weights, mlp_weights, tp_size, fsdp_size, collective_id, tile=512):
@@ -949,7 +880,7 @@
     return pl.pallas_call(
         functools.partial(layer_kernel, chunks=chunks, tp_size=tp_size, fsdp_size=fsdp_size, tile=tile),
         in_specs=[smem] + [vmem] * 5 + [any_space] * 9,
-        out_specs=[any_space] * 17 + [vmem] * 6,
+        out_specs=[any_space] * 20 + [vmem] * 6,
         out_shape=[
             S((3, width, units), bf),
             S((width, 4 * inner), bf),
@@ -961,11 +892,14 @@
             S(grid_rows + (width,), bf),
             S(flat_rows + (units,), bf), S(flat_rows + (units,), bf), S(flat_rows + (units,), bf),
             S(grid_rows + (width,), bf),
-            S((rows, width), bf),
+            S((rows // chunks, width), bf),
             S((rows, width), f32),
             S((tp_size, chunks, c_rows, width), bf),
             S((3, width // fsdp_size, units), bf),
-            S((3, levels, width // 2, units), bf),
+            S((3, levels - 1, width // 2, units), bf),
+            S((length, width), bf),
+            S((rows, width), f32),
+            S((3, 2, width // fsdp_size // 2, units), bf),
             S((1, width), f32), S((8, 128), f32), S((heads, 1, length), f32), S((heads, hd, hd), f32), S((heads, 1, hd), f32), S((8, width), f32),
         ],
         scratch_shapes=[
@@ -977,9 +911,9 @@
             V((chunks, tp_size - 1, c_rows, width), bf), V((chunks, tp_size - 1, c_rows, width), bf),
             V((rows, width), bf),
             V((rows, width), f32), V((c_rows, width), f32),
-            DMA((9 + chunks,)), DMA((6,)), DMA((3 + tp_size + tp_size * chunks,)),
+            DMA((9 + chunks,)), DMA((6,)), DMA((max(17, 3 + tp_size + tp_size * chunks),)),
             DMA((2 * tp_size,)), DMA((8 + tp_size,)),
-            DMA((3, levels, 2, fsdp_size // 2)), DMA((3, levels, 2, fsdp_size // 2)),
+            DMA((3, levels - 1, 2, fsdp_size // 2)), DMA((3, levels - 1, 2, fsdp_size // 2)),
             DMA((levels,)), DMA((levels,)),
             DMA((4, 2, fsdp_size)), DMA((4, 2, fsdp_size)),
             DMA((1 + 6 * chunks, 2, tp_size - 1)), DMA((1 + 6 * chunks, 2, tp_size - 1)),
@@ -994,43 +928,407 @@
     )
 
 
-def contract_rows(first_mat, second_mat):
-    return lax.dot_general(
-        first_mat, second_mat, (((0,), (0,)), ((), ())), preferred_element_type=jnp.float32
+def tail_kernel(
+    bounds, gains, live_ref, mem_ref, norm_ref, gate_ref, lse_ref, gain_two_ref, stat_ref,
+    branch_hbm, attn_hbm, qkv_hbm, mix_hbm, one_hbm, comb_hbm, stream_hbm, all_hbm, gmid_hbm, mid_hbm, terms_hbm, send_hbm,
+    grad_out, result_out, land_mlp, land, kept_out,
+    dmem_ref, dnorm_ref, sums,
+    attn_w, g_ref, spare_ref, rows_ref, one_ref, qkv, dqkv, mixed_ref, gc_ref, part, land_r, land_l, dk_acc, dv_acc,
+    sums_land,
+    load_sem, out_sem, mlp_send, mlp_recv, sums_send, sums_recv, trade_send, trade_recv, line_send, line_recv,
+    *, chunks, tp_size, fsdp_size, tile,
+):
+    n = tp_size
+    bf16, f32 = jnp.bfloat16, jnp.float32
+    t, f = lax.axis_index("tp"), lax.axis_index("fsdp")
+    c_rows, width = part.shape[2], part.shape[3]
+    rows_dev = c_rows * chunks
+    length = n * rows_dev
+    heads, hd = mem_ref.shape[0], mem_ref.shape[2]
+    inner = heads * hd
+    shard = width // fsdp_size
+    half_rows = shard // 2
+    spare = width // 2
+    levels, tp_levels = fsdp_size.bit_length() - 1, n.bit_length() - 1
+    orders = [[1] + [1 << b for b in range(1, levels)], [1] + [1 << b for b in range(levels - 1, 0, -1)]]
+    line = Line(n, line_send, line_recv)
+    total, extra = gc_ref.at[0:c_rows, :], gc_ref.at[c_rows : 2 * c_rows, :]
+    count = [0]
+
+    def load(src, dst):
+        item = pltpu.make_async_copy(src, dst, load_sem.at[count[0]])
+        count[0] += 1
+        item.start()
+        return item
+
+    def peer(bit):
+        return lax.bitwise_xor(f, bit)
+
+    def place(s, c):
+        return slice(c * n * c_rows + s * c_rows, c * n * c_rows + (s + 1) * c_rows)
+
+    def origin(s, c):
+        return slice(s * rows_dev + c * c_rows, s * rows_dev + (c + 1) * c_rows)
+
+    weight_load = load(attn_hbm, attn_w)
+    branch_load = load(branch_hbm, rows_ref)
+    terms_load = load(terms_hbm, part.at[chunks])
+    comb_load = load(comb_hbm, spare_ref.at[:, 0:inner])
+    qkv_load = load(qkv_hbm, qkv)
+    mix_load = load(mix_hbm, mixed_ref)
+    one_loads = [load(one_hbm.at[origin(s, c), :], one_ref.at[place(s, c), :]) for c in range(chunks) for s in range(n)]
+
+    barrier = pltpu.get_barrier_semaphore()
+    for k in range(1, n):
+        pl.semaphore_signal(barrier, inc=1, device_id={"tp": lax.rem(t + k, n)}, device_id_type=MESH)
+    for b in range(levels):
+        pl.semaphore_signal(barrier, inc=1, device_id={"fsdp": peer(1 << b)}, device_id_type=MESH)
+    pl.semaphore_wait(barrier, n - 1 + levels)
+
+    mlp_trades = [
+        pltpu.make_async_remote_copy(
+            src_ref=send_hbm.at[g, half],
+            dst_ref=land_mlp.at[g, half],
+            send_sem=mlp_send.at[g, half],
+            recv_sem=mlp_recv.at[g, half],
+            device_id={"fsdp": peer(orders[half][-1])},
+            device_id_type=MESH,
+        )
+        for g in range(3)
+        for half in range(2)
+    ]
+    for item in mlp_trades:
+        item.start()
+
+    def lands(c):
+        return part.at[c], land_r.at[c], land_l.at[c]
+
+    def scatter(c, k):
+        line.scatter_step(c, k, *lands(c))
+
+    terms_load.wait()
+    scatter(chunks, 0)
+
+    for item in (weight_load, branch_load, comb_load):
+        item.wait()
+
+    def store_grad(j, wide, cols, terms):
+        for q in range(wide // shard):
+            mask = lax.bitwise_xor(j * (wide // shard) + q, f)
+            row = lax.rem(mask, 2) * spare + (mask // 2) * shard
+            g_ref[pl.ds(pl.multiple_of(row, shard), shard), cols] = terms[q * shard : (q + 1) * shard].astype(bf16)
+
+    wide = 256
+
+    @pl.loop(0, n)
+    def _(s):
+        rows = pl.ds(pl.multiple_of(s * rows_dev, rows_dev), rows_dev)
+        gc_ref[:, pl.ds(pl.multiple_of(s * inner, inner), inner)] = dot32(
+            rows_ref[rows, :], attn_w[:, 3 * inner : 4 * inner], NN
+        )
+
+    sums[...] = jnp.zeros_like(sums)
+    sums[1:2, :] = gain_two_ref[...]
+    lane = lax.broadcasted_iota(jnp.int32, (1, width), 1)
+    qkv_load.wait()
+    mix_load.wait()
+
+    prefix, valid = bounds[0], bounds[1]
+    scale = hd ** -0.5
+
+    @pl.loop(0, heads)
+    def _(h):
+        def lanes(group):
+            return pl.ds(pl.multiple_of(group * inner + h * hd, hd), hd)
+
+        gate = jax.nn.sigmoid(gate_ref[h])
+        memory, norm = mem_ref[h], norm_ref[h]
+        dmem_ref[h] = jnp.zeros((hd, hd), f32)
+        dnorm_ref[h] = jnp.zeros((1, hd), f32)
+        dgate = jnp.zeros((1, hd), f32)
+        for s in range(n - 1, -1, -1):
+            first = s * rows_dev
+            reach = key_reach(first, rows_dev, length)
+            rows = slice(first, first + rows_dev)
+            q = qkv[rows, lanes(0)]
+            gc = gc_ref[:, pl.ds(pl.multiple_of(s * inner + h * hd, hd), hd)]
+            mixed = mixed_ref[rows, lanes(0)]
+            qm = mapped(q.astype(f32))
+            inverse = 1.0 / jnp.sum(qm * norm, axis=-1, keepdims=True)
+            retrieved = dot_three(qm, memory, NN) * inverse
+            dgate = dgate + jnp.sum(gc * (retrieved - mixed), axis=0, keepdims=True)
+            gnum = gate * gc * inverse
+            gden = -jnp.sum(gnum * retrieved, axis=-1, keepdims=True)
+            dmem_ref[h] += dot_three(qm, gnum, TN)
+            dnorm_ref[h] += jnp.sum(gden * qm, axis=0, keepdims=True)
+            dq_mem = (dot_three(gnum, memory, NT) + gden * norm) * jnp.minimum(qm, 1.0)
+            low = ((1.0 - gate) * gc).astype(bf16)
+            delta = jnp.sum((low.astype(f32) * mixed).T, axis=0, keepdims=True)
+            keys = qkv[0:reach, lanes(1)]
+            scores = dot32(keys, q, NT) * (scale * LOG2E)
+            limit = key_limit(first, rows_dev, prefix, valid)
+            scores = jnp.where(
+                lax.broadcasted_iota(jnp.int32, scores.shape, 0) <= limit, scores - lse_ref[h, :, rows], NEG
+            )
+            probs = jnp.exp2(scores)
+            gp = dot32(qkv[0:reach, lanes(2)], low, NT)
+            gs = (probs * (gp - delta)).astype(bf16)
+            dv = dot32(probs.astype(bf16), low, NN)
+            dk = dot32(gs, q, NN)
+            if s == n - 1:
+                dv_acc[...] = dv
+                dk_acc[...] = dk
+            else:
+                dv_acc[0:reach, :] += dv
+                dk_acc[0:reach, :] += dk
+            dq = (dot32(keys, gs, TN).T * scale + dq_mem).astype(bf16)
+            for c in range(chunks):
+                dqkv[place(s, c), lanes(0)] = dq[c * c_rows : (c + 1) * c_rows]
+        for s in range(n):
+            for c in range(chunks):
+                dqkv[place(s, c), lanes(1)] = (dk_acc[origin(s, c), :] * scale).astype(bf16)
+                dqkv[place(s, c), lanes(2)] = dv_acc[origin(s, c), :].astype(bf16)
+        dgate_sum = jnp.sum(dgate * (gate * (1.0 - gate)), axis=-1, keepdims=True)
+        sums[2:3, :] += jnp.where(lane == t * heads + h, dgate_sum, 0.0)
+        for k in range(1, n - 1):
+            @pl.when(h == k)
+            def _():
+                scatter(chunks, k)
+
+    @pl.loop(0, width // wide)
+    def _(j):
+        cols = pl.ds(pl.multiple_of(j * wide, wide), wide)
+        store_grad(j, wide, slice(3 * inner, 4 * inner), dot32(rows_ref[:, cols], spare_ref[:, 0:inner], TN))
+
+    all_loads = [load(all_hbm.at[origin(s, c), :], rows_ref.at[place(s, c), :]) for c in range(chunks) for s in range(n)]
+    for item in all_loads:
+        item.wait()
+
+    for c in range(chunks):
+        here = slice(c * n * c_rows, (c + 1) * n * c_rows)
+        inverse_all = inverse_rms(rows_ref[here, :].astype(f32))
+        flat = part.at[c].reshape(n * c_rows, width)
+
+        @pl.loop(0, width // tile)
+        def _(j):
+            cols = pl.ds(pl.multiple_of(j * tile, tile), tile)
+            terms = dot32(dqkv[here, :], attn_w[cols, 0 : 3 * inner], NT)
+            flat[:, cols] = terms.astype(bf16)
+            unit = rows_ref[here, cols].astype(f32) * inverse_all
+            sums[0:1, cols] += jnp.sum(terms * unit, axis=0, keepdims=True)
+
+        scatter(c, 0)
+
+    own_rows = slice(rows_dev - c_rows, rows_dev)
+    mid_load = load(mid_hbm.at[own_rows, :], extra)
+    line.scatter_end(chunks, *lands(chunks), total)
+    mid_load.wait()
+    branch = total[...]
+    result = extra[...] + branch
+    live = live_ref[own_rows, :]
+    part[chunks, t] = result.astype(bf16)
+    result_save = pltpu.make_async_copy(part.at[chunks, t], result_out, out_sem.at[0])
+    result_save.start()
+
+    def square_sum(v):
+        return jnp.sum(jnp.sum(v * v, axis=-1, keepdims=True) * live, axis=0, keepdims=True)
+
+    stats = (stat_ref[1:2, 0:1] + square_sum(result), stat_ref[0:1, 0:1], stat_ref[2:3, 0:1] + square_sum(branch))
+    for at, value in enumerate(stats):
+        sums[3:4, :] += jnp.where(lane == 3 * f + at, value, 0.0)
+
+    def sums_step(at):
+        target = {"fsdp": peer(1 << at)} if at < levels else {"tp": lax.bitwise_xor(t, 1 << (at - levels))}
+        return pltpu.make_async_remote_copy(
+            src_ref=sums,
+            dst_ref=sums_land.at[at],
+            send_sem=sums_send.at[at],
+            recv_sem=sums_recv.at[at],
+            device_id=target,
+            device_id_type=MESH,
+        )
+
+    def sums_add(at):
+        sums_step(at).wait()
+        sums[...] += sums_land[at]
+
+    sums_step(0).start()
+
+    for item in one_loads:
+        item.wait()
+
+    @pl.loop(0, width // wide)
+    def _(j):
+        cols = pl.ds(pl.multiple_of(j * wide, wide), wide)
+        store_grad(j, wide, slice(0, 3 * inner), dot32(one_ref[:, cols], dqkv[...], TN))
+
+    first_trade = pltpu.make_async_remote_copy(
+        src_ref=g_ref.at[spare : 2 * spare, :],
+        dst_ref=land.at[0],
+        send_sem=trade_send.at[0, 0, 0],
+        recv_sem=trade_recv.at[0, 0, 0],
+        device_id={"fsdp": peer(1)},
+        device_id_type=MESH,
     )
-
-
-def times_transpose(first_mat, second_mat):
-    return lax.dot_general(
-        first_mat, second_mat, (((1,), (1,)), ((), ())), preferred_element_type=jnp.float32
+    first_trade.start()
+
+    def trades(i):
+        for half in range(2):
+            order = orders[half]
+            bit = order[i]
+            for mask in range(fsdp_size):
+                if all(mask & b == 0 for b in order[: i + 1]):
+                    there = (mask // 2) * shard + half * half_rows
+                    here = ((mask ^ bit) // 2) * shard + half * half_rows
+                    yield there, pltpu.make_async_remote_copy(
+                        src_ref=g_ref.at[here : here + half_rows, :],
+                        dst_ref=land.at[i, there : there + half_rows, :],
+                        send_sem=trade_send.at[i, half, mask // 2],
+                        recv_sem=trade_recv.at[i, half, mask // 2],
+                        device_id={"fsdp": peer(bit)},
+                        device_id_type=MESH,
+                    )
+
+    def add_rows(mine, came):
+        g_ref[mine, :] = (g_ref[mine, :].astype(f32) + spare_ref[came, :].astype(f32)).astype(bf16)
+
+    scatter(0, 1)
+    sums_add(0)
+    sums_step(1).start()
+    scatter(1, 1)
+    first_trade.wait_recv()
+    first_load = load(land.at[0], spare_ref)
+    first_load.wait()
+
+    @pl.loop(0, spare // half_rows)
+    def _(r):
+        rows = pl.ds(pl.multiple_of(r * half_rows, half_rows), half_rows)
+        add_rows(rows, rows)
+
+    for _, item in trades(1):
+        item.start()
+    for k in range(2, n - 1):
+        scatter(0, k)
+    sums_add(1)
+    sums_step(2).start()
+
+    one_gain = gains[0:1, :]
+
+    def finish(c):
+        rows = slice(c * c_rows, (c + 1) * c_rows)
+        gmid_load = load(gmid_hbm.at[rows, :], extra)
+        stream_load = load(stream_hbm.at[rows, :], part.at[chunks, 0])
+        line.scatter_end(c, *lands(c), total)
+        gmid_load.wait()
+        stream_load.wait()
+        v = part[chunks, 0].astype(f32)
+        inv = inverse_rms(v)
+        u = v * inv
+        e = total[...] * one_gain
+        total[...] = extra[...] + inv * (e - u * jnp.mean(e * u, axis=-1, keepdims=True))
+        save = pltpu.make_async_copy(total, grad_out.at[rows, :], out_sem.at[1])
+        save.start()
+        save.wait()
+
+    result_save.wait()
+    line.scatter_sent(chunks, *lands(chunks))
+    for at in range(2, levels):
+        sums_add(at)
+        sums_step(at + 1).start()
+    for k in range(2, n - 1):
+        scatter(1, k)
+    for i in range(1, levels - 1):
+        arrived = list(trades(i))
+        loads = []
+        for there, item in arrived:
+            item.wait_recv()
+            loads.append(load(land.at[i, there : there + half_rows, :], spare_ref.at[there : there + half_rows, :]))
+        for item in loads:
+            item.wait()
+        for there, _ in arrived:
+            rows = slice(there, there + half_rows)
+            add_rows(rows, rows)
+        for _, item in trades(i + 1):
+            item.start()
+    kept_save = pltpu.make_async_copy(g_ref.at[0:shard, :], kept_out, out_sem.at[2])
+    kept_save.start()
+    finish(0)
+    for at in range(levels, levels + tp_levels):
+        sums_add(at)
+        if at + 1 < levels + tp_levels:
+            sums_step(at + 1).start()
+    finish(1)
+    for _, item in trades(levels - 1):
+        item.wait_recv()
+    kept_save.wait()
+    for item in mlp_trades:
+        item.wait()
+    first_trade.wait_send()
+    for i in range(1, levels):
+        for _, item in trades(i):
+            item.wait_send()
+    for c in range(chunks):
+        line.scatter_sent(c, *lands(c))
+
+
+def whole_tail(
+    bounds, gains, live, memory, norm, gate, lse, gain_two, stat,
+    branch, attn_full, qkv, mix, flat_one, comb, stream, stream_all, gmid, mid, terms, to_send, tp_size, fsdp_size, collective_id, tile=512,
+):
+    chunks = 2
+    rows, width = stream.shape
+    length = rows * tp_size
+    c_rows = rows // chunks
+    heads, hd = memory.shape[:2]
+    inner = heads * hd
+    units = to_send.shape[-1]
+    shard = width // fsdp_size
+    levels, tp_levels = fsdp_size.bit_length() - 1, tp_size.bit_length() - 1
+    bf, f32 = jnp.bfloat16, jnp.float32
+    S, V, DMA = jax.ShapeDtypeStruct, pltpu.VMEM, pltpu.SemaphoreType.DMA
+    any_space = pl.BlockSpec(memory_space=pl.ANY)
+    vmem = pl.BlockSpec(memory_space=pltpu.VMEM)
+    smem = pl.BlockSpec(memory_space=pltpu.SMEM)
+    adds = sum(2 * (fsdp_size >> (i + 1)) for i in range(1, levels - 1))
+    loads = 6 + 2 * length // c_rows + 2 + 4 + adds
+    return pl.pallas_call(
+        functools.partial(tail_kernel, chunks=chunks, tp_size=tp_size, fsdp_size=fsdp_size, tile=tile),
+        in_specs=[smem] + [vmem] * 8 + [any_space] * 12,
+        out_specs=[any_space] * 5 + [vmem] * 3,
+        out_shape=[
+            S((rows, width), f32),
+            S((c_rows, width), bf),
+            S(to_send.shape, bf),
+            S((levels, width // 2, 4 * inner), bf),
+            S((shard, 4 * inner), bf),
+            S((heads, hd, hd), f32), S((heads, 1, hd), f32), S((8, width), f32),
+        ],
+        scratch_shapes=[
+            V((width, 4 * inner), bf),
+            V((width, 4 * inner), bf),
+            V((width // 2, 4 * inner), bf),
+            V((length, width), bf),
+            V((length, width), bf),
+            V((length, 3 * inner), bf), V((length, 3 * inner), bf),
+            V((length, inner), f32), V((rows, tp_size * inner), f32),
+            V((chunks + 1, tp_size, c_rows, width), bf),
+            V((chunks + 1, tp_size - 1, c_rows, width), bf), V((chunks + 1, tp_size - 1, c_rows, width), bf),
+            V((length, hd), f32), V((length, hd), f32),
+            V((levels + tp_levels, 8, width), f32),
+            DMA((loads,)), DMA((3,)),
+            DMA((3, 2)), DMA((3, 2)),
+            DMA((levels + tp_levels,)), DMA((levels + tp_levels,)),
+            DMA((levels, 2, fsdp_size // 2)), DMA((levels, 2, fsdp_size // 2)),
+            DMA((chunks + 1, 2, tp_size - 1)), DMA((chunks + 1, 2, tp_size - 1)),
+        ],
+        compiler_params=pltpu.CompilerParams(
+            collective_id=collective_id, has_side_effects=True, vmem_limit_bytes=60 * 2**20
+        ),
+        name="tail_kernel",
+    )(
+        bounds, gains, live, memory, norm.reshape(heads, 1, hd), jnp.broadcast_to(gate[:, None, None], (heads, 1, hd)),
+        lse, gain_two, stat, branch, attn_full, qkv, mix, flat_one, comb, stream, stream_all, gmid, mid, terms, to_send,
     )
-
-
-def halve(terms, axis, bits):
-    size = lax.axis_size(axis)
-    here = lax.axis_index(axis)
-    left = [1 << b for b in range(size.bit_length() - 2, -1, -1)]
-    for bit in bits:
-        at = left.index(bit)
-        mine = lax.rem(here // bit, 2)
-        kept = lax.dynamic_index_in_dim(terms, mine, at, keepdims=False)
-        sent = lax.dynamic_index_in_dim(terms, 1 - mine, at, keepdims=False)
-        came = lax.ppermute(sent, axis, [(i, i ^ bit) for i in range(size)])
-        total = kept.astype(jnp.float32) + came.astype(jnp.float32)
-        left.pop(at)
-        terms = total if not left else total.astype(jnp.bfloat16)
-    return terms
-
-
-def scatter_blocks(grad, axis):
-    size = lax.axis_size(axis)
-    levels = size.bit_length() - 1
-    ups = [1 << b for b in range(1, levels)]
-    rows = grad.shape[0] // size
-    split = grad.reshape((2,) * levels + (2, rows // 2, grad.shape[1]))
-    first = halve(lax.index_in_dim(split, 0, levels, keepdims=False), axis, [1] + ups)
-    second = halve(lax.index_in_dim(split, 1, levels, keepdims=False), axis, [1] + ups[::-1])
-    return jnp.concatenate([first, second], axis=0)
 
 
 def on_device(
@@ -1070,55 +1368,32 @@
     local_position = tp_here * len_dev + jnp.arange(len_dev, dtype=jnp.int32)
     live_here = (local_position < valid_len).astype(f32)[:, None]
     (
-        _, attn_full, flat_one, qkv_rows, combined, local_mix, _, _, _, _, _, _,
-        stream_out, grad_middle, branch_low, kept, landed, gain_two_terms, stats, log_total, memory_next, normalizer_next, gains,
+        _, attn_full, flat_one, qkv_rows, combined, local_mix, _, _, _, _, _, mlp_terms,
+        first_out, grad_middle, branch_low, kept, _, stream_all, middle_rows, to_send,
+        gain_two_terms, stats, log_total, memory_next, normalizer_next, gains,
     ) = whole_layer(
         bounds, gains, live_here, memory[0], normalizer[0], mem_gate, stream, cotangent,
         (w_query, w_key, w_value, w_out), (w_gate, w_up, w_down), tp_size, fsdp_size, 1,
     )
     inner = w_query.shape[1]
-    combined = combined.reshape(seq_len, inner)
-    branch_low = branch_low.reshape(seq_len, width)
-    query_full, key_full, value_full, out_full = (attn_full[:, p * inner : (p + 1) * inner] for p in range(4))
-
+    stream_grad, second_out, landed, attn_landed, attn_kept, grad_memory, grad_normalizer, joined = whole_tail(
+        bounds, gains, live_here, memory[0], normalizer[0], mem_gate, log_total, gain_two_terms, stats,
+        branch_low.reshape(seq_len, width), attn_full, qkv_rows, local_mix, flat_one, combined.reshape(seq_len, inner),
+        stream, stream_all, grad_middle, middle_rows, mlp_terms[1], to_send, tp_size, fsdp_size, 2,
+    )
+    stream_out = jnp.concatenate([first_out, second_out], axis=0)
     gate_grad, up_grad, down_grad = (
-        kept[g].astype(f32) + landed[g, -1, :shard].astype(f32) for g in range(3)
+        kept[g].astype(f32) + landed[g].reshape(shard, -1).astype(f32) for g in range(3)
     )
-    out_grad = scatter_blocks(contract_rows(branch_low, combined).astype(bf16), "fsdp")
-    grad_combined = jnp.dot(branch_low, out_full, preferred_element_type=f32)
-    query_low, key_low, value_low, grad_memory, grad_normalizer, gate_parts = attend_back(
-        bounds, qkv_rows, grad_combined, local_mix, log_total,
-        memory[0], normalizer[0], mem_gate,
+    query_grad, key_grad, value_grad, out_grad = (
+        attn_kept[:, p * inner : (p + 1) * inner].astype(f32)
+        + attn_landed[-1, :shard, p * inner : (p + 1) * inner].astype(f32)
+        for p in range(4)
     )
-    one_terms = (
-        times_transpose(query_low, query_full)
-        + times_transpose(key_low, key_full)
-        + times_transpose(value_low, value_full)
-    )
-    grad_normed_one = lax.psum_scatter(one_terms.astype(bf16), "tp", scatter_dimension=0, tiled=True).astype(f32)
-    query_grad = scatter_blocks(contract_rows(flat_one, query_low).astype(bf16), "fsdp")
-    key_grad = scatter_blocks(contract_rows(flat_one, key_low).astype(bf16), "fsdp")
-    value_grad = scatter_blocks(contract_rows(flat_one, value_low).astype(bf16), "fsdp")
-
-    stream_f = stream.astype(f32)
-    inverse = lax.rsqrt(jnp.mean(stream_f * stream_f, axis=-1, keepdims=True) + norm_eps)
-    unit = stream_f * inverse
-    gain_one_terms = jnp.sum(grad_normed_one * unit, axis=0)
-    scaled = grad_normed_one * gains[0]
-    stream_grad = grad_middle + inverse * (scaled - unit * jnp.mean(scaled * unit, axis=-1, keepdims=True))
-
-    gate_terms = jnp.zeros((tp_size, heads_here), f32).at[tp_here].set(jnp.sum(gate_parts, axis=(1, 2)))
-    stat_terms = jnp.zeros((fsdp_size, 3), f32).at[seq_here].set(jnp.stack([stats[1, 0], stats[0, 0], stats[2, 0]]))
-    joined = lax.psum(
-        jnp.concatenate([gain_one_terms, gain_two_terms[0], gate_terms.reshape(-1), stat_terms.reshape(-1)]),
-        ("fsdp", "tp"),
-    )
-    gain_one_grad = lax.dynamic_slice_in_dim(joined[:width], seq_here * shard, shard)
-    gain_two_grad = lax.dynamic_slice_in_dim(joined[width : 2 * width], seq_here * shard, shard)
-    gates = joined[2 * width : 2 * width + tp_size * heads_here].reshape(tp_size, heads_here)
-    sums = joined[2 * width + tp_size * heads_here :].reshape(fsdp_size, 3)
-    gate_grad_logit = lax.dynamic_index_in_dim(gates, tp_here, 0, keepdims=False)
-    stat_sums = lax.dynamic_index_in_dim(sums, seq_here, 0)
+    gain_one_grad = lax.dynamic_slice(joined, (0, seq_here * shard), (1, shard))[0]
+    gain_two_grad = lax.dynamic_slice(joined, (1, seq_here * shard), (1, shard))[0]
+    gate_grad_logit = lax.dynamic_slice(joined, (2, tp_here * heads_here), (1, heads_here))[0]
+    stat_sums = lax.dynamic_slice(joined, (3, seq_here * 3), (1, 3))
     token_count = valid_len.astype(f32) * width
     rms_stats = jnp.sqrt(stat_sums / token_count + rms_eps)
     return (

time: 809 us -> 734 us (0.907)
  the two profiles are of different devices: /device:TPU:0 before, /device:TPU:25 now
where the time goes in v4:
time: 734 us; the launch traced here: 725 us
  Pallas kernels  693 us (94%)
  local copies, waits for them, and re-layouts  16.7 us (2%)
  other arithmetic  12.8 us (2%)
    pallas_call x1, Pallas kernels, whole_layer(): pl.pallas_call(functools.partial(layer_kernel, chunks=chunks, tp_size=tp_...  521 us
    pallas_call x1, Pallas kernels, whole_tail(): pl.pallas_call(functools.partial(tail_kernel, chunks=chunks, tp_size=tp_s...  172 us

profile of v4, /device:TPU:25, one launch (start us, length us, event | category | flops | bytes accessed | tf_op | source)
XLA Modules:
  0.0 724.8 jit_solution(1679742753631153861)
XLA Ops:
  0.7 1.2 dynamic_slice.19
  2.6 1.2 dynamic_slice.18
  3.8 1.9 pad_add_fusion.bounds
  5.7 0.7 stack.13
  6.3 0.7 stack.14
  7.0 1.3 broadcast_in_dim.13.gate_ref
  8.3 1.3 fusion.live_ref
  9.7 521.1 %layer_kernel.1 = (bf16[3,2048,2048]{2,1,0:T(8,128)(2,1)}, bf16[2048,2048]{1,0:T(8,128)(2,1)}, bf16[1024,2048]{1,0:T(8,128)(2,1)}, bf16[1024,1536]{1,0:T(8,128)(...) custom-call(s32[2]{0:T(128)} %pad_add_fusion.bounds, ...), custom_call_target="tpu_custom_call" | custom-call | tf_op jit(solution)/shard_map/layer_kernel/pallas_call | solution.py:880
  530.8 3.2 slice_bitcast_fusion.terms_hbm
  534.0 172.3 %tail_kernel.1 = (f32[256,2048]{1,0:T(8,128)}, bf16[128,2048]{1,0:T(8,128)(2,1)}, bf16[3,2,128,2048]{3,2,1,0:T(8,128)(2,1)}, bf16[3,1024,2048]{2,1,0:T(8,128)(2,...) custom-call(s32[2]{0:T(128)} %pad_add_fusion.bounds, ...), custom_call_target="tpu_custom_call" | custom-call | tf_op jit(solution)/shard_map/tail_kernel/pallas_call | solution.py:1294
  706.3 1.4 add_sqrt_fusion
  707.7 1.3 dynamic-slice_bitcast_fusion
  709.0 2.1 maximum_bitcast_fusion
  711.1 1.4 constant_dynamic-slice_fusion
  712.5 2.8 convert_add_fusion.3
  715.3 0.2 fusion.1
  715.5 1.7 copy-done.1
  717.2 3.3 convert_add_fusion
  720.5 0.0 copy-done.2
  720.5 1.3 copy.39
  721.8 0.7 copy.40
  722.5 0.6 copy.41
  723.1 0.7 copy.42
  723.8 0.6 copy.43
  (20 shorter events, 0.1 us)
Async XLA Ops:
  8.3 1.4 copy-start.5
  534.0 175.0 %copy-start.4 = (bf16[128,2048]{1,0:T(8,128)(2,1)S(1)}, bf16[128,2048]{1,0:T(8,128)(2,1)}, u32[]{:S(2)}) copy-start(bf16[128,2048]{1,0:T(8,128)(2,1)} %get-tuple-element.44) | copy-start | bytes 1572868
  706.3 6.2 copy-start.3
  712.5 2.8 copy-start
  715.3 1.9 copy-start.1
  717.2 3.3 copy-start.2
  720.5 1.3 copy-start.6
  720.5 2.0 copy-start.8
  720.5 2.6 copy-start.7
  720.5 3.3 copy-start.9

commit v5 on v4

--- a/solution.py
+++ b/solution.py
@@ -46,6 +46,7 @@
 norm_eps = 1e-06
 MESH = pl.DeviceIdType.MESH
 RIGHT, LEFT = 0, 1
+PIECE = 32
 
 
 class Line:
@@ -67,39 +68,61 @@
     def arrived(self, phase, way, slot, dst):
         self.copy(phase, way, slot, dst, dst).wait_recv()
 
-    def scatter_step(self, phase, k, part, land_right, land_left):
+    def scatter_step(self, phase, step, part, land_right, land_left):
         n, t = self.size, self.here
-        far, near = n - 1 - k, k
-
-        def pass_on(way, shard, land, first):
+
+        def pass_on(way, slot, shard, land, first):
             @pl.when(jnp.logical_not(first))
             def _():
-                self.arrived(phase, way, k, land)
-                part[shard] = (part[shard].astype(jnp.float32) + land[...].astype(jnp.float32)).astype(part.dtype)
-
-            self.copy(phase, way, k, part.at[shard], land).start()
-
-        @pl.when(t < far)
+                self.arrived(phase, way, slot, land)
+
+                @pl.loop(0, part.shape[1] // PIECE)
+                def _(r):
+                    rows = pl.ds(pl.multiple_of(r * PIECE, PIECE), PIECE)
+                    came = land[rows, :].astype(jnp.float32)
+                    part[shard, rows, :] = (part[shard, rows, :].astype(jnp.float32) + came).astype(part.dtype)
+
+            self.copy(phase, way, slot, part.at[shard], land).start()
+
+        right, left = step - t, step - (n - 1 - t)
+        far, near = n - 1 - right, left
+
+        @pl.when((right >= 0) & (far > t))
         def _():
-            pass_on(RIGHT, far, land_right.at[far - 1], t == 0)
-
-        @pl.when(t > near)
+            pass_on(RIGHT, right, far, land_right.at[far - 1], t == 0)
+
+        @pl.when((left >= 0) & (near < t))
         def _():
-            pass_on(LEFT, near, land_left.at[near], t == n - 1)
+            pass_on(LEFT, left, near, land_left.at[near], t == n - 1)
 
     def scatter_end(self, phase, part, land_right, land_left, total):
         n, t = self.size, self.here
-        total[...] = part[t].astype(jnp.float32)
+
+        def over(work):
+            @pl.loop(0, part.shape[1] // PIECE)
+            def _(r):
+                work(pl.ds(pl.multiple_of(r * PIECE, PIECE), PIECE))
+
+        def own(rows):
+            total[rows, :] = part[t, rows, :].astype(jnp.float32)
+
+        def from_left(rows):
+            total[rows, :] += land_right[t - 1, rows, :].astype(jnp.float32)
+
+        def from_right(rows):
+            total[rows, :] += land_left[t, rows, :].astype(jnp.float32)
+
+        over(own)
 
         @pl.when(t > 0)
         def _():
             self.arrived(phase, RIGHT, n - 1 - t, land_right.at[t - 1])
-            total[...] += land_right[t - 1].astype(jnp.float32)
+            over(from_left)
 
         @pl.when(t < n - 1)
         def _():
             self.arrived(phase, LEFT, t, land_left.at[t])
-            total[...] += land_left[t].astype(jnp.float32)
+            over(from_right)
 
     def scatter_sent(self, phase, part, land_right, land_left):
         n, t = self.size, self.here
@@ -342,10 +365,14 @@
         item.wait()
 
     def norm_one(s):
-        v = stream_at(s)[...].astype(f32)
-        flat_one[pl.ds(pl.multiple_of(s * rows_dev, rows_dev), rows_dev), :] = (
-            v * inverse_rms(v) * gain[0:1, :]
-        ).astype(bf16)
+        raw = stream_at(s)
+
+        @pl.loop(0, rows_dev // PIECE)
+        def _(r):
+            v = raw[pl.ds(pl.multiple_of(r * PIECE, PIECE), PIECE), :].astype(f32)
+            flat_one[pl.ds(pl.multiple_of(s * rows_dev + r * PIECE, PIECE), PIECE), :] = (
+                v * inverse_rms(v) * gain[0:1, :]
+            ).astype(bf16)
 
     def project_one(s):
         rows = pl.ds(pl.multiple_of(s * rows_dev, rows_dev), rows_dev)
@@ -475,14 +502,24 @@
                 hid[:, c * inner : (c + 1) * inner], attn_w[cols, 3 * inner : 4 * inner], NT
             ).astype(bf16)
 
+    def by_piece(c, work):
+        @pl.loop(0, c_rows // PIECE)
+        def _(r):
+            piece = pl.ds(pl.multiple_of(r * PIECE, PIECE), PIECE)
+            work(piece, pl.ds(pl.multiple_of(c * c_rows + r * PIECE, PIECE), PIECE))
+
+    def square_sum(v, live):
+        return jnp.sum(jnp.sum(v * v, axis=-1, keepdims=True) * live, axis=0, keepdims=True)
+
     def norm_two(c):
-        rows = slice(c * c_rows, (c + 1) * c_rows)
-        branch = total[...]
-        live = live_ref[rows, :]
-        stat_ref[0:1, :] += jnp.sum(jnp.sum(branch * branch, axis=-1, keepdims=True) * live, axis=0, keepdims=True)
-        m = stream[rows, :].astype(f32) + branch
-        mid[rows, :] = m
-        x[c, t] = (m * inverse_rms(m) * gain[1:2, :]).astype(bf16)
+        def work(piece, rows):
+            branch = total[piece, :]
+            stat_ref[0:1, :] += square_sum(branch, live_ref[rows, :])
+            m = stream[rows, :].astype(f32) + branch
+            mid[rows, :] = m
+            x[c, t, piece, :] = (m * inverse_rms(m) * gain[1:2, :]).astype(bf16)
+
+        by_piece(c, work)
 
     def first_half(c, service):
         flat = x.at[c].reshape(n * c_rows, width)
@@ -516,16 +553,18 @@
             ul[:, cols] = dot32(hid[...], w_three[2, cols, :], NT).astype(bf16)
 
     def norm_back(c):
-        rows = slice(c * c_rows, (c + 1) * c_rows)
-        m = mid[rows, :]
-        inv = inverse_rms(m)
-        u = m * inv
-        gn = total[...]
-        e = gn * gain[1:2, :]
-        ggain_ref[...] += jnp.sum(gn * u, axis=0, keepdims=True)
-        gm = stream[rows, :].astype(f32) + inv * (e - u * jnp.mean(e * u, axis=-1, keepdims=True))
-        total[...] = gm
-        x[c, t] = gm.astype(bf16)
+        def work(piece, rows):
+            m = mid[rows, :]
+            inv = inverse_rms(m)
+            u = m * inv
+            gn = total[piece, :]
+            e = gn * gain[1:2, :]
+            ggain_ref[...] += jnp.sum(gn * u, axis=0, keepdims=True)
+            gm = stream[rows, :].astype(f32) + inv * (e - u * jnp.mean(e * u, axis=-1, keepdims=True))
+            total[piece, :] = gm
+            x[c, t, piece, :] = gm.astype(bf16)
+
+        by_piece(c, work)
 
     def scatter(kind, c, k):
         line.scatter_step(ph(kind, c), k, *lands(c))
@@ -627,14 +666,17 @@
         scatter(RS2, c, 0)
 
     def finish_branch(c):
-        rows = slice(c * c_rows, (c + 1) * c_rows)
         line.scatter_end(ph(RS2, c), *lands(c), total)
-        branch = total[...]
-        result = mid[rows, :] + branch
-        live = live_ref[rows, :]
-        stat_ref[1:2, :] += jnp.sum(jnp.sum(result * result, axis=-1, keepdims=True) * live, axis=0, keepdims=True)
-        stat_ref[2:3, :] += jnp.sum(jnp.sum(branch * branch, axis=-1, keepdims=True) * live, axis=0, keepdims=True)
-        part[c, t] = result.astype(bf16)
+
+        def work(piece, rows):
+            branch = total[piece, :]
+            result = mid[rows, :] + branch
+            live = live_ref[rows, :]
+            stat_ref[1:2, :] += square_sum(result, live)
+            stat_ref[2:3, :] += square_sum(branch, live)
+            part[c, t, piece, :] = result.astype(bf16)
+
+        by_piece(c, work)
         send_out("result", c, part.at[c, t], result_out, 6)
         outs["result", c].wait()
 
@@ -972,7 +1014,7 @@
 
     weight_load = load(attn_hbm, attn_w)
     branch_load = load(branch_hbm, rows_ref)
-    terms_load = load(terms_hbm, part.at[chunks])
+    terms_load = load(terms_hbm.at[chunks - 1], part.at[chunks])
     comb_load = load(comb_hbm, spare_ref.at[:, 0:inner])
     qkv_load = load(qkv_hbm, qkv)
     mix_load = load(mix_hbm, mixed_ref)
@@ -1123,19 +1165,27 @@
     mid_load = load(mid_hbm.at[own_rows, :], extra)
     line.scatter_end(chunks, *lands(chunks), total)
     mid_load.wait()
-    branch = total[...]
-    result = extra[...] + branch
-    live = live_ref[own_rows, :]
-    part[chunks, t] = result.astype(bf16)
+
+    def by_piece(work):
+        @pl.loop(0, c_rows // PIECE)
+        def _(r):
+            work(pl.ds(pl.multiple_of(r * PIECE, PIECE), PIECE), r * PIECE)
+
+    def close_branch(piece, first):
+        branch = total[piece, :]
+        result = extra[piece, :] + branch
+        live = live_ref[pl.ds(pl.multiple_of(rows_dev - c_rows + first, PIECE), PIECE), :]
+        part[chunks, t, piece, :] = result.astype(bf16)
+        values = (result, branch)
+        for at, value in zip((0, 2), values):
+            squares = jnp.sum(jnp.sum(value * value, axis=-1, keepdims=True) * live, axis=0, keepdims=True)
+            sums[3:4, :] += jnp.where(lane == 3 * f + at, squares, 0.0)
+
+    by_piece(close_branch)
     result_save = pltpu.make_async_copy(part.at[chunks, t], result_out, out_sem.at[0])
     result_save.start()
-
-    def square_sum(v):
-        return jnp.sum(jnp.sum(v * v, axis=-1, keepdims=True) * live, axis=0, keepdims=True)
-
-    stats = (stat_ref[1:2, 0:1] + square_sum(result), stat_ref[0:1, 0:1], stat_ref[2:3, 0:1] + square_sum(branch))
-    for at, value in enumerate(stats):
-        sums[3:4, :] += jnp.where(lane == 3 * f + at, value, 0.0)
+    for at, row in enumerate((1, 0, 2)):
+        sums[3:4, :] += jnp.where(lane == 3 * f + at, stat_ref[row : row + 1, 0:1], 0.0)
 
     def sums_step(at):
         target = {"fsdp": peer(1 << at)} if at < levels else {"tp": lax.bitwise_xor(t, 1 << (at - levels))}
@@ -1221,11 +1271,15 @@
         line.scatter_end(c, *lands(c), total)
         gmid_load.wait()
         stream_load.wait()
-        v = part[chunks, 0].astype(f32)
-        inv = inverse_rms(v)
-        u = v * inv
-        e = total[...] * one_gain
-        total[...] = extra[...] + inv * (e - u * jnp.mean(e * u, axis=-1, keepdims=True))
+
+        def close(piece, first):
+            v = part[chunks, 0, piece, :].astype(f32)
+            inv = inverse_rms(v)
+            u = v * inv
+            e = total[piece, :] * one_gain
+            total[piece, :] = extra[piece, :] + inv * (e - u * jnp.mean(e * u, axis=-1, keepdims=True))
+
+        by_piece(close)
         save = pltpu.make_async_copy(total, grad_out.at[rows, :], out_sem.at[1])
         save.start()
         save.wait()
@@ -1379,7 +1433,7 @@
     stream_grad, second_out, landed, attn_landed, attn_kept, grad_memory, grad_normalizer, joined = whole_tail(
         bounds, gains, live_here, memory[0], normalizer[0], mem_gate, log_total, gain_two_terms, stats,
         branch_low.reshape(seq_len, width), attn_full, qkv_rows, local_mix, flat_one, combined.reshape(seq_len, inner),
-        stream, stream_all, grad_middle, middle_rows, mlp_terms[1], to_send, tp_size, fsdp_size, 2,
+        stream, stream_all, grad_middle, middle_rows, mlp_terms, to_send, tp_size, fsdp_size, 2,
     )
     stream_out = jnp.concatenate([first_out, second_out], axis=0)
     gate_grad, up_grad, down_grad = (

time: 734 us -> 598 us (0.81)
  the two profiles are of different devices: /device:TPU:25 before, /device:TPU:0 now
where the time goes in v5:
time: 598 us; the launch traced here: 590 us
  Pallas kernels  562 us (94%)
  local copies, waits for them, and re-layouts  13.6 us (2%)
  other arithmetic  13.1 us (2%)
    pallas_call x1, Pallas kernels, whole_layer(): pl.pallas_call(functools.partial(layer_kernel, chunks=chunks, tp_size=tp_...  445 us
    pallas_call x1, Pallas kernels, whole_tail(): pl.pallas_call(functools.partial(tail_kernel, chunks=chunks, tp_size=tp_s...  116 us

profile of v5, /device:TPU:0, one launch (start us, length us, event | category | flops | bytes accessed | tf_op | source)
XLA Modules:
  0.0 590.0 jit_solution(11391790998709318994)
XLA Ops:
  0.7 1.2 dynamic_slice.19
  2.6 1.2 dynamic_slice.18
  3.8 1.9 pad_add_fusion.bounds
  5.7 0.7 stack.13
  6.3 0.7 stack.14
  7.0 1.3 broadcast_in_dim.13.gate_ref
  8.3 1.3 fusion.live_ref
  9.7 445.2 %layer_kernel.1 = (bf16[3,2048,2048]{2,1,0:T(8,128)(2,1)}, bf16[2048,2048]{1,0:T(8,128)(2,1)}, bf16[1024,2048]{1,0:T(8,128)(2,1)}, bf16[1024,1536]{1,0:T(8,128)(...) custom-call(s32[2]{0:T(128)} %pad_add_fusion.bounds, ...), custom_call_target="tpu_custom_call" | custom-call | tf_op jit(solution)/shard_map/layer_kernel/pallas_call | solution.py:922
  454.9 0.0 copy-start.3
  454.9 116.3 %tail_kernel.1 = (f32[256,2048]{1,0:T(8,128)}, bf16[128,2048]{1,0:T(8,128)(2,1)}, bf16[3,2,128,2048]{3,2,1,0:T(8,128)(2,1)}, bf16[3,1024,2048]{2,1,0:T(8,128)(2,...) custom-call(s32[2]{0:T(128)} %pad_add_fusion.bounds, ...), custom_call_target="tpu_custom_call" | custom-call | tf_op jit(solution)/shard_map/tail_kernel/pallas_call | solution.py:1348
  571.2 1.3 add_sqrt_fusion
  572.5 1.3 dynamic-slice_bitcast_fusion
  573.8 2.3 maximum_bitcast_fusion
  576.0 1.4 constant_dynamic-slice_fusion
  577.5 3.0 convert_add_fusion.3
  580.4 0.0 copy-done
  580.4 0.2 fusion.1
  580.7 1.7 copy-done.1
  582.3 3.3 convert_add_fusion
  585.6 1.3 copy.39
  587.0 0.7 copy.40
  587.7 0.6 copy.41
  588.2 0.7 copy.42
  588.9 0.6 copy.43
  (17 shorter events, 0.0 us)
Async XLA Ops:
  8.3 1.4 copy-start.4
  454.9 118.8 %copy-start.3 = (bf16[128,2048]{1,0:T(8,128)(2,1)S(1)}, bf16[128,2048]{1,0:T(8,128)(2,1)}, u32[]{:S(2)}) copy-start(bf16[128,2048]{1,0:T(8,128)(2,1)} %get-tuple-element.44) | copy-start | bytes 1572868
  573.8 6.7 %copy-start = (bf16[3,2,128,2048]{3,2,1,0:T(8,128)(2,1)S(1)}, bf16[3,2,128,2048]{3,2,1,0:T(8,128)(2,1)}, u32[]{:S(2)}) copy-start(bf16[3,2,128,2048]{3,2,1,0:T(8,128)(2,1)} %get-tuple-element.66) | copy-start | bytes 9437188
  580.4 1.9 copy-start.1
  582.3 3.3 copy-start.2
  585.6 1.3 copy-start.5
  585.6 2.0 copy-start.7
  585.6 2.6 copy-start.6
  585.6 3.3 copy-start.8

commit v6 on v5

--- a/solution.py
+++ b/solution.py
@@ -474,6 +474,8 @@
 
     for s in range(n):
         attend_rows(s)
+        if s == n - 2:
+            line.gather_step(ph(COT, 0), 1, cot_at(0))
     for stage in range(2, cube.levels):
         push(2, stage)
     comb_saves = []
@@ -580,7 +582,6 @@
     cube.sent(0, block_of(0))
     gate_load = pltpu.make_async_copy(mlp_hbm.at[0], w_three.at[0], load_sem.at[0])
     gate_load.start()
-    gather(COT, 0, 1)
     gather(COT, 1, 1)
     update_memory()
     scatter(RS1, 0, 1)
@@ -817,8 +818,11 @@
             for _, _, item in trades(g, i):
                 item.wait_send()
 
+    def skip():
+        pass
+
     cot_loads[0].wait()
-    first_half(0, during(*[functools.partial(gather, AG2, 1, k) for k in range(1, n)]))
+    first_half(0, during(skip, functools.partial(gather, AG2, 1, 1), skip, functools.partial(gather, AG2, 1, 2)))
     cot_loads[1].start()
     save_chunk(0)
     line.scatter_sent(ph(RS1, 0), *lands(0))
@@ -828,12 +832,14 @@
     outs["ul", 0].wait()
     scatter(RS3, 0, 0)
     branch_terms(0)
+    for k in range(3, n):
+        gather(AG2, 1, k)
     save_terms(0)
     outs["hid", 0].wait()
     outs["gl", 0].wait()
     await_terms(0)
     cot_loads[1].wait()
-    first_half(1, during(lambda: None, *[functools.partial(scatter, RS3, 0, k) for k in range(1, n - 1)]))
+    first_half(1, during(functools.partial(scatter, RS3, 0, 1), skip, functools.partial(scatter, RS3, 0, 2)))
     save_chunk(1)
     line.scatter_sent(ph(RS1, 1), *lands(1))
     second_half(1)
@@ -853,18 +859,14 @@
     start_branch(0)
     await_terms(1)
 
-    def skip():
-        pass
-
     def z_one():
         for k in range(2, n - 1):
             scatter(RS3, 1, k)
         gather(AG4, 0, 2)
 
-    weight_grad(0, during(*[skip] * 6, z_one))
+    weight_grad(0, during(*[skip] * 3, z_one))
     scatter(RS2, 0, 1)
-    weight_grad(1)
-    finish_back(1)
+    weight_grad(1, during(*[skip] * 4, functools.partial(finish_back, 1), functools.partial(add_first, 0)))
     mid_save = pltpu.make_async_copy(mid, mid_out, own_sem.at[5])
     mid_save.start()
     for k in range(3, n):
@@ -872,11 +874,8 @@
     send_out("branch", 0, x.at[0], branch_out.at[:, 0], 0)
     for k in range(2, n - 1):
         scatter(RS2, 0, k)
-    add_first(0)
-    gather(AG4, 1, 1)
-    weight_grad(2)
+    weight_grad(2, during(skip, functools.partial(gather, AG4, 1, 1), skip, functools.partial(add_first, 1)))
     finish_branch(0)
-    add_first(1)
     gather(AG4, 1, 2)
     add_first(2)
     for i in range(1, cube.levels - 1):

time: 598 us -> 578 us (0.967)
  Pallas kernels: 562 us -> 542 us
    pallas_call x1, Pallas kernels: 445 us -> 427 us  [whole_layer(): pl.pallas_call(functools.partial(layer_kernel, chunks=chunks, tp_size=tp_...]
where the time goes in v6:
time: 578 us; the launch traced here: 570 us
  Pallas kernels  542 us (94%)
  local copies, waits for them, and re-layouts  13.6 us (2%)
  other arithmetic  13.1 us (2%)
    pallas_call x1, Pallas kernels, whole_layer(): pl.pallas_call(functools.partial(layer_kernel, chunks=chunks, tp_size=tp_...  427 us
    pallas_call x1, Pallas kernels, whole_tail(): pl.pallas_call(functools.partial(tail_kernel, chunks=chunks, tp_size=tp_s...  115 us

profile of v6, /device:TPU:0, one launch (start us, length us, event | category | flops | bytes accessed | tf_op | source)
XLA Modules:
  0.0 570.4 jit_solution(7710401443950254634)
XLA Ops:
  0.7 1.2 dynamic_slice.19
  2.6 1.2 dynamic_slice.18
  3.8 1.9 pad_add_fusion.bounds
  5.7 0.7 stack.13
  6.3 0.7 stack.14
  7.0 1.3 broadcast_in_dim.13.gate_ref
  8.3 1.3 fusion.live_ref
  9.7 427.2 %layer_kernel.1 = (bf16[3,2048,2048]{2,1,0:T(8,128)(2,1)}, bf16[2048,2048]{1,0:T(8,128)(2,1)}, bf16[1024,2048]{1,0:T(8,128)(2,1)}, bf16[1024,1536]{1,0:T(8,128)(...) custom-call(s32[2]{0:T(128)} %pad_add_fusion.bounds, ...), custom_call_target="tpu_custom_call" | custom-call | tf_op jit(solution)/shard_map/layer_kernel/pallas_call | solution.py:921
  436.9 0.0 copy-start.3
  436.9 114.7 %tail_kernel.1 = (f32[256,2048]{1,0:T(8,128)}, bf16[128,2048]{1,0:T(8,128)(2,1)}, bf16[3,2,128,2048]{3,2,1,0:T(8,128)(2,1)}, bf16[3,1024,2048]{2,1,0:T(8,128)(2,...) custom-call(s32[2]{0:T(128)} %pad_add_fusion.bounds, ...), custom_call_target="tpu_custom_call" | custom-call | tf_op jit(solution)/shard_map/tail_kernel/pallas_call | solution.py:1347
  551.6 1.3 add_sqrt_fusion
  552.9 1.3 dynamic-slice_bitcast_fusion
  554.2 2.3 maximum_bitcast_fusion
  556.5 1.4 constant_dynamic-slice_fusion
  557.9 3.0 convert_add_fusion.3
  560.8 0.0 copy-done
  560.8 0.2 fusion.1
  561.1 1.7 copy-done.1
  562.7 3.3 convert_add_fusion
  566.0 1.3 copy.39
  567.4 0.7 copy.40
  568.1 0.6 copy.41
  568.6 0.7 copy.42
  569.4 0.6 copy.43
  (17 shorter events, 0.0 us)
Async XLA Ops:
  8.3 1.4 copy-start.4
  436.9 117.3 %copy-start.3 = (bf16[128,2048]{1,0:T(8,128)(2,1)S(1)}, bf16[128,2048]{1,0:T(8,128)(2,1)}, u32[]{:S(2)}) copy-start(bf16[128,2048]{1,0:T(8,128)(2,1)} %get-tuple-element.44) | copy-start | bytes 1572868
  554.2 6.7 %copy-start = (bf16[3,2,128,2048]{3,2,1,0:T(8,128)(2,1)S(1)}, bf16[3,2,128,2048]{3,2,1,0:T(8,128)(2,1)}, u32[]{:S(2)}) copy-start(bf16[3,2,128,2048]{3,2,1,0:T(8,128)(2,1)} %get-tuple-element.66) | copy-start | bytes 9437188
  560.8 1.9 copy-start.1
  562.7 3.3 copy-start.2
  566.0 1.3 copy-start.5
  566.0 2.0 copy-start.7
  566.0 2.6 copy-start.6
  566.0 3.3 copy-start.8

commit v7 on v6

--- a/solution.py
+++ b/solution.py
@@ -1211,6 +1211,10 @@
         cols = pl.ds(pl.multiple_of(j * wide, wide), wide)
         store_grad(j, wide, slice(0, 3 * inner), dot32(one_ref[:, cols], dqkv[...], TN))
 
+        @pl.when(j == 4)
+        def _():
+            scatter(0, 1)
+
     first_trade = pltpu.make_async_remote_copy(
         src_ref=g_ref.at[spare : 2 * spare, :],
         dst_ref=land.at[0],
@@ -1241,10 +1245,9 @@
     def add_rows(mine, came):
         g_ref[mine, :] = (g_ref[mine, :].astype(f32) + spare_ref[came, :].astype(f32)).astype(bf16)
 
-    scatter(0, 1)
+    scatter(1, 1)
     sums_add(0)
     sums_step(1).start()
-    scatter(1, 1)
     first_trade.wait_recv()
     first_load = load(land.at[0], spare_ref)
     first_load.wait()

time: 578 us -> 578 us (level)
  no operation moved by 1% of the time
where the time goes in v7:
time: 578 us; the launch traced here: 570 us
  Pallas kernels  542 us (94%)
  local copies, waits for them, and re-layouts  13.6 us (2%)
  other arithmetic  13.1 us (2%)
    pallas_call x1, Pallas kernels, whole_layer(): pl.pallas_call(functools.partial(layer_kernel, chunks=chunks, tp_size=tp_...  427 us
    pallas_call x1, Pallas kernels, whole_tail(): pl.pallas_call(functools.partial(tail_kernel, chunks=chunks, tp_size=tp_s...  115 us

profile of v7, /device:TPU:0, one launch (start us, length us, event | category | flops | bytes accessed | tf_op | source)
XLA Modules:
  0.0 570.4 jit_solution(15679812448500221629)
XLA Ops:
  0.7 1.2 dynamic_slice.19
  2.6 1.2 dynamic_slice.18
  3.8 1.9 pad_add_fusion.bounds
  5.7 0.7 stack.13
  6.3 0.7 stack.14
  7.0 1.3 broadcast_in_dim.13.gate_ref
  8.3 1.3 fusion.live_ref
  9.7 427.2 %layer_kernel.1 = (bf16[3,2048,2048]{2,1,0:T(8,128)(2,1)}, bf16[2048,2048]{1,0:T(8,128)(2,1)}, bf16[1024,2048]{1,0:T(8,128)(2,1)}, bf16[1024,1536]{1,0:T(8,128)(...) custom-call(s32[2]{0:T(128)} %pad_add_fusion.bounds, ...), custom_call_target="tpu_custom_call" | custom-call | tf_op jit(solution)/shard_map/layer_kernel/pallas_call | solution.py:921
  436.9 0.0 copy-start.3
  436.9 114.7 %tail_kernel.1 = (f32[256,2048]{1,0:T(8,128)}, bf16[128,2048]{1,0:T(8,128)(2,1)}, bf16[3,2,128,2048]{3,2,1,0:T(8,128)(2,1)}, bf16[3,1024,2048]{2,1,0:T(8,128)(2,...) custom-call(s32[2]{0:T(128)} %pad_add_fusion.bounds, ...), custom_call_target="tpu_custom_call" | custom-call | tf_op jit(solution)/shard_map/tail_kernel/pallas_call | solution.py:1350
  551.6 1.3 add_sqrt_fusion
  552.9 1.3 dynamic-slice_bitcast_fusion
  554.2 2.3 maximum_bitcast_fusion
  556.5 1.4 constant_dynamic-slice_fusion
  557.9 3.0 convert_add_fusion.3
  560.8 0.0 copy-done
  560.8 0.2 fusion.1
  561.1 1.7 copy-done.1
  562.7 3.3 convert_add_fusion
  566.0 1.3 copy.39
  567.4 0.7 copy.40
  568.1 0.6 copy.41
  568.6 0.7 copy.42
  569.4 0.6 copy.43
  (17 shorter events, 0.0 us)
Async XLA Ops:
  8.3 1.4 copy-start.4
  436.9 117.3 %copy-start.3 = (bf16[128,2048]{1,0:T(8,128)(2,1)S(1)}, bf16[128,2048]{1,0:T(8,128)(2,1)}, u32[]{:S(2)}) copy-start(bf16[128,2048]{1,0:T(8,128)(2,1)} %get-tuple-element.44) | copy-start | bytes 1572868
  554.2 6.7 %copy-start = (bf16[3,2,128,2048]{3,2,1,0:T(8,128)(2,1)S(1)}, bf16[3,2,128,2048]{3,2,1,0:T(8,128)(2,1)}, u32[]{:S(2)}) copy-start(bf16[3,2,128,2048]{3,2,1,0:T(8,128)(2,1)} %get-tuple-element.66) | copy-start | bytes 9437188
  560.8 1.9 copy-start.1
  562.7 3.3 copy-start.2
  566.0 1.3 copy-start.5
  566.0 2.0 copy-start.7
  566.0 2.6 copy-start.6
  566.0 3.3 copy-start.8
